TPU v7x, 512 devices: a whole 4x4x16 slice. The times are simulated.
512 devices in a mesh: dp: 64 (over y_hi, z, core), mp: 8 (over y_lo, x).
Axes of the slice: x: 4, y: 4 (y_hi: 2, y_lo: 2; y = y_hi * 2 + y_lo), z: 16, core: 2. Of those that a mesh axis runs over, the one named last changes fastest.
Arguments:
- queries: bfloat16 [2048, 4096], P('dp', 'mp'), may hold values from -16 to 16, as said below
- passages: bfloat16 [2048, 4096], P('dp', 'mp'), may hold values from -6 to 6, as said below
- negatives: bfloat16 [14336, 4096], P('dp', 'mp'), may hold values from -8 to 8
- hard_owner: int32 [2048, 7], P('dp'), may hold values from 0 to 63, all different within a row; in each aligned block of 32 rows (0 to 31, 32 to 63, ...) at most 7 rows name the same one
- hard_row: int32 [2048, 7], P('dp'), may hold values from 0 to 223
Outputs:
- query_grad: bfloat16 [2048, 4096], P('dp', 'mp')
- passage_grad: bfloat16 [2048, 4096], P('dp', 'mp')
- negative_grad: bfloat16 [14336, 4096], P('dp', 'mp')
Inputs may be any that keep to these rules, and one draw needn't show every extreme that they name: In some draws a few queries are close to a multiple (up to 3) of some passage's direction, so that some in-batch scores reach several hundred. In some draws a few passages nearly repeat other passages. `hard_owner`: each query names 7 different owners; among the queries of one index of dp at most 7 references go to one owner, and in every draw some owner receives exactly 7 from some index. `hard_row`: rows may repeat across queries.
All inputs are finite; a program needn't handle non-finite values.
Results may differ from a plain program's by a relative error of at most 0.013.
Values may be sent and summed in bfloat16 or wider, within the bound.
No kernel may reach another device: no remote copies, remote signals or barrier semaphores. Data moves between devices by JAX's collectives and lax.ppermute only.
A program may use at most 64 MiB of HBM per device.

v0:
```python
import math

import jax
import jax.numpy as jnp
from jax import lax
from jax.sharding import PartitionSpec as P

D = 4096
NEG = 7


def score_weights(batch_scores, hard_scores, first_col):
    row_top = jnp.maximum(jnp.max(batch_scores, axis=1), jnp.max(hard_scores, axis=1))
    exp_total = jnp.sum(jnp.exp(batch_scores - row_top[:, None]), axis=1) + jnp.sum(
        jnp.exp(hard_scores - row_top[:, None]), axis=1
    )
    log_total = row_top + jnp.log(exp_total)
    columns = jnp.arange(batch_scores.shape[1], dtype=jnp.int32)[None, :]
    targets = first_col + jnp.arange(batch_scores.shape[0], dtype=jnp.int32)[:, None]
    positive = (columns == targets).astype(jnp.float32)
    batch_weights = (jnp.exp(batch_scores - log_total[:, None]) - positive).astype(jnp.bfloat16)
    hard_weights = jnp.exp(hard_scores - log_total[:, None]).astype(jnp.bfloat16)
    return (batch_weights, hard_weights)


def shards(queries, passages, negatives, hard_owner, hard_row):
    row_count = queries.shape[0]
    col_width = queries.shape[1]
    groups = lax.axis_size("dp")
    slot_cap = (2 * row_count * NEG + groups - 1) // groups
    score_scale = 3.0 / math.sqrt(D)
    dp_index = lax.axis_index("dp")
    owner_flat = hard_owner.reshape(-1)
    row_flat = hard_row.reshape(-1)
    onehot = (owner_flat[:, None] == jnp.arange(groups, dtype=jnp.int32)[None, :]).astype(jnp.int32)
    owner_ranks = jnp.cumsum(onehot, axis=0) - 1
    slot_index = jnp.sum(owner_ranks * onehot, axis=1)
    slot_place = owner_flat * slot_cap + slot_index
    requests = (
        jnp.zeros((groups * slot_cap,), jnp.int32)
        .at[slot_place]
        .set(row_flat)
        .reshape(groups, slot_cap)
    )
    asked_rows = lax.all_to_all(requests, "dp", split_axis=0, concat_axis=0, tiled=True)
    served = jnp.take(negatives, asked_rows.reshape(-1), axis=0).reshape(
        groups, slot_cap, col_width
    )
    replies = lax.all_to_all(served, "dp", split_axis=0, concat_axis=0, tiled=True)
    fetched = jnp.take(replies.reshape(groups * slot_cap, col_width), slot_place, axis=0).reshape(
        row_count, NEG, col_width
    )
    all_passages = lax.all_gather(passages, "dp", axis=0, tiled=True)
    hard_part = jnp.einsum("qd,qkd->qk", queries, fetched, preferred_element_type=jnp.float32)
    batch_part = jnp.einsum("qd,pd->qp", queries, all_passages, preferred_element_type=jnp.float32)
    batch_sum, hard_sum = lax.psum((batch_part, hard_part), "mp")
    batch_w, hard_w = score_weights(
        batch_sum * score_scale, hard_sum * score_scale, dp_index * row_count
    )
    query_acc = jnp.einsum("qp,pd->qd", batch_w, all_passages, preferred_element_type=jnp.float32)
    query_acc = query_acc + jnp.einsum(
        "qk,qkd->qd", hard_w, fetched, preferred_element_type=jnp.float32
    )
    query_out = query_acc.astype(jnp.bfloat16)
    weight_cols = lax.all_to_all(batch_w, "dp", split_axis=1, concat_axis=0, tiled=True)
    passage_acc = jnp.einsum(
        "qp,qd->pd",
        weight_cols,
        lax.all_gather(queries, "dp", axis=0, tiled=True),
        preferred_element_type=jnp.float32,
    )
    passage_out = passage_acc.astype(jnp.bfloat16)
    hard_float = hard_w.astype(jnp.float32)
    neg_terms = (hard_float[:, :, None] * queries.astype(jnp.float32)[:, None, :]).astype(
        jnp.bfloat16
    )
    outgoing = (
        jnp.zeros((groups * slot_cap, col_width), jnp.bfloat16)
        .at[slot_place]
        .set(neg_terms.reshape(-1, col_width))
    )
    incoming = lax.all_to_all(
        outgoing.reshape(groups, slot_cap, col_width), "dp", split_axis=0, concat_axis=0, tiled=True
    )
    neg_acc = (
        jnp.zeros((negatives.shape[0], col_width), jnp.float32)
        .at[asked_rows.reshape(-1)]
        .add(incoming.reshape(-1, col_width).astype(jnp.float32))
    )
    return (query_out, passage_out, neg_acc.astype(jnp.bfloat16))


def solution(mesh):
    return jax.shard_map(
        shards,
        mesh=mesh,
        in_specs=(P("dp", "mp"), P("dp", "mp"), P("dp", "mp"), P("dp", None), P("dp", None)),
        out_specs=(P("dp", "mp"), P("dp", "mp"), P("dp", "mp")),
        check_vma=False,
    )
```

profile of v0, /device:TPU:1, one launch (start us, length us, event | category | flops | bytes accessed | tf_op | source)
XLA Modules:
  0.0 416.3 jit_solution(3690078278130381903)
XLA Ops:
  7.2 0.7 all-gather.3.cloned.1.call-update
  7.9 0.8 copy.15
  8.9 0.6 reduce-window.6
  9.8 0.8 copy.19
  10.8 1.3 scatter_custom_fusion
  12.2 34.4 %all_to_all.38 = s32[64,1,7]{2,1,0:T(1,128)S(1)} all-to-all(s32[64,1,7]{2,1,0:T(1,128)S(1)} %bitcast.41), channel_id=1, replica_groups=mesh['dp'=64,'mp'=8] {'dp'}, dimensions={0} | all-to-all | bytes 3584 | tf_op jit(solution)/shard_map/all_to_all | solution.py:45
  47.1 0.7 reduce.5
  48.0 2.1 gather_fusion
  50.3 1.0 broadcast_select_fusion
  51.3 4.6 %all-to-all-start.1 = ((bf16[64,7,512]{2,1,0:T(8,128)(2,1)}), bf16[64,7,512]{2,1,0:T(8,128)(2,1)S(1)}, u32[]{:S(2)}, u32[]{:S(2)}) async-start(bf16[64,7,512]{2,1,0:T(8,128)(2,1)} %broadcast_select_fusion), calls=%async_computation.1 | async-start | bytes 1048576 | tf_op jit(solution)/shard_map/all_to_all | solution.py:49
  56.0 108.7 %all-gather.3.cloned.1.call-done = bf16[2048,512]{1,0:T(8,128)(2,1)} async-done(((bf16[32,512]{1,0:T(8,128)(2,1)}), bf16[2048,512]{1,0:T(8,128)(2,1)}) %all-gather.3.cloned.1.call-update) | async-done | bytes 2097168 | tf_op jit(solution)/shard_map/all_gather | solution.py:53
  164.7 3.0 fusion.20
  167.8 0.7 all-gather.5.cloned.1.call-update
  168.8 1.1 gather_fusion.1
  170.3 26.6 %psum.15 = f32[32,7]{1,0:T(8,128)S(1)} all-reduce(f32[32,7]{1,0:T(8,128)S(1)} %bitcast.42), channel_id=1, replica_groups=mesh['dp'=64,'mp'=8] {'mp'}, use_global_device_ids=true, to_apply=%region_6.7 | all-reduce | flops 224 | bytes 1792 | tf_op jit(solution)/shard_map/psum | solution.py:56
  197.0 49.1 %all-reduce.3.cloned.1.call-done = f32[32,2048]{1,0:T(8,128)} async-done(((f32[32,2048]{1,0:T(8,128)}), f32[32,2048]{1,0:T(8,128)}) %all-reduce.3.cloned.1.call-update) | async-done | bytes 262160 | tf_op jit(solution)/shard_map/psum | solution.py:56
  246.2 1.1 multiply_reduce_fusion
  247.4 1.2 exponential_reduce_fusion
  248.6 1.1 subtract_convert_fusion
  250.5 1.1 reshape.230
  251.5 20.7 %all-to-all-start.2 = ((bf16[64,2,512]{2,1,0:T(2,128)(2,1)}), bf16[64,2,512]{2,1,0:T(2,128)(2,1)}, u32[]{:S(2)}, u32[]{:S(2)}) async-start(bf16[64,2,512]{2,1,0:T(2,128)(2,1)} %reshape.230), calls=%async_computation.2 | async-start | bytes 262144 | tf_op jit(solution)/shard_map/all_to_all | solution.py:65
  272.5 1.6 scatter_custom_fusion.1
  274.2 0.9 reshape.166
  275.1 16.1 %all-to-all-done.2 = bf16[64,2,512]{2,1,0:T(2,128)(2,1)} async-done(((bf16[64,2,512]{2,1,0:T(2,128)(2,1)}), bf16[64,2,512]{2,1,0:T(2,128)(2,1)}, u32[]{:S(2)}, u32[]{:S(2)}) %all-to-all-start.2) | async-done | bytes 131104 | tf_op jit(solution)/shard_map/all_to_all | solution.py:65
  291.2 4.4 %all-to-all-start.3 = ((bf16[64,7,512]{2,1,0:T(8,128)(2,1)}), bf16[64,7,512]{2,1,0:T(8,128)(2,1)S(1)}, u32[]{:S(2)}, u32[]{:S(2)}) async-start(bf16[64,7,512]{2,1,0:T(8,128)(2,1)} %reshape.166), calls=%async_computation.3 | async-start | bytes 1048576 | tf_op jit(solution)/shard_map/all_to_all | solution.py:82
  295.6 1.2 fusion.6
  296.9 1.1 fusion
  298.0 1.3 reshape.231
  299.2 103.7 %all-gather.5.cloned.1.call-done = bf16[2048,512]{1,0:T(8,128)(2,1)} async-done(((bf16[32,512]{1,0:T(8,128)(2,1)}), bf16[2048,512]{1,0:T(8,128)(2,1)}) %all-gather.5.cloned.1.call-update) | async-done | bytes 2097168 | tf_op jit(solution)/shard_map/all_gather | solution.py:69
  402.9 2.7 convolution_convert_fusion
  405.7 3.3 scatter_custom_fusion.2
  409.1 0.7 convert_element_type.43
  (53 shorter events, 4.0 us)
Async XLA Ops:
  7.2 40.8 %copy-start = (bf16[224,512]{1,0:T(8,128)(2,1)S(1)}, bf16[224,512]{1,0:T(8,128)(2,1)}, u32[]{:S(2)}) copy-start(bf16[224,512]{1,0:T(8,128)(2,1)} %param.7) | copy-start | bytes 688132
  7.2 157.5 %all-gather.3.cloned.1.call-start = ((), (), s32[]{:S(2)}) async-start(), calls=%async_computation.4 | async-start | bytes 2129920 | tf_op jit(solution)/shard_map/all_gather | solution.py:53
  50.1 114.5 %copy-start.2 = (bf16[32,512]{1,0:T(8,128)(2,1)S(1)}, bf16[32,512]{1,0:T(8,128)(2,1)}, u32[]{:S(2)}) copy-start(bf16[32,512]{1,0:T(8,128)(2,1)} %param.5) | copy-start | bytes 98308
  51.3 117.3 %all-to-all-start.1 = ((bf16[64,7,512]{2,1,0:T(8,128)(2,1)}), bf16[64,7,512]{2,1,0:T(8,128)(2,1)S(1)}, u32[]{:S(2)}, u32[]{:S(2)}) async-start(bf16[64,7,512]{2,1,0:T(8,128)(2,1)} %broadcast_select_fusion), calls=%async_computation.1 | async-start | bytes 1048576 | tf_op jit(solution)/shard_map/all_to_all | solution.py:49
  55.9 190.2 %all-reduce.3.cloned.1.call-start = ((), (), s32[]{:S(2)}) async-start(), calls=%async_computation.5 | async-start | bytes 524288 | tf_op jit(solution)/shard_map/psum | solution.py:56
  167.7 2.3 copy-start.3
  167.7 235.2 %all-gather.5.cloned.1.call-start = ((), (), s32[]{:S(2)}) async-start(), calls=%async_computation.6 | async-start | bytes 2129920 | tf_op jit(solution)/shard_map/all_gather | solution.py:69
  169.9 79.8 %copy-start.4 = (bf16[32,7,512]{2,1,0:T(8,128)(2,1)}, bf16[32,7,512]{2,1,0:T(8,128)(2,1)S(1)}, u32[]{:S(2)}) copy-start(bf16[32,7,512]{2,1,0:T(8,128)(2,1)S(1)} %gather.15) | copy-start | bytes 688132
  251.5 39.7 %all-to-all-start.2 = ((bf16[64,2,512]{2,1,0:T(2,128)(2,1)}), bf16[64,2,512]{2,1,0:T(2,128)(2,1)}, u32[]{:S(2)}, u32[]{:S(2)}) async-start(bf16[64,2,512]{2,1,0:T(2,128)(2,1)} %reshape.230), calls=%async_computation.2 | async-start | bytes 262144 | tf_op jit(solution)/shard_map/all_to_all | solution.py:65
  272.3 24.6 %copy-start.1 = (bf16[2048,512]{1,0:T(8,128)(2,1)S(1)}, bf16[2048,512]{1,0:T(8,128)(2,1)}, u32[]{:S(2)}) copy-start(bf16[2048,512]{1,0:T(8,128)(2,1)} %all-gather.3.cloned.1.call-done) | copy-start | bytes 6291460
  291.2 114.4 %all-to-all-start.3 = ((bf16[64,7,512]{2,1,0:T(8,128)(2,1)}), bf16[64,7,512]{2,1,0:T(8,128)(2,1)S(1)}, u32[]{:S(2)}, u32[]{:S(2)}) async-start(bf16[64,7,512]{2,1,0:T(8,128)(2,1)} %reshape.166), calls=%async_computation.3 | async-start | bytes 1048576 | tf_op jit(solution)/shard_map/all_to_all | solution.py:82
Sparse Core Ops, SparseCore 0:
  11.3 153.3 all-gather.2
  167.8 78.2 all-reduce.2
  250.0 152.9 all-gather.4
where the time goes:
time: 417 us; the launch traced here: 416 us
  waiting for transfers between devices  279 us (67%)
  blocking collectives  61 us (15%)
  starting transfers between devices  29.8 us (7%)
  between operations  14.1 us (3%)
  local copies, waits for them, and re-layouts  12.2 us (3%)
  other arithmetic  11.9 us (3%)
  matrix products  8.35 us (2%)
    all_gather x1, waiting for transfers between devices, shards(): all_passages = lax.all_gather(passages, 'dp', axis=0, tiled=True)  109 us
    all_gather x1, waiting for transfers between devices, shards(): lax.all_gather(queries, 'dp', axis=0, tiled=True)  104 us
    psum x1, waiting for transfers between devices, shards(): batch_sum, hard_sum = lax.psum((batch_part, hard_part), 'mp')  49.1 us
    all_to_all x1, blocking collectives, shards(): lax.all_to_all(requests, 'dp', split_axis=0, concat_axis=0, tiled=True)  34.4 us
    psum x1, blocking collectives, shards(): batch_sum, hard_sum = lax.psum((batch_part, hard_part), 'mp')  26.6 us
    all_to_all x1, starting transfers between devices, shards(): lax.all_to_all(batch_w, 'dp', split_axis=1, concat_axis=0, tiled=True)  20.7 us
    all_to_all x1, waiting for transfers between devices, shards(): lax.all_to_all(batch_w, 'dp', split_axis=1, concat_axis=0, tiled=True)  16.1 us
  transfers between devices with their start and end apart: 6, of which 4 were waited for; matrix products, arithmetic and copies ran while one was open for 7% of the time, Pallas kernels for 0%

commit v1 on v0

v1 whole, which is shorter than its diff:
```python
import math

import jax
import jax.numpy as jnp
from jax import lax
from jax.experimental import pallas as pl
from jax.experimental.pallas import tpu as pltpu
from jax.sharding import Mesh
from jax.sharding import PartitionSpec as P

BF16 = jnp.bfloat16
F32 = jnp.float32
NZ = 16
NB = 4
ABSENT = -1e30
VMEM_LIMIT = 48 * 1024 * 1024


def call(kernel, out_shapes, *args, smem=0, scratch=()):
    specs = [pl.BlockSpec(memory_space=pltpu.SMEM)] * smem
    specs += [pl.BlockSpec(memory_space=pltpu.VMEM)] * (len(args) - smem)
    return pl.pallas_call(
        kernel,
        out_shape=[jax.ShapeDtypeStruct(shape, dtype) for shape, dtype in out_shapes],
        in_specs=specs,
        out_specs=[pl.BlockSpec(memory_space=pltpu.VMEM)] * len(out_shapes),
        scratch_shapes=list(scratch),
        compiler_params=pltpu.CompilerParams(vmem_limit_bytes=VMEM_LIMIT),
    )(*args)


def pack_kernel(place, queries, passages, negatives, owners, rows, sent, columns):
    yh, z, c = place[0], place[1], place[2]
    width = queries.shape[1]
    line = lax.broadcasted_iota(jnp.int32, (NZ * 16, 128), 0)
    lane = lax.broadcasted_iota(jnp.int32, (NZ * 16, 128), 1)
    block = line % 16
    owner = (yh ^ (block // 2)) * (2 * NZ) + (line // 16) * 2 + (c ^ (block % 2))
    owner = jnp.where((block < NB) & (lane // 32 == z % 4), owner, -2)
    asked = jnp.full((NZ * 16, 128), -1, jnp.int32)
    for k in range(owners.shape[0]):
        asked = jnp.where(owners[k : k + 1, :] == owner, rows[k : k + 1, :], asked)
    asked = asked.astype(F32).astype(BF16)
    pieces = [queries[:, l * 128 : (l + 1) * 128] for l in range(width // 128)]
    for to in range(NZ):
        for l, piece in enumerate(pieces):
            sent[to, l * 32 : (l + 1) * 32, :] = piece
        sent[to, 128:144, :] = asked[to * 16 : (to + 1) * 16, :]
    columns[0:32, :] = passages[...]
    columns[32:256, :] = negatives[...]


def score_kernel(came, col0, col1, col2, col3, parts, queries, asked):
    scale = 3.0 / math.sqrt(4096)
    for z in range(NZ):
        for l in range(4):
            queries[z * 32 : (z + 1) * 32, l * 128 : (l + 1) * 128] = came[z, l * 32 : (l + 1) * 32, :]
    for g in range(4):
        rows = came[4 * g, 128:144, :].astype(F32)
        for z in range(4 * g + 1, 4 * g + 4):
            rows = jnp.maximum(rows, came[z, 128:144, :].astype(F32))
        asked[:, g * 128 : (g + 1) * 128] = rows[0:8, :].astype(jnp.int32)
    every = queries[...]
    place = lax.broadcasted_iota(jnp.int32, (224, 512), 0)
    for o, cols in enumerate((col0, col1, col2, col3)):
        part = lax.dot_general(cols[...], every, (((1,), (1,)), ((), ())), preferred_element_type=F32)
        want = asked[o : o + 1, :]
        hard = jnp.sum(jnp.where(place == want, part[32:256, :], 0.0), axis=0, keepdims=True) * scale
        hard = jnp.where(want >= 0, hard, ABSENT)
        h, a = o // 2, o % 2
        for l in range(4):
            lanes = slice(l * 128, (l + 1) * 128)
            parts[h * 4 + l, a * 32 : (a + 1) * 32, :] = part[0:32, lanes] * scale
            parts[h * 4 + l, 64 + a : 65 + a, :] = hard[:, lanes]
            if a == 1:
                parts[h * 4 + l, 66:72, :] = jnp.zeros((6, 128), F32)


def add_kernel(came, sent):
    total = came[0]
    for i in range(1, 8):
        total = total + came[i]
    for i in range(8):
        sent[i] = total


def stat_kernel(scores, sent):
    for l in range(4):
        batch = [scores[h * 4 + l, 0:64, :] for h in range(2)]
        hard = [scores[h * 4 + l, 64:66, :] for h in range(2)]
        top = jnp.maximum(
            jnp.max(jnp.maximum(batch[0], batch[1]), axis=0, keepdims=True),
            jnp.max(jnp.maximum(hard[0], hard[1]), axis=0, keepdims=True),
        )
        total = jnp.sum(jnp.exp(batch[0] - top) + jnp.exp(batch[1] - top), axis=0, keepdims=True)
        total = total + jnp.sum(jnp.exp(hard[0] - top) + jnp.exp(hard[1] - top), axis=0, keepdims=True)
        for to in range(NZ):
            sent[to, l : l + 1, :] = top
            sent[to, 4 + l : 5 + l, :] = total


def grad_kernel(place, stats, scores, asked, queries, col0, col1, col2, col3, q_part, keep, give, q_acc):
    z = place[1]
    logs = []
    for l in range(4):
        tops = stats[:, l, :]
        top = jnp.max(tops, axis=0, keepdims=True)
        total = jnp.sum(stats[:, 4 + l, :] * jnp.exp(tops - top), axis=0, keepdims=True)
        logs.append(top + jnp.log(total))
    log_total = jnp.concatenate(logs, axis=1)
    every = queries[...]
    line = lax.broadcasted_iota(jnp.int32, (224, 512), 0)
    row = lax.broadcasted_iota(jnp.int32, (32, 512), 0)
    lane = lax.broadcasted_iota(jnp.int32, (32, 512), 1)
    for o, cols in enumerate((col0, col1, col2, col3)):
        h, a = o // 2, o % 2
        batch = jnp.concatenate([scores[h * 4 + l, a * 32 : (a + 1) * 32, :] for l in range(4)], axis=1)
        hard = jnp.concatenate([scores[h * 4 + l, 64 + a : 65 + a, :] for l in range(4)], axis=1)
        weights = jnp.exp(batch - log_total)
        if o == 0:
            weights = weights - (lane == z * 32 + row).astype(F32)
        hard = jnp.exp(hard - log_total)
        hard = jnp.where(line == asked[o : o + 1, :], hard, 0.0)
        both = jnp.concatenate([weights.astype(BF16), hard.astype(BF16)], axis=0)
        col_grad = jnp.dot(both, every, preferred_element_type=F32).astype(BF16)
        (give if a else keep)[h] = col_grad
        term = lax.dot_general(both, cols[...], (((0,), (0,)), ((), ())), preferred_element_type=F32)
        if o == 0:
            q_acc[...] = term
        elif o < NB - 1:
            q_acc[...] += term
        else:
            q_part[...] = (q_acc[...] + term).astype(BF16).reshape(NZ, 32, 512)


def pair_kernel(keep, came, own, sent):
    own[...] = keep[0].astype(F32) + came[0].astype(F32)
    sent[...] = (keep[1].astype(F32) + came[1].astype(F32)).astype(BF16)


def column_kernel(own, came, passage_out, negative_out):
    passage_out[...] = (own[0:32, :] + came[0:32, :].astype(F32)).astype(BF16)
    negative_out[...] = (own[32:256, :] + came[32:256, :].astype(F32)).astype(BF16)


def query_kernel(came, query_out):
    total = came[0].astype(F32)
    for z in range(1, NZ):
        total = total + came[z].astype(F32)
    query_out[...] = total.astype(BF16)


def swap(x, axis):
    return lax.ppermute(x, axis, [(0, 1), (1, 0)])


def exchange(x, axis):
    return lax.all_to_all(x, axis, split_axis=0, concat_axis=0, tiled=True)


def shards(queries, passages, negatives, hard_owner, hard_row):
    place = jnp.stack([lax.axis_index("yh"), lax.axis_index("z"), lax.axis_index("c")]).astype(jnp.int32)
    owners = jnp.tile(hard_owner.T, (1, 4))
    rows = jnp.tile(hard_row.T, (1, 4))
    sent, col0 = call(
        pack_kernel, [((NZ, 144, 128), BF16), ((256, 512), BF16)],
        place, queries, passages, negatives, owners, rows, smem=1,
    )
    col2 = swap(col0, "yh")
    col1 = swap(col0, "c")
    col3 = swap(col2, "c")
    came = exchange(sent, "z")
    parts, every, asked = call(
        score_kernel, [((8, 72, 128), F32), ((512, 512), BF16), ((8, 512), jnp.int32)],
        came, col0, col1, col2, col3,
    )
    (summed,) = call(add_kernel, [((8, 72, 128), F32)], exchange(parts, ("yl", "x")))
    scores = exchange(summed, ("yl", "x"))
    (stats,) = call(stat_kernel, [((NZ, 8, 128), F32)], scores)
    stats = exchange(stats, "z")
    q_part, keep, give = call(
        grad_kernel, [((NZ, 32, 512), BF16), ((2, 256, 512), BF16), ((2, 256, 512), BF16)],
        place, stats, scores, asked, every, col0, col1, col2, col3,
        smem=1, scratch=[pltpu.VMEM((512, 512), F32)],
    )
    own, cross = call(pair_kernel, [((256, 512), F32), ((256, 512), BF16)], keep, swap(give, "c"))
    cross = swap(cross, "yh")
    q_came = exchange(q_part, "z")
    passage_out, negative_out = call(column_kernel, [((32, 512), BF16), ((224, 512), BF16)], own, cross)
    (query_out,) = call(query_kernel, [((32, 512), BF16)], q_came)
    return (query_out, passage_out, negative_out)


def solution(mesh):
    fine = Mesh(mesh.devices.reshape(2, NZ, 2, 2, 4), ("yh", "z", "c", "yl", "x"))
    dp, mp = ("yh", "z", "c"), ("yl", "x")
    return jax.shard_map(
        shards,
        mesh=fine,
        in_specs=(P(dp, mp), P(dp, mp), P(dp, mp), P(dp, None), P(dp, None)),
        out_specs=(P(dp, mp), P(dp, mp), P(dp, mp)),
        check_vma=False,
    )
```

time: 417 us -> 127 us (0.30)
  the two profiles are of different devices: /device:TPU:1 before, /device:TPU:16 now
where the time goes in v1:
time: 127 us; the launch traced here: 126 us
  waiting for transfers between devices  44.5 us (35%)
  blocking collectives  42.9 us (34%)
  starting transfers between devices  29.3 us (23%)
  Pallas kernels  6.61 us (5%)
  local copies, waits for them, and re-layouts  2.38 us (2%)
    all_to_all x3, blocking collectives, exchange(): return lax.all_to_all(x, axis, split_axis=0, concat_axis=0, tiled=True)  42.9 us
    all_to_all x2, waiting for transfers between devices, exchange(): return lax.all_to_all(x, axis, split_axis=0, concat_axis=0, tiled=True)  24.9 us
    ppermute x5, waiting for transfers between devices, swap(): return lax.ppermute(x, axis, [(0, 1), (1, 0)])  19.6 us
    all_to_all x2, starting transfers between devices, exchange(): return lax.all_to_all(x, axis, split_axis=0, concat_axis=0, tiled=True)  18.8 us
    ppermute x5, starting transfers between devices, swap(): return lax.ppermute(x, axis, [(0, 1), (1, 0)])  10.5 us
    pallas_call x8, Pallas kernels, call(): pl.pallas_call(kernel, out_shape=[jax.ShapeDtypeStruct(shape, dtype) for...  6.61 us
  transfers between devices with their start and end apart: 7, of which 6 were waited for; matrix products, arithmetic and copies ran while one was open for 0% of the time, Pallas kernels for 1%

profile of v1, /device:TPU:16, one launch (start us, length us, event | category | flops | bytes accessed | tf_op | source)
XLA Modules:
  0.0 126.5 jit_solution(16692883168679711767)
XLA Ops:
  0.6 0.0 copy-start.3
  0.6 0.7 copy-done.3
  1.3 0.1 tile.9.owners
  1.4 0.6 copy-done.4
  2.0 0.1 tile.21.rows
  2.1 0.1 pad_add_fusion.place
  2.2 0.0 copy-done.2
  2.2 0.9 copy-done
  3.1 1.5 %shard_map.76 = (bf16[16,144,128]{2,1,0:T(8,128)(2,1)}, bf16[256,512]{1,0:T(8,128)(2,1)S(1)}) custom-call(s32[3]{0:T(128)S(1)} %pad_add_fusion.place, bf16[32,512]{1,0:T(8,128)(2,1)S(1)} %copy-done.1, bf16[32,512]{1,0:T(8,128)(2,1)S(1)} %copy-done.2, bf16[224,512]{1,0:T(8,128)(2,1)S(1)} %copy-done, s32[7,128]{1,0:T(8,128)S(1)} %tile.9.owners, ...), custom_call_target="tpu_custom_call" | custom-call | tf_op jit(solution)/shard_map/pallas_call | solution.py:22
  4.6 15.2 %all-to-all-start = ((bf16[16,144,128]{2,1,0:T(8,128)(2,1)}), bf16[16,144,128]{2,1,0:T(8,128)(2,1)S(1)}, u32[]{:S(2)}, u32[]{:S(2)}) async-start(bf16[16,144,128]{2,1,0:T(8,128)(2,1)} %get-tuple-element.15), calls=%async_computation | async-start | bytes 1179648 | tf_op jit(solution)/shard_map/all_to_all | solution.py:158
  19.8 2.2 %collective-permute-start.1 = (bf16[256,512]{1,0:T(8,128)(2,1)S(1)}, bf16[256,512]{1,0:T(8,128)(2,1)S(1)}, u32[]{:S(2)}, u32[]{:S(2)}) collective-permute-start(bf16[256,512]{1,0:T(8,128)(2,1)S(1)} %get-tuple-element.16.col0), channel_id=1, source_target_pairs={{0,256},{256,0},{1,257},{257,1},{2,258},{258,2},{3,259},{259,3},{4... | collective-permute-start | bytes 786440 | tf_op jit(solution)/shard_map/ppermute | solution.py:154
  22.1 1.9 %collective-permute-start = (bf16[256,512]{1,0:T(8,128)(2,1)S(1)}, bf16[256,512]{1,0:T(8,128)(2,1)S(1)}, u32[]{:S(2)}, u32[]{:S(2)}) collective-permute-start(bf16[256,512]{1,0:T(8,128)(2,1)S(1)} %get-tuple-element.16.col0), channel_id=1, source_target_pairs={{0,8},{8,0},{1,9},{9,1},{2,10},{10,2},{3,11},{11,3},{4,12},{12,4},... | collective-permute-start | bytes 786440 | tf_op jit(solution)/shard_map/ppermute | solution.py:154
  24.0 7.0 %collective-permute-done.1.col2 = bf16[256,512]{1,0:T(8,128)(2,1)S(1)} collective-permute-done((bf16[256,512]{1,0:T(8,128)(2,1)S(1)}, bf16[256,512]{1,0:T(8,128)(2,1)S(1)}, u32[]{:S(2)}, u32[]{:S(2)}) %collective-permute-start.1) | collective-permute-done | bytes 262176 | tf_op jit(solution)/shard_map/ppermute | solution.py:154
  31.0 1.9 %collective-permute-start.2 = (bf16[256,512]{1,0:T(8,128)(2,1)S(1)}, bf16[256,512]{1,0:T(8,128)(2,1)S(1)}, u32[]{:S(2)}, u32[]{:S(2)}) collective-permute-start(bf16[256,512]{1,0:T(8,128)(2,1)S(1)} %collective-permute-done.1.col2), channel_id=1, source_target_pairs={{0,8},{8,0},{1,9},{9,1},{2,10},{10,2},{3,11},{11,3},{4,12},{12,4},... | collective-permute-start | bytes 786440 | tf_op jit(solution)/shard_map/ppermute | solution.py:154
  32.9 0.0 collective-permute-done.col1
  32.9 1.5 %collective-permute-done.2.col3 = bf16[256,512]{1,0:T(8,128)(2,1)S(1)} collective-permute-done((bf16[256,512]{1,0:T(8,128)(2,1)S(1)}, bf16[256,512]{1,0:T(8,128)(2,1)S(1)}, u32[]{:S(2)}, u32[]{:S(2)}) %collective-permute-start.2) | collective-permute-done | bytes 262176 | tf_op jit(solution)/shard_map/ppermute | solution.py:154
  34.4 16.2 %all-to-all-done.came = bf16[16,144,128]{2,1,0:T(8,128)(2,1)S(1)} async-done(((bf16[16,144,128]{2,1,0:T(8,128)(2,1)}), bf16[16,144,128]{2,1,0:T(8,128)(2,1)S(1)}, u32[]{:S(2)}, u32[]{:S(2)}) %all-to-all-start) | async-done | bytes 589856 | tf_op jit(solution)/shard_map/all_to_all | solution.py:158
  50.6 0.8 shard_map.77
  51.4 12.5 %all_to_all.25.came = f32[8,72,128]{2,1,0:T(8,128)S(1)} all-to-all(f32[8,72,128]{2,1,0:T(8,128)S(1)} %get-tuple-element.17), channel_id=1, replica_groups=mesh['yh'=2,'z'=16,'c'=2,'yl'=2,'x'=4] {'yl','x'}, dimensions={0} | all-to-all | bytes 589824 | tf_op jit(solution)/shard_map/all_to_all | solution.py:158
  64.0 10.0 %all_to_all.26.scores = f32[8,72,128]{2,1,0:T(8,128)S(1)} all-to-all(f32[8,72,128]{2,1,0:T(8,128)S(1)} %shard_map.78), channel_id=1, replica_groups=mesh['yh'=2,'z'=16,'c'=2,'yl'=2,'x'=4] {'yl','x'}, dimensions={0} | all-to-all | bytes 589824 | tf_op jit(solution)/shard_map/all_to_all | solution.py:158
  74.0 0.1 shard_map.79
  74.1 20.3 %all_to_all.27.stats = f32[16,8,128]{2,1,0:T(8,128)S(1)} all-to-all(f32[16,8,128]{2,1,0:T(8,128)S(1)} %shard_map.79), channel_id=1, replica_groups=mesh['yh'=2,'z'=16,'c'=2,'yl'=2,'x'=4] {'z'}, dimensions={0} | all-to-all | bytes 131072 | tf_op jit(solution)/shard_map/all_to_all | solution.py:158
  94.4 2.7 %shard_map.80 = (bf16[16,32,512]{2,1,0:T(8,128)(2,1)}, bf16[2,256,512]{2,1,0:T(8,128)(2,1)S(1)}, bf16[2,256,512]{2,1,0:T(8,128)(2,1)S(1)}) custom-call(s32[3]{0:T(128)S(1)} %pad_add_fusion.place, f32[16,8,128]{2,1,0:T(8,128)S(1)} %all_to_all.27.stats, f32[8,72,128]{2,1,0:T(8,128)S(1)} %all_to_all.26.scores, s32[8,512]{1,0:T(8,128)S(1)} %get-tuple-element.18.asked, ...), custom_call_target="tpu_custom_call" | custom-call | tf_op jit(solution)/shard_map/pallas_call | solution.py:22
  97.1 3.6 %all-to-all-start.4 = ((bf16[16,32,512]{2,1,0:T(8,128)(2,1)}), bf16[16,32,512]{2,1,0:T(8,128)(2,1)S(1)}, u32[]{:S(2)}, u32[]{:S(2)}) async-start(bf16[16,32,512]{2,1,0:T(8,128)(2,1)} %get-tuple-element.20), calls=%async_computation.4 | async-start | bytes 1048576 | tf_op jit(solution)/shard_map/all_to_all | solution.py:158
  100.7 1.9 %collective-permute-start.3 = (bf16[2,256,512]{2,1,0:T(8,128)(2,1)S(1)}, bf16[2,256,512]{2,1,0:T(8,128)(2,1)S(1)}, u32[]{:S(2)}, u32[]{:S(2)}) collective-permute-start(bf16[2,256,512]{2,1,0:T(8,128)(2,1)S(1)} %get-tuple-element.22), channel_id=1, source_target_pairs={{0,8},{8,0},{1,9},{9,1},{2,10},{10,2},{3,11},{11,3},{4,12},{12,4},... | collective-permute-start | bytes 1572872 | tf_op jit(solution)/shard_map/ppermute | solution.py:154
  102.6 1.9 %collective-permute-done.3.came = bf16[2,256,512]{2,1,0:T(8,128)(2,1)S(1)} collective-permute-done((bf16[2,256,512]{2,1,0:T(8,128)(2,1)S(1)}, bf16[2,256,512]{2,1,0:T(8,128)(2,1)S(1)}, u32[]{:S(2)}, u32[]{:S(2)}) %collective-permute-start.3) | collective-permute-done | bytes 524320 | tf_op jit(solution)/shard_map/ppermute | solution.py:154
  104.5 0.1 shard_map.82
  104.6 2.5 %collective-permute-start.4 = (bf16[256,512]{1,0:T(8,128)(2,1)S(1)}, bf16[256,512]{1,0:T(8,128)(2,1)S(1)}, u32[]{:S(2)}, u32[]{:S(2)}) collective-permute-start(bf16[256,512]{1,0:T(8,128)(2,1)S(1)} %get-tuple-element.24), channel_id=1, source_target_pairs={{0,256},{256,0},{1,257},{257,1},{2,258},{258,2},{3,259},{259,3},{4... | collective-permute-start | bytes 786440 | tf_op jit(solution)/shard_map/ppermute | solution.py:154
  107.1 9.2 %collective-permute-done.4.came = bf16[256,512]{1,0:T(8,128)(2,1)S(1)} collective-permute-done((bf16[256,512]{1,0:T(8,128)(2,1)S(1)}, bf16[256,512]{1,0:T(8,128)(2,1)S(1)}, u32[]{:S(2)}, u32[]{:S(2)}) %collective-permute-start.4) | collective-permute-done | bytes 262176 | tf_op jit(solution)/shard_map/ppermute | solution.py:154
  116.3 0.7 shard_map.83
  117.1 8.7 %all-to-all-done.4.came = bf16[16,32,512]{2,1,0:T(8,128)(2,1)S(1)} async-done(((bf16[16,32,512]{2,1,0:T(8,128)(2,1)}), bf16[16,32,512]{2,1,0:T(8,128)(2,1)S(1)}, u32[]{:S(2)}, u32[]{:S(2)}) %all-to-all-start.4) | async-done | bytes 524320 | tf_op jit(solution)/shard_map/all_to_all | solution.py:158
  125.8 0.7 shard_map.81
  (8 shorter events, 0.0 us)
Async XLA Ops:
  0.6 0.7 copy-start.3
  1.3 0.7 copy-start.4
  1.3 0.8 copy-start.2
  1.3 0.8 copy-start.1
  2.2 0.9 copy-start
  4.6 46.0 %all-to-all-start = ((bf16[16,144,128]{2,1,0:T(8,128)(2,1)}), bf16[16,144,128]{2,1,0:T(8,128)(2,1)S(1)}, u32[]{:S(2)}, u32[]{:S(2)}) async-start(bf16[16,144,128]{2,1,0:T(8,128)(2,1)} %get-tuple-element.15), calls=%async_computation | async-start | bytes 1179648 | tf_op jit(solution)/shard_map/all_to_all | solution.py:158
  19.8 11.2 %collective-permute-start.1 = (bf16[256,512]{1,0:T(8,128)(2,1)S(1)}, bf16[256,512]{1,0:T(8,128)(2,1)S(1)}, u32[]{:S(2)}, u32[]{:S(2)}) collective-permute-start(bf16[256,512]{1,0:T(8,128)(2,1)S(1)} %get-tuple-element.16.col0), channel_id=1, source_target_pairs={{0,256},{256,0},{1,257},{257,1},{2,258},{258,2},{3,259},{259,3},{4... | collective-permute-start | bytes 786440 | tf_op jit(solution)/shard_map/ppermute | solution.py:154
  22.1 10.8 %collective-permute-start = (bf16[256,512]{1,0:T(8,128)(2,1)S(1)}, bf16[256,512]{1,0:T(8,128)(2,1)S(1)}, u32[]{:S(2)}, u32[]{:S(2)}) collective-permute-start(bf16[256,512]{1,0:T(8,128)(2,1)S(1)} %get-tuple-element.16.col0), channel_id=1, source_target_pairs={{0,8},{8,0},{1,9},{9,1},{2,10},{10,2},{3,11},{11,3},{4,12},{12,4},... | collective-permute-start | bytes 786440 | tf_op jit(solution)/shard_map/ppermute | solution.py:154
  31.0 3.4 %collective-permute-start.2 = (bf16[256,512]{1,0:T(8,128)(2,1)S(1)}, bf16[256,512]{1,0:T(8,128)(2,1)S(1)}, u32[]{:S(2)}, u32[]{:S(2)}) collective-permute-start(bf16[256,512]{1,0:T(8,128)(2,1)S(1)} %collective-permute-done.1.col2), channel_id=1, source_target_pairs={{0,8},{8,0},{1,9},{9,1},{2,10},{10,2},{3,11},{11,3},{4,12},{12,4},... | collective-permute-start | bytes 786440 | tf_op jit(solution)/shard_map/ppermute | solution.py:154
  97.1 28.7 %all-to-all-start.4 = ((bf16[16,32,512]{2,1,0:T(8,128)(2,1)}), bf16[16,32,512]{2,1,0:T(8,128)(2,1)S(1)}, u32[]{:S(2)}, u32[]{:S(2)}) async-start(bf16[16,32,512]{2,1,0:T(8,128)(2,1)} %get-tuple-element.20), calls=%async_computation.4 | async-start | bytes 1048576 | tf_op jit(solution)/shard_map/all_to_all | solution.py:158
  100.7 3.8 %collective-permute-start.3 = (bf16[2,256,512]{2,1,0:T(8,128)(2,1)S(1)}, bf16[2,256,512]{2,1,0:T(8,128)(2,1)S(1)}, u32[]{:S(2)}, u32[]{:S(2)}) collective-permute-start(bf16[2,256,512]{2,1,0:T(8,128)(2,1)S(1)} %get-tuple-element.22), channel_id=1, source_target_pairs={{0,8},{8,0},{1,9},{9,1},{2,10},{10,2},{3,11},{11,3},{4,12},{12,4},... | collective-permute-start | bytes 1572872 | tf_op jit(solution)/shard_map/ppermute | solution.py:154
  104.6 11.7 %collective-permute-start.4 = (bf16[256,512]{1,0:T(8,128)(2,1)S(1)}, bf16[256,512]{1,0:T(8,128)(2,1)S(1)}, u32[]{:S(2)}, u32[]{:S(2)}) collective-permute-start(bf16[256,512]{1,0:T(8,128)(2,1)S(1)} %get-tuple-element.24), channel_id=1, source_target_pairs={{0,256},{256,0},{1,257},{257,1},{2,258},{258,2},{3,259},{259,3},{4... | collective-permute-start | bytes 786440 | tf_op jit(solution)/shard_map/ppermute | solution.py:154

commit v2 on v1

v2 whole, which is shorter than its diff:
```python
import math

import jax
import jax.numpy as jnp
from jax import lax
from jax.experimental import pallas as pl
from jax.experimental.pallas import tpu as pltpu
from jax.sharding import Mesh
from jax.sharding import PartitionSpec as P

BF16 = jnp.bfloat16
F32 = jnp.float32
NZ = 8
NB = 8
ROWS = 256
GROUPS = ROWS // 128
ABSENT = -1e30
VMEM_LIMIT = 48 * 1024 * 1024


def call(kernel, out_shapes, *args, smem=0, hbm=0, scratch=()):
    specs = [pl.BlockSpec(memory_space=pltpu.SMEM)] * smem
    specs += [pl.BlockSpec(memory_space=pltpu.HBM)] * hbm
    specs += [pl.BlockSpec(memory_space=pltpu.VMEM)] * (len(args) - smem - hbm)
    return pl.pallas_call(
        kernel,
        out_shape=[jax.ShapeDtypeStruct(shape, dtype) for shape, dtype in out_shapes],
        in_specs=specs,
        out_specs=[pl.BlockSpec(memory_space=pltpu.VMEM)] * len(out_shapes),
        scratch_shapes=list(scratch),
        compiler_params=pltpu.CompilerParams(vmem_limit_bytes=VMEM_LIMIT),
    )(*args)


def pack_kernel(place, queries, passages, negatives, owners, rows, sent, columns, mine, short, wide, sems):
    copies = [
        pltpu.make_async_copy(owners, short.at[0], sems.at[0]),
        pltpu.make_async_copy(rows, short.at[1], sems.at[1]),
        pltpu.make_async_copy(queries, mine, sems.at[2]),
        pltpu.make_async_copy(negatives, columns.at[32:256], sems.at[3]),
        pltpu.make_async_copy(passages, columns.at[0:32], sems.at[4]),
    ]
    for copy in copies:
        copy.start()
    yh, zh, zp, c = place[0], place[1], place[2], place[3]
    line = lax.broadcasted_iota(jnp.int32, (NZ * 16, 128), 0)
    lane = lax.broadcasted_iota(jnp.int32, (NZ * 16, 128), 1)
    block = line % 16
    z = (line // 16) * 2 + (zp ^ (block // 4))
    owner = ((yh ^ (block // 2 % 2)) * (2 * NZ) + z) * 2 + (c ^ (block % 2))
    owner = jnp.where((block < NB) & (lane // 32 == zh % 4), owner, -2)
    copies[0].wait()
    copies[1].wait()
    for j in range(4):
        wide[:, :, j * 32 : (j + 1) * 32] = short[...]
    asked = jnp.full((NZ * 16, 128), -1, jnp.int32)
    for k in range(short.shape[1]):
        asked = jnp.where(wide[0, k : k + 1, :] == owner, wide[1, k : k + 1, :], asked)
    asked = asked.astype(F32).astype(BF16)
    for to in range(NZ):
        sent[to, 128:144, :] = asked[to * 16 : (to + 1) * 16, :]
    copies[2].wait()
    for to in range(NZ):
        for l in range(4):
            sent[to, l * 32 : (l + 1) * 32, :] = mine[:, l * 128 : (l + 1) * 128]
    copies[3].wait()
    copies[4].wait()


def score_kernel(came, *refs):
    columns, (parts, queries, asked) = refs[:NB], refs[NB:]
    scale = 3.0 / math.sqrt(4096)
    for z in range(NZ):
        for l in range(4):
            queries[z * 32 : (z + 1) * 32, l * 128 : (l + 1) * 128] = came[z, l * 32 : (l + 1) * 32, :]
    for g in range(GROUPS):
        rows = came[4 * g, 128:144, :].astype(F32)
        for z in range(4 * g + 1, 4 * g + 4):
            rows = jnp.maximum(rows, came[z, 128:144, :].astype(F32))
        asked[:, g * 128 : (g + 1) * 128] = rows[0:NB, :].astype(jnp.int32)
    every = queries[...]
    place = lax.broadcasted_iota(jnp.int32, (224, ROWS), 0)
    for o in range(NB):
        part = lax.dot_general(columns[o][...], every, (((1,), (1,)), ((), ())), preferred_element_type=F32)
        want = asked[o : o + 1, :]
        hard = jnp.sum(jnp.where(place == want, part[32:256, :], 0.0), axis=0, keepdims=True) * scale
        hard = jnp.where(want >= 0, hard, ABSENT)
        h, a = o // 2, o % 2
        for l in range(GROUPS):
            lanes = slice(l * 128, (l + 1) * 128)
            parts[h * GROUPS + l, a * 32 : (a + 1) * 32, :] = part[0:32, lanes] * scale
            parts[h * GROUPS + l, 64 + a : 65 + a, :] = hard[:, lanes]
            if a == 1:
                parts[h * GROUPS + l, 66:72, :] = jnp.zeros((6, 128), F32)


def add_kernel(came, sent):
    total = came[0]
    for i in range(1, 8):
        total = total + came[i]
    for i in range(8):
        sent[i] = total


def stat_kernel(scores, sent):
    for l in range(GROUPS):
        batch = [scores[h * GROUPS + l, 0:64, :] for h in range(NB // 2)]
        hard = [scores[h * GROUPS + l, 64:66, :] for h in range(NB // 2)]
        top = jnp.maximum(
            jnp.max(jnp.maximum(jnp.maximum(batch[0], batch[1]), jnp.maximum(batch[2], batch[3])), axis=0, keepdims=True),
            jnp.max(jnp.maximum(jnp.maximum(hard[0], hard[1]), jnp.maximum(hard[2], hard[3])), axis=0, keepdims=True),
        )
        total = jnp.sum(sum(jnp.exp(b - top) for b in batch), axis=0, keepdims=True)
        total = total + jnp.sum(sum(jnp.exp(h - top) for h in hard), axis=0, keepdims=True)
        for to in range(NZ):
            sent[to, l : l + 1, :] = top
            sent[to, GROUPS + l : GROUPS + l + 1, :] = total
    for to in range(NZ):
        sent[to, 2 * GROUPS : 8, :] = jnp.zeros((8 - 2 * GROUPS, 128), F32)


def grad_kernel(place, stats, scores, asked, queries, *refs):
    columns, (q_part, keep, give, q_acc) = refs[:NB], refs[NB:]
    zh = place[1]
    logs = []
    for l in range(GROUPS):
        tops = stats[:, l, :]
        top = jnp.max(tops, axis=0, keepdims=True)
        total = jnp.sum(stats[:, GROUPS + l, :] * jnp.exp(tops - top), axis=0, keepdims=True)
        logs.append(top + jnp.log(total))
    log_total = jnp.concatenate(logs, axis=1)
    every = queries[...]
    line = lax.broadcasted_iota(jnp.int32, (224, ROWS), 0)
    row = lax.broadcasted_iota(jnp.int32, (32, ROWS), 0)
    lane = lax.broadcasted_iota(jnp.int32, (32, ROWS), 1)
    for o in range(NB):
        h, a = o // 2, o % 2
        batch = jnp.concatenate([scores[h * GROUPS + l, a * 32 : (a + 1) * 32, :] for l in range(GROUPS)], axis=1)
        hard = jnp.concatenate([scores[h * GROUPS + l, 64 + a : 65 + a, :] for l in range(GROUPS)], axis=1)
        weights = jnp.exp(batch - log_total)
        if o == 0:
            weights = weights - (lane == zh * 32 + row).astype(F32)
        hard = jnp.exp(hard - log_total)
        hard = jnp.where(line == asked[o : o + 1, :], hard, 0.0)
        both = jnp.concatenate([weights.astype(BF16), hard.astype(BF16)], axis=0)
        (give if a else keep)[h] = jnp.dot(both, every, preferred_element_type=F32).astype(BF16)
        term = lax.dot_general(both, columns[o][...], (((0,), (0,)), ((), ())), preferred_element_type=F32)
        if o == 0:
            q_acc[...] = term
        elif o < NB - 1:
            q_acc[...] += term
        else:
            q_part[...] = (q_acc[...] + term).astype(BF16).reshape(NZ, 32, 512)


def pair_kernel(keep, came, own, *sent):
    own[...] = keep[0].astype(F32) + came[0].astype(F32)
    for h in range(1, NB // 2):
        sent[h - 1][...] = (keep[h].astype(F32) + came[h].astype(F32)).astype(BF16)


def column_kernel(own, *refs):
    came, (passage_out, negative_out) = refs[: NB // 2 - 1], refs[NB // 2 - 1 :]
    for out, rows in ((passage_out, slice(0, 32)), (negative_out, slice(32, 256))):
        total = own[rows, :]
        for other in came:
            total = total + other[rows, :].astype(F32)
        out[...] = total.astype(BF16)


def query_kernel(came, query_out):
    total = came[0].astype(F32)
    for z in range(1, NZ):
        total = total + came[z].astype(F32)
    query_out[...] = total.astype(BF16)


def swap(x, axes):
    size = 2 ** len(axes)
    return lax.ppermute(x, axes, [(i, size - 1 - i) for i in range(size)])


def exchange(x, axes):
    return lax.all_to_all(x, axes, split_axis=0, concat_axis=0, tiled=True)


def shards(queries, passages, negatives, hard_owner, hard_row):
    place = jnp.stack([lax.axis_index(axis) for axis in ("yh", "zh", "zp", "c")]).astype(jnp.int32)
    sent, own = call(
        pack_kernel, [((NZ, 144, 128), BF16), ((256, 512), BF16)],
        place, queries, passages, negatives, hard_owner.T, hard_row.T, smem=1, hbm=5,
        scratch=[
            pltpu.VMEM((32, 512), BF16), pltpu.VMEM((2, 7, 32), jnp.int32), pltpu.VMEM((2, 7, 128), jnp.int32),
            pltpu.SemaphoreType.DMA((5,)),
        ],
    )
    came = exchange(sent, "zh")
    others = [own, swap(own, ("yh",)), swap(own, ("zp",)), swap(own, ("yh", "zp"))]
    columns = [block for other in others for block in (other, swap(other, ("c",)))]
    parts, every, asked = call(
        score_kernel, [((8, 72, 128), F32), ((ROWS, 512), BF16), ((NB, ROWS), jnp.int32)], came, *columns
    )
    (summed,) = call(add_kernel, [((8, 72, 128), F32)], exchange(parts, ("yl", "x")))
    scores = exchange(summed, ("yl", "x"))
    (stats,) = call(stat_kernel, [((NZ, 8, 128), F32)], scores)
    stats = exchange(stats, "zh")
    q_part, keep, give = call(
        grad_kernel, [((NZ, 32, 512), BF16), ((NB // 2, 256, 512), BF16), ((NB // 2, 256, 512), BF16)],
        place, stats, scores, asked, every, *columns, smem=1, scratch=[pltpu.VMEM((ROWS, 512), F32)],
    )
    mine, by_yh, by_zp, by_both = call(
        pair_kernel, [((256, 512), F32)] + [((256, 512), BF16)] * 3, keep, swap(give, ("c",))
    )
    q_came = exchange(q_part, "zh")
    passage_out, negative_out = call(
        column_kernel, [((32, 512), BF16), ((224, 512), BF16)],
        mine, swap(by_both, ("yh", "zp")), swap(by_yh, ("yh",)), swap(by_zp, ("zp",)),
    )
    (query_out,) = call(query_kernel, [((32, 512), BF16)], q_came)
    return (query_out, passage_out, negative_out)


def solution(mesh):
    fine = Mesh(mesh.devices.reshape(2, NZ, 2, 2, 2, 4), ("yh", "zh", "zp", "c", "yl", "x"))
    dp, mp = ("yh", "zh", "zp", "c"), ("yl", "x")
    return jax.shard_map(
        shards,
        mesh=fine,
        in_specs=(P(dp, mp), P(dp, mp), P(dp, mp), P(dp, None), P(dp, None)),
        out_specs=(P(dp, mp), P(dp, mp), P(dp, mp)),
        check_vma=False,
    )
```

time: 127 us -> 137 us (1.079)
  the two profiles are of different devices: /device:TPU:16 before, /device:TPU:1 now
where the time goes in v2:
time: 137 us; the launch traced here: 136 us
  starting transfers between devices  56.9 us (42%)
  blocking collectives  43.9 us (32%)
  waiting for transfers between devices  22.6 us (16%)
  Pallas kernels  7.82 us (6%)
  local copies, waits for them, and re-layouts  3.73 us (3%)
    all_to_all x3, blocking collectives, exchange(): return lax.all_to_all(x, axes, split_axis=0, concat_axis=0, tiled=True)  43.9 us
    ppermute x11, starting transfers between devices, swap(): return lax.ppermute(x, axes, [(i, size - 1 - i) for i in range(size)])  37.8 us
    all_to_all x2, starting transfers between devices, exchange(): return lax.all_to_all(x, axes, split_axis=0, concat_axis=0, tiled=True)  19.1 us
    ppermute x11, waiting for transfers between devices, swap(): return lax.ppermute(x, axes, [(i, size - 1 - i) for i in range(size)])  12.9 us
    all_to_all x2, waiting for transfers between devices, exchange(): return lax.all_to_all(x, axes, split_axis=0, concat_axis=0, tiled=True)  9.7 us
    pallas_call x8, Pallas kernels, call(): pl.pallas_call(kernel, out_shape=[jax.ShapeDtypeStruct(shape, dtype) for...  7.82 us
    unnamed x12, local copies, waits for them, and re-layouts  3.73 us
  transfers between devices with their start and end apart: 13, of which 6 were waited for; matrix products, arithmetic and copies ran while one was open for 0% of the time, Pallas kernels for 1%

profile of v2, /device:TPU:1, one launch (start us, length us, event | category | flops | bytes accessed | tf_op | source)
XLA Modules:
  0.0 135.9 jit_solution(13542498917960496502)
XLA Ops:
  0.7 0.7 copy-done.2
  1.4 0.9 copy-done.1
  2.3 0.8 copy-done.3
  3.1 0.7 copy-done.5
  3.8 1.9 %shard_map.76 = (bf16[8,144,128]{2,1,0:T(8,128)(2,1)}, bf16[256,512]{1,0:T(8,128)(2,1)S(1)}) custom-call(s32[4]{0:T(128)S(1)} %pad_add_fusion.place, bf16[32,512]{1,0:T(8,128)(2,1)S(1)} %copy-done.2, bf16[32,512]{1,0:T(8,128)(2,1)S(1)} %copy-done.3, bf16[224,512]{1,0:T(8,128)(2,1)S(1)} %copy-done.1, s32[7,32]{1,0:T(8,128)S(1)} %bitcast.6, s32[7,32]{1,0:T(8,128)S(1)} %bitcast.7), custom_call_target="tpu_custom_call" | custom-call | tf_op jit(solution)/shard_map/pallas_call | solution.py:25
  5.7 15.7 %all-to-all-start = ((bf16[8,144,128]{2,1,0:T(8,128)(2,1)}), bf16[8,144,128]{2,1,0:T(8,128)(2,1)S(1)}, u32[]{:S(2)}, u32[]{:S(2)}) async-start(bf16[8,144,128]{2,1,0:T(8,128)(2,1)} %get-tuple-element.17), calls=%async_computation | async-start | bytes 589824 | tf_op jit(solution)/shard_map/all_to_all | solution.py:184
  21.3 5.3 %collective-permute-start.5 = (bf16[256,512]{1,0:T(8,128)(2,1)S(1)}, bf16[256,512]{1,0:T(8,128)(2,1)S(1)}, u32[]{:S(2)}, u32[]{:S(2)}) collective-permute-start(bf16[256,512]{1,0:T(8,128)(2,1)S(1)} %get-tuple-element.18.refs_0_), channel_id=1, source_target_pairs={{0,272},{16,256},{256,16},{272,0},{1,273},{17,257},{257,17},{273,1... | collective-permute-start | bytes 786440 | tf_op jit(solution)/shard_map/ppermute | solution.py:180
  26.6 2.6 %collective-permute-start.3 = (bf16[256,512]{1,0:T(8,128)(2,1)S(1)}, bf16[256,512]{1,0:T(8,128)(2,1)S(1)}, u32[]{:S(2)}, u32[]{:S(2)}) collective-permute-start(bf16[256,512]{1,0:T(8,128)(2,1)S(1)} %get-tuple-element.18.refs_0_), channel_id=1, source_target_pairs={{0,16},{16,0},{1,17},{17,1},{2,18},{18,2},{3,19},{19,3},{4,20},{20... | collective-permute-start | bytes 786440 | tf_op jit(solution)/shard_map/ppermute | solution.py:180
  29.2 2.0 %collective-permute-start.1 = (bf16[256,512]{1,0:T(8,128)(2,1)S(1)}, bf16[256,512]{1,0:T(8,128)(2,1)S(1)}, u32[]{:S(2)}, u32[]{:S(2)}) collective-permute-start(bf16[256,512]{1,0:T(8,128)(2,1)S(1)} %get-tuple-element.18.refs_0_), channel_id=1, source_target_pairs={{0,256},{256,0},{1,257},{257,1},{2,258},{258,2},{3,259},{259,3},{4... | collective-permute-start | bytes 786440 | tf_op jit(solution)/shard_map/ppermute | solution.py:180
  31.2 3.7 %collective-permute-start = (bf16[256,512]{1,0:T(8,128)(2,1)S(1)}, bf16[256,512]{1,0:T(8,128)(2,1)S(1)}, u32[]{:S(2)}, u32[]{:S(2)}) collective-permute-start(bf16[256,512]{1,0:T(8,128)(2,1)S(1)} %get-tuple-element.18.refs_0_), channel_id=1, source_target_pairs={{0,8},{8,0},{1,9},{9,1},{2,10},{10,2},{3,11},{11,3},{4,12},{12,4},... | collective-permute-start | bytes 786440 | tf_op jit(solution)/shard_map/ppermute | solution.py:180
  34.9 8.4 %collective-permute-done.5.refs_6_ = bf16[256,512]{1,0:T(8,128)(2,1)S(1)} collective-permute-done((bf16[256,512]{1,0:T(8,128)(2,1)S(1)}, bf16[256,512]{1,0:T(8,128)(2,1)S(1)}, u32[]{:S(2)}, u32[]{:S(2)}) %collective-permute-start.5) | collective-permute-done | bytes 262176 | tf_op jit(solution)/shard_map/ppermute | solution.py:180
  43.3 4.5 %collective-permute-start.6 = (bf16[256,512]{1,0:T(8,128)(2,1)S(1)}, bf16[256,512]{1,0:T(8,128)(2,1)S(1)}, u32[]{:S(2)}, u32[]{:S(2)}) collective-permute-start(bf16[256,512]{1,0:T(8,128)(2,1)S(1)} %collective-permute-done.5.refs_6_), channel_id=1, source_target_pairs={{0,8},{8,0},{1,9},{9,1},{2,10},{10,2},{3,11},{11,3},{4,12},{12,4},... | collective-permute-start | bytes 786440 | tf_op jit(solution)/shard_map/ppermute | solution.py:180
  47.8 1.9 %collective-permute-start.4 = (bf16[256,512]{1,0:T(8,128)(2,1)S(1)}, bf16[256,512]{1,0:T(8,128)(2,1)S(1)}, u32[]{:S(2)}, u32[]{:S(2)}) collective-permute-start(bf16[256,512]{1,0:T(8,128)(2,1)S(1)} %collective-permute-done.3.refs_4_), channel_id=1, source_target_pairs={{0,8},{8,0},{1,9},{9,1},{2,10},{10,2},{3,11},{11,3},{4,12},{12,4},... | collective-permute-start | bytes 786440 | tf_op jit(solution)/shard_map/ppermute | solution.py:180
  49.8 2.4 %collective-permute-start.2 = (bf16[256,512]{1,0:T(8,128)(2,1)S(1)}, bf16[256,512]{1,0:T(8,128)(2,1)S(1)}, u32[]{:S(2)}, u32[]{:S(2)}) collective-permute-start(bf16[256,512]{1,0:T(8,128)(2,1)S(1)} %collective-permute-done.1.refs_2_), channel_id=1, source_target_pairs={{0,8},{8,0},{1,9},{9,1},{2,10},{10,2},{3,11},{11,3},{4,12},{12,4},... | collective-permute-start | bytes 786440 | tf_op jit(solution)/shard_map/ppermute | solution.py:180
  52.2 1.1 collective-permute-done.2.refs_3_
  53.3 0.8 shard_map.77
  54.1 12.4 %all_to_all.25.came = f32[8,72,128]{2,1,0:T(8,128)S(1)} all-to-all(f32[8,72,128]{2,1,0:T(8,128)S(1)} %get-tuple-element.19), channel_id=1, replica_groups=mesh['yh'=2,'zh'=8,'zp'=2,'c'=2,'yl'=2,'x'=4] {'yl','x'}, dimensions={0} | all-to-all | bytes 589824 | tf_op jit(solution)/shard_map/all_to_all | solution.py:184
  66.5 8.9 %all_to_all.26.scores = f32[8,72,128]{2,1,0:T(8,128)S(1)} all-to-all(f32[8,72,128]{2,1,0:T(8,128)S(1)} %shard_map.78), channel_id=1, replica_groups=mesh['yh'=2,'zh'=8,'zp'=2,'c'=2,'yl'=2,'x'=4] {'yl','x'}, dimensions={0} | all-to-all | bytes 589824 | tf_op jit(solution)/shard_map/all_to_all | solution.py:184
  75.5 22.6 %all_to_all.27.stats = f32[8,8,128]{2,1,0:T(8,128)S(1)} all-to-all(f32[8,8,128]{2,1,0:T(8,128)S(1)} %shard_map.79), channel_id=1, replica_groups=mesh['yh'=2,'zh'=8,'zp'=2,'c'=2,'yl'=2,'x'=4] {'zh'}, dimensions={0} | all-to-all | bytes 65536 | tf_op jit(solution)/shard_map/all_to_all | solution.py:184
  98.1 2.8 %shard_map.80 = (bf16[8,32,512]{2,1,0:T(8,128)(2,1)S(1)}, bf16[4,256,512]{2,1,0:T(8,128)(2,1)S(1)}, bf16[4,256,512]{2,1,0:T(8,128)(2,1)}) custom-call(s32[4]{0:T(128)S(1)} %pad_add_fusion.place, f32[8,8,128]{2,1,0:T(8,128)S(1)} %all_to_all.27.stats, f32[8,72,128]{2,1,0:T(8,128)S(1)} %all_to_all.26.scores, s32[8,256]{1,0:T(8,128)S(1)} %get-tuple-element.20.asked, ...), custom_call_target="tpu_custom_call" | custom-call | tf_op jit(solution)/shard_map/pallas_call | solution.py:25
  100.9 0.7 copy-done
  101.5 5.6 %collective-permute-start.7 = (bf16[4,256,512]{2,1,0:T(8,128)(2,1)}, bf16[4,256,512]{2,1,0:T(8,128)(2,1)S(1)}, u32[]{:S(2)}, u32[]{:S(2)}) collective-permute-start(bf16[4,256,512]{2,1,0:T(8,128)(2,1)} %get-tuple-element.24), channel_id=1, source_target_pairs={{0,8},{8,0},{1,9},{9,1},{2,10},{10,2},{3,11},{11,3},{4,12},{12,4},... | collective-permute-start | bytes 3145736 | tf_op jit(solution)/shard_map/ppermute | solution.py:180
  107.1 3.4 %all-to-all-start.4 = ((bf16[8,32,512]{2,1,0:T(8,128)(2,1)}), bf16[8,32,512]{2,1,0:T(8,128)(2,1)S(1)}, u32[]{:S(2)}, u32[]{:S(2)}) async-start(bf16[8,32,512]{2,1,0:T(8,128)(2,1)} %copy-done), calls=%async_computation.4 | async-start | bytes 524288 | tf_op jit(solution)/shard_map/all_to_all | solution.py:184
  110.6 0.9 shard_map.82
  111.4 5.0 %collective-permute-start.8 = (bf16[256,512]{1,0:T(8,128)(2,1)}, bf16[256,512]{1,0:T(8,128)(2,1)S(1)}, u32[]{:S(2)}, u32[]{:S(2)}) collective-permute-start(bf16[256,512]{1,0:T(8,128)(2,1)} %get-tuple-element.26), channel_id=1, source_target_pairs={{0,272},{16,256},{256,16},{272,0},{1,273},{17,257},{257,17},{273,1... | collective-permute-start | bytes 786440 | tf_op jit(solution)/shard_map/ppermute | solution.py:180
  116.4 2.3 %collective-permute-start.9 = (bf16[256,512]{1,0:T(8,128)(2,1)S(1)}, bf16[256,512]{1,0:T(8,128)(2,1)S(1)}, u32[]{:S(2)}, u32[]{:S(2)}) collective-permute-start(bf16[256,512]{1,0:T(8,128)(2,1)S(1)} %get-tuple-element.27), channel_id=1, source_target_pairs={{0,256},{256,0},{1,257},{257,1},{2,258},{258,2},{3,259},{259,3},{4... | collective-permute-start | bytes 786440 | tf_op jit(solution)/shard_map/ppermute | solution.py:180
  118.7 2.6 %collective-permute-start.10 = (bf16[256,512]{1,0:T(8,128)(2,1)S(1)}, bf16[256,512]{1,0:T(8,128)(2,1)S(1)}, u32[]{:S(2)}, u32[]{:S(2)}) collective-permute-start(bf16[256,512]{1,0:T(8,128)(2,1)S(1)} %get-tuple-element.28), channel_id=1, source_target_pairs={{0,16},{16,0},{1,17},{17,1},{2,18},{18,2},{3,19},{19,3},{4,20},{20... | collective-permute-start | bytes 786440 | tf_op jit(solution)/shard_map/ppermute | solution.py:180
  121.3 9.7 %all-to-all-done.4.came = bf16[8,32,512]{2,1,0:T(8,128)(2,1)S(1)} async-done(((bf16[8,32,512]{2,1,0:T(8,128)(2,1)}), bf16[8,32,512]{2,1,0:T(8,128)(2,1)S(1)}, u32[]{:S(2)}, u32[]{:S(2)}) %all-to-all-start.4) | async-done | bytes 262176 | tf_op jit(solution)/shard_map/all_to_all | solution.py:184
  131.0 0.7 shard_map.81
  131.8 1.2 collective-permute-done.9.refs_1_
  133.0 2.0 %collective-permute-done.10.refs_2_ = bf16[256,512]{1,0:T(8,128)(2,1)S(1)} collective-permute-done((bf16[256,512]{1,0:T(8,128)(2,1)S(1)}, bf16[256,512]{1,0:T(8,128)(2,1)S(1)}, u32[]{:S(2)}, u32[]{:S(2)}) %collective-permute-start.10) | collective-permute-done | bytes 262176 | tf_op jit(solution)/shard_map/ppermute | solution.py:180
  135.1 0.8 shard_map.83
  (18 shorter events, 0.3 us)
Async XLA Ops:
  0.6 0.8 copy-start.2
  0.6 0.7 copy-start.4
  1.4 0.9 copy-start.1
  2.3 0.8 copy-start.3
  3.1 0.7 copy-start.5
  5.7 47.7 %all-to-all-start = ((bf16[8,144,128]{2,1,0:T(8,128)(2,1)}), bf16[8,144,128]{2,1,0:T(8,128)(2,1)S(1)}, u32[]{:S(2)}, u32[]{:S(2)}) async-start(bf16[8,144,128]{2,1,0:T(8,128)(2,1)} %get-tuple-element.17), calls=%async_computation | async-start | bytes 589824 | tf_op jit(solution)/shard_map/all_to_all | solution.py:184
  21.3 22.0 %collective-permute-start.5 = (bf16[256,512]{1,0:T(8,128)(2,1)S(1)}, bf16[256,512]{1,0:T(8,128)(2,1)S(1)}, u32[]{:S(2)}, u32[]{:S(2)}) collective-permute-start(bf16[256,512]{1,0:T(8,128)(2,1)S(1)} %get-tuple-element.18.refs_0_), channel_id=1, source_target_pairs={{0,272},{16,256},{256,16},{272,0},{1,273},{17,257},{257,17},{273,1... | collective-permute-start | bytes 786440 | tf_op jit(solution)/shard_map/ppermute | solution.py:180
  26.6 21.3 %collective-permute-start.3 = (bf16[256,512]{1,0:T(8,128)(2,1)S(1)}, bf16[256,512]{1,0:T(8,128)(2,1)S(1)}, u32[]{:S(2)}, u32[]{:S(2)}) collective-permute-start(bf16[256,512]{1,0:T(8,128)(2,1)S(1)} %get-tuple-element.18.refs_0_), channel_id=1, source_target_pairs={{0,16},{16,0},{1,17},{17,1},{2,18},{18,2},{3,19},{19,3},{4,20},{20... | collective-permute-start | bytes 786440 | tf_op jit(solution)/shard_map/ppermute | solution.py:180
  29.2 20.6 %collective-permute-start.1 = (bf16[256,512]{1,0:T(8,128)(2,1)S(1)}, bf16[256,512]{1,0:T(8,128)(2,1)S(1)}, u32[]{:S(2)}, u32[]{:S(2)}) collective-permute-start(bf16[256,512]{1,0:T(8,128)(2,1)S(1)} %get-tuple-element.18.refs_0_), channel_id=1, source_target_pairs={{0,256},{256,0},{1,257},{257,1},{2,258},{258,2},{3,259},{259,3},{4... | collective-permute-start | bytes 786440 | tf_op jit(solution)/shard_map/ppermute | solution.py:180
  31.2 21.0 %collective-permute-start = (bf16[256,512]{1,0:T(8,128)(2,1)S(1)}, bf16[256,512]{1,0:T(8,128)(2,1)S(1)}, u32[]{:S(2)}, u32[]{:S(2)}) collective-permute-start(bf16[256,512]{1,0:T(8,128)(2,1)S(1)} %get-tuple-element.18.refs_0_), channel_id=1, source_target_pairs={{0,8},{8,0},{1,9},{9,1},{2,10},{10,2},{3,11},{11,3},{4,12},{12,4},... | collective-permute-start | bytes 786440 | tf_op jit(solution)/shard_map/ppermute | solution.py:180
  43.3 8.9 %collective-permute-start.6 = (bf16[256,512]{1,0:T(8,128)(2,1)S(1)}, bf16[256,512]{1,0:T(8,128)(2,1)S(1)}, u32[]{:S(2)}, u32[]{:S(2)}) collective-permute-start(bf16[256,512]{1,0:T(8,128)(2,1)S(1)} %collective-permute-done.5.refs_6_), channel_id=1, source_target_pairs={{0,8},{8,0},{1,9},{9,1},{2,10},{10,2},{3,11},{11,3},{4,12},{12,4},... | collective-permute-start | bytes 786440 | tf_op jit(solution)/shard_map/ppermute | solution.py:180
  47.8 4.4 %collective-permute-start.4 = (bf16[256,512]{1,0:T(8,128)(2,1)S(1)}, bf16[256,512]{1,0:T(8,128)(2,1)S(1)}, u32[]{:S(2)}, u32[]{:S(2)}) collective-permute-start(bf16[256,512]{1,0:T(8,128)(2,1)S(1)} %collective-permute-done.3.refs_4_), channel_id=1, source_target_pairs={{0,8},{8,0},{1,9},{9,1},{2,10},{10,2},{3,11},{11,3},{4,12},{12,4},... | collective-permute-start | bytes 786440 | tf_op jit(solution)/shard_map/ppermute | solution.py:180
  49.8 3.6 %collective-permute-start.2 = (bf16[256,512]{1,0:T(8,128)(2,1)S(1)}, bf16[256,512]{1,0:T(8,128)(2,1)S(1)}, u32[]{:S(2)}, u32[]{:S(2)}) collective-permute-start(bf16[256,512]{1,0:T(8,128)(2,1)S(1)} %collective-permute-done.1.refs_2_), channel_id=1, source_target_pairs={{0,8},{8,0},{1,9},{9,1},{2,10},{10,2},{3,11},{11,3},{4,12},{12,4},... | collective-permute-start | bytes 786440 | tf_op jit(solution)/shard_map/ppermute | solution.py:180
  100.9 0.7 copy-start
  101.5 9.0 %collective-permute-start.7 = (bf16[4,256,512]{2,1,0:T(8,128)(2,1)}, bf16[4,256,512]{2,1,0:T(8,128)(2,1)S(1)}, u32[]{:S(2)}, u32[]{:S(2)}) collective-permute-start(bf16[4,256,512]{2,1,0:T(8,128)(2,1)} %get-tuple-element.24), channel_id=1, source_target_pairs={{0,8},{8,0},{1,9},{9,1},{2,10},{10,2},{3,11},{11,3},{4,12},{12,4},... | collective-permute-start | bytes 3145736 | tf_op jit(solution)/shard_map/ppermute | solution.py:180
  107.1 23.9 %all-to-all-start.4 = ((bf16[8,32,512]{2,1,0:T(8,128)(2,1)}), bf16[8,32,512]{2,1,0:T(8,128)(2,1)S(1)}, u32[]{:S(2)}, u32[]{:S(2)}) async-start(bf16[8,32,512]{2,1,0:T(8,128)(2,1)} %copy-done), calls=%async_computation.4 | async-start | bytes 524288 | tf_op jit(solution)/shard_map/all_to_all | solution.py:184
  111.4 20.3 %collective-permute-start.8 = (bf16[256,512]{1,0:T(8,128)(2,1)}, bf16[256,512]{1,0:T(8,128)(2,1)S(1)}, u32[]{:S(2)}, u32[]{:S(2)}) collective-permute-start(bf16[256,512]{1,0:T(8,128)(2,1)} %get-tuple-element.26), channel_id=1, source_target_pairs={{0,272},{16,256},{256,16},{272,0},{1,273},{17,257},{257,17},{273,1... | collective-permute-start | bytes 786440 | tf_op jit(solution)/shard_map/ppermute | solution.py:180
  116.4 16.6 %collective-permute-start.9 = (bf16[256,512]{1,0:T(8,128)(2,1)S(1)}, bf16[256,512]{1,0:T(8,128)(2,1)S(1)}, u32[]{:S(2)}, u32[]{:S(2)}) collective-permute-start(bf16[256,512]{1,0:T(8,128)(2,1)S(1)} %get-tuple-element.27), channel_id=1, source_target_pairs={{0,256},{256,0},{1,257},{257,1},{2,258},{258,2},{3,259},{259,3},{4... | collective-permute-start | bytes 786440 | tf_op jit(solution)/shard_map/ppermute | solution.py:180
  118.7 16.4 %collective-permute-start.10 = (bf16[256,512]{1,0:T(8,128)(2,1)S(1)}, bf16[256,512]{1,0:T(8,128)(2,1)S(1)}, u32[]{:S(2)}, u32[]{:S(2)}) collective-permute-start(bf16[256,512]{1,0:T(8,128)(2,1)S(1)} %get-tuple-element.28), channel_id=1, source_target_pairs={{0,16},{16,0},{1,17},{17,1},{2,18},{18,2},{3,19},{19,3},{4,20},{20... | collective-permute-start | bytes 786440 | tf_op jit(solution)/shard_map/ppermute | solution.py:180

commit v3 on v1

v3 whole, which is shorter than its diff:
```python
import math

import jax
import jax.numpy as jnp
from jax import lax
from jax.experimental import pallas as pl
from jax.experimental.pallas import tpu as pltpu
from jax.sharding import Mesh
from jax.sharding import PartitionSpec as P

BF16 = jnp.bfloat16
F32 = jnp.float32
NZ = 16
NH = 8
NB = 4
ROWS = 512
ABSENT = -1e30
VMEM_LIMIT = 48 * 1024 * 1024
PACK_LIMIT = 62 * 1024 * 1024


def call(kernel, out_shapes, *args, smem=0, hbm=0, scratch=(), limit=VMEM_LIMIT):
    specs = [pl.BlockSpec(memory_space=pltpu.SMEM)] * smem
    specs += [pl.BlockSpec(memory_space=pl.ANY)] * hbm
    specs += [pl.BlockSpec(memory_space=pltpu.VMEM)] * (len(args) - smem - hbm)
    return pl.pallas_call(
        kernel,
        out_shape=[jax.ShapeDtypeStruct(shape, dtype) for shape, dtype in out_shapes],
        in_specs=specs,
        out_specs=[pl.BlockSpec(memory_space=pltpu.VMEM)] * len(out_shapes),
        scratch_shapes=list(scratch),
        compiler_params=pltpu.CompilerParams(vmem_limit_bytes=limit),
    )(*args)


def pack_kernel(place, queries, owners, rows, sent, mine, short, wide, sems):
    copies = [
        pltpu.make_async_copy(owners, short.at[0], sems.at[0]),
        pltpu.make_async_copy(rows, short.at[1], sems.at[1]),
        pltpu.make_async_copy(queries, mine, sems.at[2]),
    ]
    for copy in copies:
        copy.start()
    yh, zh, zp, c = place[0], place[1], place[2], place[3]
    line = lax.broadcasted_iota(jnp.int32, (NH * 16, 128), 0)
    lane = lax.broadcasted_iota(jnp.int32, (NH * 16, 128), 1)
    block = line % 16
    z = (line // 16) * 2 + (zp ^ (block // 4))
    owner = ((yh ^ (block // 2 % 2)) * NZ + z) * 2 + (c ^ (block % 2))
    owner = jnp.where((block < 2 * NB) & (lane // 32 == zh % 4), owner, -2)
    copies[0].wait()
    copies[1].wait()
    for j in range(4):
        wide[:, :, j * 32 : (j + 1) * 32] = short[...]
    asked = jnp.full((NH * 16, 128), -1, jnp.int32)
    for k in range(short.shape[1]):
        asked = jnp.where(wide[0, k : k + 1, :] == owner, wide[1, k : k + 1, :], asked)
    asked = asked.astype(F32).astype(BF16)
    for to in range(NH):
        sent[to, 128:144, :] = asked[to * 16 : (to + 1) * 16, :]
    copies[2].wait()
    for to in range(NH):
        for l in range(4):
            sent[to, l * 32 : (l + 1) * 32, :] = mine[:, l * 128 : (l + 1) * 128]


def column_pack_kernel(passages, negatives, columns, sems):
    copies = [
        pltpu.make_async_copy(negatives, columns.at[32:256], sems.at[0]),
        pltpu.make_async_copy(passages, columns.at[0:32], sems.at[1]),
    ]
    for copy in copies:
        copy.start()
    for copy in copies:
        copy.wait()


def score_kernel(near, far, col0, col1, col2, col3, parts, queries, asked):
    scale = 3.0 / math.sqrt(4096)
    for s, came in enumerate((near, far)):
        for z in range(NH):
            for l in range(4):
                rows = slice((s * NH + z) * 32, (s * NH + z + 1) * 32)
                queries[rows, l * 128 : (l + 1) * 128] = came[z, l * 32 : (l + 1) * 32, :]
        for g in range(2):
            rows = came[4 * g, 128:144, :].astype(F32)
            for z in range(4 * g + 1, 4 * g + 4):
                rows = jnp.maximum(rows, came[z, 128:144, :].astype(F32))
            rows = rows[s * NB : (s + 1) * NB, :].astype(jnp.int32)
            asked[0:NB, (2 * s + g) * 128 : (2 * s + g + 1) * 128] = rows
    asked[NB:8, :] = jnp.full((8 - NB, ROWS), -1, jnp.int32)
    every = queries[...]
    place = lax.broadcasted_iota(jnp.int32, (224, ROWS), 0)
    for o, cols in enumerate((col0, col1, col2, col3)):
        part = lax.dot_general(cols[...], every, (((1,), (1,)), ((), ())), preferred_element_type=F32)
        want = asked[o : o + 1, :]
        hard = jnp.sum(jnp.where(place == want, part[32:256, :], 0.0), axis=0, keepdims=True) * scale
        hard = jnp.where(want >= 0, hard, ABSENT)
        h, a = o // 2, o % 2
        for l in range(4):
            lanes = slice(l * 128, (l + 1) * 128)
            parts[h * 4 + l, a * 32 : (a + 1) * 32, :] = part[0:32, lanes] * scale
            parts[h * 4 + l, 64 + a : 65 + a, :] = hard[:, lanes]
            if a == 1:
                parts[h * 4 + l, 66:72, :] = jnp.zeros((6, 128), F32)


def add_kernel(came, sent):
    total = came[0]
    for i in range(1, 8):
        total = total + came[i]
    for i in range(8):
        sent[i] = total


def stat_kernel(place, scores, sent, tops):
    zp = place[2]
    pairs = []
    for l in range(4):
        batch = [scores[h * 4 + l, 0:64, :] for h in range(2)]
        hard = [scores[h * 4 + l, 64:66, :] for h in range(2)]
        top = jnp.maximum(
            jnp.max(jnp.maximum(batch[0], batch[1]), axis=0, keepdims=True),
            jnp.max(jnp.maximum(hard[0], hard[1]), axis=0, keepdims=True),
        )
        total = jnp.sum(jnp.exp(batch[0] - top) + jnp.exp(batch[1] - top), axis=0, keepdims=True)
        total = total + jnp.sum(jnp.exp(hard[0] - top) + jnp.exp(hard[1] - top), axis=0, keepdims=True)
        pairs.append((top, total))
    tops[...] = jnp.concatenate([top for top, _ in pairs], axis=1)
    for l in range(4):
        for k in range(2):
            row = jnp.where(zp == 0, pairs[l][k], pairs[l ^ 2][k])
            for to in range(NZ):
                sent[to, 4 * k + l : 4 * k + l + 1, :] = row


def block_scores(scores, o):
    h, a = o // 2, o % 2
    batch = jnp.concatenate([scores[h * 4 + l, a * 32 : (a + 1) * 32, :] for l in range(4)], axis=1)
    hard = jnp.concatenate([scores[h * 4 + l, 64 + a : 65 + a, :] for l in range(4)], axis=1)
    return batch, hard


def block_weights(batch, hard, want):
    line = lax.broadcasted_iota(jnp.int32, (224, ROWS), 0)
    hard = jnp.where(line == want, hard, 0.0)
    return jnp.concatenate([batch.astype(BF16), hard.astype(BF16)], axis=0)


def is_target(zh):
    row = lax.broadcasted_iota(jnp.int32, (32, ROWS), 0)
    lane = lax.broadcasted_iota(jnp.int32, (32, ROWS), 1)
    return lane == zh * 32 + row


def share_kernel(place, scores, tops, asked, col0, col1, col2, col3, keep, give, q_acc):
    top = tops[...]
    for o, cols in enumerate((col0, col1, col2, col3)):
        batch, hard = block_scores(scores, o)
        weights = jnp.exp(batch - top)
        if o == 0:
            weights = jnp.where(is_target(place[1]), 0.0, weights)
        both = block_weights(weights, jnp.exp(hard - top), asked[o : o + 1, :])
        term = lax.dot_general(both, cols[...], (((0,), (0,)), ((), ())), preferred_element_type=F32)
        if o == 0:
            q_acc[...] = term
        elif o < NB - 1:
            q_acc[...] += term
        else:
            total = (q_acc[...] + term).astype(BF16)
            keep[...] = total[0:256, :]
            give[...] = total[256:512, :]


def join_kernel(place, stats, keep, came, sent, logs):
    z, zp = place[1] * 2 + place[2], place[2]
    absolute = []
    for l in range(4):
        tops = stats[:, l, :]
        top = jnp.max(tops, axis=0, keepdims=True)
        absolute.append(top + jnp.log(jnp.sum(stats[:, 4 + l, :] * jnp.exp(tops - top), axis=0, keepdims=True)))
    mine = stats[z]
    other = stats[z ^ 1]
    relative = [jnp.where(zp == 0, absolute[l], absolute[l ^ 2]) for l in range(4)]
    logs[...] = jnp.concatenate(relative, axis=1)
    rows = []
    for tops in (mine, other):
        for l in range(2):
            rows.append(jnp.exp(jnp.where(zp == 0, tops[l : l + 1, :], tops[l + 2 : l + 3, :]) - relative[l]))
    factors = jnp.concatenate(rows + [jnp.zeros((124, 128), F32)], axis=0).T
    for l in range(2):
        lines = slice(l * 128, (l + 1) * 128)
        total = keep[lines, :].astype(F32) * factors[:, l : l + 1] + came[lines, :].astype(F32) * factors[:, 2 + l : 3 + l]
        sent[l * 4 : (l + 1) * 4] = total.astype(BF16).reshape(4, 32, 512)


def column_grad_kernel(place, logs, scores, asked, queries, keep, give, at_target):
    log_total = logs[...]
    every = queries[...]
    for o in range(NB):
        batch, hard = block_scores(scores, o)
        weights = jnp.exp(batch - log_total)
        if o == 0:
            target = is_target(place[1])
            weights = jnp.where(target, weights - 1.0, weights)
            own = jnp.sum(jnp.where(target, weights, 0.0), axis=1, keepdims=True)
            at_target[...] = jnp.broadcast_to(own.astype(BF16).astype(F32), (32, 128))
        both = block_weights(weights, jnp.exp(hard - log_total), asked[o : o + 1, :])
        (give if o % 2 else keep)[o // 2] = jnp.dot(both, every, preferred_element_type=F32).astype(BF16)


def pair_kernel(keep, came, own, sent):
    own[...] = keep[0].astype(F32) + came[0].astype(F32)
    sent[...] = (keep[1].astype(F32) + came[1].astype(F32)).astype(BF16)


def column_kernel(own, came, passage_out, negative_out):
    passage_out[...] = (own[0:32, :] + came[0:32, :].astype(F32)).astype(BF16)
    negative_out[...] = (own[32:256, :] + came[32:256, :].astype(F32)).astype(BF16)


def query_kernel(came, at_target, passages, query_out):
    total = at_target[:, 0:1] * passages[...].astype(F32)
    for z in range(NH):
        total = total + came[z].astype(F32)
    query_out[...] = total.astype(BF16)


def swap(x, axis):
    return lax.ppermute(x, axis, [(0, 1), (1, 0)])


def exchange(x, axes):
    return lax.all_to_all(x, axes, split_axis=0, concat_axis=0, tiled=True)


def shards(queries, passages, negatives, hard_owner, hard_row):
    place = jnp.stack([lax.axis_index(axis) for axis in ("yh", "zh", "zp", "c")]).astype(jnp.int32)
    (sent,) = call(
        pack_kernel, [((NH, 144, 128), BF16)],
        place, queries, hard_owner.T, hard_row.T, smem=1, hbm=3, limit=PACK_LIMIT,
        scratch=[
            pltpu.VMEM((32, 512), BF16), pltpu.VMEM((2, 7, 32), jnp.int32), pltpu.VMEM((2, 7, 128), jnp.int32),
            pltpu.SemaphoreType.DMA((3,)),
        ],
    )
    near = exchange(sent, "zh")
    far = swap(near, "zp")
    (col0,) = call(
        column_pack_kernel, [((256, 512), BF16)], passages, negatives, hbm=2, limit=PACK_LIMIT,
        scratch=[pltpu.SemaphoreType.DMA((2,))],
    )
    col2 = swap(col0, "yh")
    col1 = swap(col0, "c")
    col3 = swap(col2, "c")
    parts, every, asked = call(
        score_kernel, [((8, 72, 128), F32), ((ROWS, 512), BF16), ((8, ROWS), jnp.int32)],
        near, far, col0, col1, col2, col3,
    )
    (summed,) = call(add_kernel, [((8, 72, 128), F32)], exchange(parts, ("yl", "x")))
    scores = exchange(summed, ("yl", "x"))
    stats, tops = call(stat_kernel, [((NZ, 8, 128), F32), ((1, ROWS), F32)], place, scores, smem=1)
    stats = exchange(stats, ("zh", "zp"))
    q_keep, q_give = call(
        share_kernel, [((256, 512), BF16), ((256, 512), BF16)],
        place, scores, tops, asked, col0, col1, col2, col3, smem=1, scratch=[pltpu.VMEM((ROWS, 512), F32)],
    )
    q_pair, logs = call(
        join_kernel, [((NH, 32, 512), BF16), ((1, ROWS), F32)], place, stats, q_keep, swap(q_give, "zp"), smem=1
    )
    q_came = exchange(q_pair, "zh")
    keep, give, at_target = call(
        column_grad_kernel, [((2, 256, 512), BF16), ((2, 256, 512), BF16), ((32, 128), F32)],
        place, logs, scores, asked, every, smem=1,
    )
    own, cross = call(pair_kernel, [((256, 512), F32), ((256, 512), BF16)], keep, swap(give, "c"))
    cross = swap(cross, "yh")
    passage_out, negative_out = call(column_kernel, [((32, 512), BF16), ((224, 512), BF16)], own, cross)
    (query_out,) = call(query_kernel, [((32, 512), BF16)], q_came, at_target, passages)
    return (query_out, passage_out, negative_out)


def solution(mesh):
    fine = Mesh(mesh.devices.reshape(2, NH, 2, 2, 2, 4), ("yh", "zh", "zp", "c", "yl", "x"))
    dp, mp = ("yh", "zh", "zp", "c"), ("yl", "x")
    return jax.shard_map(
        shards,
        mesh=fine,
        in_specs=(P(dp, mp), P(dp, mp), P(dp, mp), P(dp, None), P(dp, None)),
        out_specs=(P(dp, mp), P(dp, mp), P(dp, mp)),
        check_vma=False,
    )
```

time: 127 us -> 122 us (0.961)
  the two profiles are of different devices: /device:TPU:16 before, /device:TPU:1 now
where the time goes in v3:
time: 122 us; the launch traced here: 121 us
  starting transfers between devices  50.4 us (41%)
  blocking collectives  36.6 us (30%)
  waiting for transfers between devices  20.5 us (17%)
  Pallas kernels  11.1 us (9%)
    all_to_all x3, blocking collectives, exchange(): return lax.all_to_all(x, axes, split_axis=0, concat_axis=0, tiled=True)  36.6 us
    ppermute x7, starting transfers between devices, swap(): return lax.ppermute(x, axis, [(0, 1), (1, 0)])  31.4 us
    all_to_all x2, starting transfers between devices, exchange(): return lax.all_to_all(x, axes, split_axis=0, concat_axis=0, tiled=True)  19.1 us
    all_to_all x2, waiting for transfers between devices, exchange(): return lax.all_to_all(x, axes, split_axis=0, concat_axis=0, tiled=True)  11.2 us
    pallas_call x11, Pallas kernels, call(): pl.pallas_call(kernel, out_shape=[jax.ShapeDtypeStruct(shape, dtype) for...  11.1 us
    ppermute x7, waiting for transfers between devices, swap(): return lax.ppermute(x, axis, [(0, 1), (1, 0)])  9.35 us
  transfers between devices with their start and end apart: 9, of which 4 were waited for; matrix products, arithmetic and copies ran while one was open for 0% of the time, Pallas kernels for 3%

profile of v3, /device:TPU:1, one launch (start us, length us, event | category | flops | bytes accessed | tf_op | source)
XLA Modules:
  0.0 121.0 jit_solution(1519522976616811209)
XLA Ops:
  0.6 0.7 pad_add_fusion.place
  1.3 2.2 %shard_map.76 = bf16[8,144,128]{2,1,0:T(8,128)(2,1)} custom-call(s32[4]{0:T(128)} %pad_add_fusion.place, bf16[32,512]{1,0:T(8,128)(2,1)} %queries.1, s32[7,32]{1,0:T(8,128)} %bitcast.6, s32[7,32]{1,0:T(8,128)} %bitcast.7), custom_call_target="tpu_custom_call" | custom-call | tf_op jit(solution)/shard_map/pallas_call | solution.py:26
  3.5 15.7 %all-to-all-start = ((bf16[8,144,128]{2,1,0:T(8,128)(2,1)}), bf16[8,144,128]{2,1,0:T(8,128)(2,1)S(1)}, u32[]{:S(2)}, u32[]{:S(2)}) async-start(bf16[8,144,128]{2,1,0:T(8,128)(2,1)} %shard_map.76), calls=%async_computation | async-start | bytes 589824 | tf_op jit(solution)/shard_map/all_to_all | solution.py:234
  19.2 1.7 %shard_map.77.col0 = bf16[256,512]{1,0:T(8,128)(2,1)} custom-call(bf16[32,512]{1,0:T(8,128)(2,1)} %passages.3, bf16[224,512]{1,0:T(8,128)(2,1)} %negatives.1), custom_call_target="tpu_custom_call" | custom-call | tf_op jit(solution)/shard_map/pallas_call | solution.py:26
  20.9 4.8 %collective-permute-start.2 = (bf16[256,512]{1,0:T(8,128)(2,1)}, bf16[256,512]{1,0:T(8,128)(2,1)S(1)}, u32[]{:S(2)}, u32[]{:S(2)}) collective-permute-start(bf16[256,512]{1,0:T(8,128)(2,1)} %shard_map.77.col0), channel_id=1, source_target_pairs={{0,256},{256,0},{1,257},{257,1},{2,258},{258,2},{3,259},{259,3},{4... | collective-permute-start | bytes 786440 | tf_op jit(solution)/shard_map/ppermute | solution.py:230
  25.7 11.2 %all-to-all-done.near = bf16[8,144,128]{2,1,0:T(8,128)(2,1)S(1)} async-done(((bf16[8,144,128]{2,1,0:T(8,128)(2,1)}), bf16[8,144,128]{2,1,0:T(8,128)(2,1)S(1)}, u32[]{:S(2)}, u32[]{:S(2)}) %all-to-all-start) | async-done | bytes 294944 | tf_op jit(solution)/shard_map/all_to_all | solution.py:234
  36.9 2.4 %collective-permute-start = (bf16[8,144,128]{2,1,0:T(8,128)(2,1)S(1)}, bf16[8,144,128]{2,1,0:T(8,128)(2,1)S(1)}, u32[]{:S(2)}, u32[]{:S(2)}) collective-permute-start(bf16[8,144,128]{2,1,0:T(8,128)(2,1)S(1)} %all-to-all-done.near), channel_id=1, source_target_pairs={{0,16},{16,0},{1,17},{17,1},{2,18},{18,2},{3,19},{19,3},{4,20},{20... | collective-permute-start | bytes 884744 | tf_op jit(solution)/shard_map/ppermute | solution.py:230
  39.2 7.5 %collective-permute-start.1 = (bf16[256,512]{1,0:T(8,128)(2,1)}, bf16[256,512]{1,0:T(8,128)(2,1)S(1)}, u32[]{:S(2)}, u32[]{:S(2)}) collective-permute-start(bf16[256,512]{1,0:T(8,128)(2,1)} %shard_map.77.col0), channel_id=1, source_target_pairs={{0,8},{8,0},{1,9},{9,1},{2,10},{10,2},{3,11},{11,3},{4,12},{12,4},... | collective-permute-start | bytes 786440 | tf_op jit(solution)/shard_map/ppermute | solution.py:230
  46.7 0.0 collective-permute-done.2.col2
  46.7 1.9 %collective-permute-start.3 = (bf16[256,512]{1,0:T(8,128)(2,1)S(1)}, bf16[256,512]{1,0:T(8,128)(2,1)S(1)}, u32[]{:S(2)}, u32[]{:S(2)}) collective-permute-start(bf16[256,512]{1,0:T(8,128)(2,1)S(1)} %collective-permute-done.2.col2), channel_id=1, source_target_pairs={{0,8},{8,0},{1,9},{9,1},{2,10},{10,2},{3,11},{11,3},{4,12},{12,4},... | collective-permute-start | bytes 786440 | tf_op jit(solution)/shard_map/ppermute | solution.py:230
  48.7 0.0 collective-permute-done.1.col1
  48.7 1.5 %collective-permute-done.3.col3 = bf16[256,512]{1,0:T(8,128)(2,1)S(1)} collective-permute-done((bf16[256,512]{1,0:T(8,128)(2,1)S(1)}, bf16[256,512]{1,0:T(8,128)(2,1)S(1)}, u32[]{:S(2)}, u32[]{:S(2)}) %collective-permute-start.3) | collective-permute-done | bytes 262176 | tf_op jit(solution)/shard_map/ppermute | solution.py:230
  50.2 0.9 copy-done
  51.1 0.8 shard_map.78
  51.9 12.4 %all_to_all.25.came = f32[8,72,128]{2,1,0:T(8,128)S(1)} all-to-all(f32[8,72,128]{2,1,0:T(8,128)S(1)} %get-tuple-element.19), channel_id=1, replica_groups=mesh['yh'=2,'zh'=8,'zp'=2,'c'=2,'yl'=2,'x'=4] {'yl','x'}, dimensions={0} | all-to-all | bytes 589824 | tf_op jit(solution)/shard_map/all_to_all | solution.py:234
  64.4 9.0 %all_to_all.26.scores = f32[8,72,128]{2,1,0:T(8,128)S(1)} all-to-all(f32[8,72,128]{2,1,0:T(8,128)S(1)} %shard_map.79), channel_id=1, replica_groups=mesh['yh'=2,'zh'=8,'zp'=2,'c'=2,'yl'=2,'x'=4] {'yl','x'}, dimensions={0} | all-to-all | bytes 589824 | tf_op jit(solution)/shard_map/all_to_all | solution.py:234
  73.3 0.6 shard_map.80
  74.0 1.3 %shard_map.81 = (bf16[256,512]{1,0:T(8,128)(2,1)S(1)}, bf16[256,512]{1,0:T(8,128)(2,1)S(1)}) custom-call(s32[4]{0:T(128)S(1)} %copy-done.2, f32[8,72,128]{2,1,0:T(8,128)S(1)} %all_to_all.26.scores, f32[1,512]{1,0:T(1,128)S(1)} %get-tuple-element.21.tops, s32[8,512]{1,0:T(8,128)S(1)} %get-tuple-element.22.asked, bf16[256,512]{1,0:T(8,128)(2,1)S(1)} %copy-done, ...), custom_call_target="tpu_custom_call" | custom-call | tf_op jit(solution)/shard_map/pallas_call | solution.py:26
  75.3 2.8 %collective-permute-start.4 = (bf16[256,512]{1,0:T(8,128)(2,1)S(1)}, bf16[256,512]{1,0:T(8,128)(2,1)S(1)}, u32[]{:S(2)}, u32[]{:S(2)}) collective-permute-start(bf16[256,512]{1,0:T(8,128)(2,1)S(1)} %get-tuple-element.24), channel_id=1, source_target_pairs={{0,16},{16,0},{1,17},{17,1},{2,18},{18,2},{3,19},{19,3},{4,20},{20... | collective-permute-start | bytes 786440 | tf_op jit(solution)/shard_map/ppermute | solution.py:230
  78.1 15.2 %all_to_all.27.stats = f32[16,8,128]{2,1,0:T(8,128)S(1)} all-to-all(f32[16,8,128]{2,1,0:T(8,128)S(1)} %get-tuple-element.20), channel_id=1, replica_groups=mesh['yh'=2,'zh'=8,'zp'=2,'c'=2,'yl'=2,'x'=4] {'zh','zp'}, dimensions={0} | all-to-all | bytes 131072 | tf_op jit(solution)/shard_map/all_to_all | solution.py:234
  93.2 0.0 collective-permute-done.4.came
  93.2 1.6 %shard_map.82 = (bf16[8,32,512]{2,1,0:T(8,128)(2,1)}, f32[1,512]{1,0:T(1,128)S(1)}) custom-call(s32[4]{0:T(128)S(1)} %copy-done.2, f32[16,8,128]{2,1,0:T(8,128)S(1)} %all_to_all.27.stats, bf16[256,512]{1,0:T(8,128)(2,1)S(1)} %get-tuple-element.23.keep, bf16[256,512]{1,0:T(8,128)(2,1)S(1)} %collective-permute-done.4.came), custom_call_target="tpu_custom_call" | custom-call | tf_op jit(solution)/shard_map/pallas_call | solution.py:26
  94.8 3.4 %all-to-all-start.4 = ((bf16[8,32,512]{2,1,0:T(8,128)(2,1)}), bf16[8,32,512]{2,1,0:T(8,128)(2,1)S(1)}, u32[]{:S(2)}, u32[]{:S(2)}) async-start(bf16[8,32,512]{2,1,0:T(8,128)(2,1)} %get-tuple-element.25), calls=%async_computation.4 | async-start | bytes 524288 | tf_op jit(solution)/shard_map/all_to_all | solution.py:234
  98.2 1.3 %shard_map.83 = (bf16[2,256,512]{2,1,0:T(8,128)(2,1)S(1)}, bf16[2,256,512]{2,1,0:T(8,128)(2,1)S(1)}, f32[32,128]{1,0:T(8,128)S(1)}) custom-call(s32[4]{0:T(128)S(1)} %copy-done.2, f32[1,512]{1,0:T(1,128)S(1)} %get-tuple-element.26.logs, f32[8,72,128]{2,1,0:T(8,128)S(1)} %all_to_all.26.scores, s32[8,512]{1,0:T(8,128)S(1)} %get-tuple-element.22.asked, ...), custom_call_target="tpu_custom_call" | custom-call | tf_op jit(solution)/shard_map/pallas_call | solution.py:26
  99.5 7.4 %collective-permute-start.5 = (bf16[2,256,512]{2,1,0:T(8,128)(2,1)S(1)}, bf16[2,256,512]{2,1,0:T(8,128)(2,1)S(1)}, u32[]{:S(2)}, u32[]{:S(2)}) collective-permute-start(bf16[2,256,512]{2,1,0:T(8,128)(2,1)S(1)} %get-tuple-element.30), channel_id=1, source_target_pairs={{0,8},{8,0},{1,9},{9,1},{2,10},{10,2},{3,11},{11,3},{4,12},{12,4},... | collective-permute-start | bytes 1572872 | tf_op jit(solution)/shard_map/ppermute | solution.py:230
  107.0 1.5 %collective-permute-done.5.came = bf16[2,256,512]{2,1,0:T(8,128)(2,1)S(1)} collective-permute-done((bf16[2,256,512]{2,1,0:T(8,128)(2,1)S(1)}, bf16[2,256,512]{2,1,0:T(8,128)(2,1)S(1)}, u32[]{:S(2)}, u32[]{:S(2)}) %collective-permute-start.5) | collective-permute-done | bytes 524320 | tf_op jit(solution)/shard_map/ppermute | solution.py:230
  108.5 0.1 shard_map.85
  108.6 4.6 %collective-permute-start.6 = (bf16[256,512]{1,0:T(8,128)(2,1)S(1)}, bf16[256,512]{1,0:T(8,128)(2,1)S(1)}, u32[]{:S(2)}, u32[]{:S(2)}) collective-permute-start(bf16[256,512]{1,0:T(8,128)(2,1)S(1)} %get-tuple-element.32), channel_id=1, source_target_pairs={{0,256},{256,0},{1,257},{257,1},{2,258},{258,2},{3,259},{259,3},{4... | collective-permute-start | bytes 786440 | tf_op jit(solution)/shard_map/ppermute | solution.py:230
  113.2 6.3 %collective-permute-done.6.came = bf16[256,512]{1,0:T(8,128)(2,1)S(1)} collective-permute-done((bf16[256,512]{1,0:T(8,128)(2,1)S(1)}, bf16[256,512]{1,0:T(8,128)(2,1)S(1)}, u32[]{:S(2)}, u32[]{:S(2)}) %collective-permute-start.6) | collective-permute-done | bytes 262176 | tf_op jit(solution)/shard_map/ppermute | solution.py:230
  119.5 0.7 shard_map.86
  120.2 0.0 copy-done.1
  120.3 0.7 shard_map.84
  (7 shorter events, 0.0 us)
Async XLA Ops:
  3.5 33.3 %all-to-all-start = ((bf16[8,144,128]{2,1,0:T(8,128)(2,1)}), bf16[8,144,128]{2,1,0:T(8,128)(2,1)S(1)}, u32[]{:S(2)}, u32[]{:S(2)}) async-start(bf16[8,144,128]{2,1,0:T(8,128)(2,1)} %shard_map.76), calls=%async_computation | async-start | bytes 589824 | tf_op jit(solution)/shard_map/all_to_all | solution.py:234
  20.9 25.9 %collective-permute-start.2 = (bf16[256,512]{1,0:T(8,128)(2,1)}, bf16[256,512]{1,0:T(8,128)(2,1)S(1)}, u32[]{:S(2)}, u32[]{:S(2)}) collective-permute-start(bf16[256,512]{1,0:T(8,128)(2,1)} %shard_map.77.col0), channel_id=1, source_target_pairs={{0,256},{256,0},{1,257},{257,1},{2,258},{258,2},{3,259},{259,3},{4... | collective-permute-start | bytes 786440 | tf_op jit(solution)/shard_map/ppermute | solution.py:230
  36.9 13.3 %collective-permute-start = (bf16[8,144,128]{2,1,0:T(8,128)(2,1)S(1)}, bf16[8,144,128]{2,1,0:T(8,128)(2,1)S(1)}, u32[]{:S(2)}, u32[]{:S(2)}) collective-permute-start(bf16[8,144,128]{2,1,0:T(8,128)(2,1)S(1)} %all-to-all-done.near), channel_id=1, source_target_pairs={{0,16},{16,0},{1,17},{17,1},{2,18},{18,2},{3,19},{19,3},{4,20},{20... | collective-permute-start | bytes 884744 | tf_op jit(solution)/shard_map/ppermute | solution.py:230
  39.2 9.4 %collective-permute-start.1 = (bf16[256,512]{1,0:T(8,128)(2,1)}, bf16[256,512]{1,0:T(8,128)(2,1)S(1)}, u32[]{:S(2)}, u32[]{:S(2)}) collective-permute-start(bf16[256,512]{1,0:T(8,128)(2,1)} %shard_map.77.col0), channel_id=1, source_target_pairs={{0,8},{8,0},{1,9},{9,1},{2,10},{10,2},{3,11},{11,3},{4,12},{12,4},... | collective-permute-start | bytes 786440 | tf_op jit(solution)/shard_map/ppermute | solution.py:230
  46.7 3.4 %collective-permute-start.3 = (bf16[256,512]{1,0:T(8,128)(2,1)S(1)}, bf16[256,512]{1,0:T(8,128)(2,1)S(1)}, u32[]{:S(2)}, u32[]{:S(2)}) collective-permute-start(bf16[256,512]{1,0:T(8,128)(2,1)S(1)} %collective-permute-done.2.col2), channel_id=1, source_target_pairs={{0,8},{8,0},{1,9},{9,1},{2,10},{10,2},{3,11},{11,3},{4,12},{12,4},... | collective-permute-start | bytes 786440 | tf_op jit(solution)/shard_map/ppermute | solution.py:230
  50.2 1.0 copy-start
  64.4 9.0 %copy-start.2 = (s32[4]{0:T(128)S(1)}, s32[4]{0:T(128)}, u32[]{:S(2)}) copy-start(s32[4]{0:T(128)} %pad_add_fusion.place) | copy-start | bytes 52
  75.3 18.0 %collective-permute-start.4 = (bf16[256,512]{1,0:T(8,128)(2,1)S(1)}, bf16[256,512]{1,0:T(8,128)(2,1)S(1)}, u32[]{:S(2)}, u32[]{:S(2)}) collective-permute-start(bf16[256,512]{1,0:T(8,128)(2,1)S(1)} %get-tuple-element.24), channel_id=1, source_target_pairs={{0,16},{16,0},{1,17},{17,1},{2,18},{18,2},{3,19},{19,3},{4,20},{20... | collective-permute-start | bytes 786440 | tf_op jit(solution)/shard_map/ppermute | solution.py:230
  94.8 25.4 %all-to-all-start.4 = ((bf16[8,32,512]{2,1,0:T(8,128)(2,1)}), bf16[8,32,512]{2,1,0:T(8,128)(2,1)S(1)}, u32[]{:S(2)}, u32[]{:S(2)}) async-start(bf16[8,32,512]{2,1,0:T(8,128)(2,1)} %get-tuple-element.25), calls=%async_computation.4 | async-start | bytes 524288 | tf_op jit(solution)/shard_map/all_to_all | solution.py:234
  99.5 8.9 %collective-permute-start.5 = (bf16[2,256,512]{2,1,0:T(8,128)(2,1)S(1)}, bf16[2,256,512]{2,1,0:T(8,128)(2,1)S(1)}, u32[]{:S(2)}, u32[]{:S(2)}) collective-permute-start(bf16[2,256,512]{2,1,0:T(8,128)(2,1)S(1)} %get-tuple-element.30), channel_id=1, source_target_pairs={{0,8},{8,0},{1,9},{9,1},{2,10},{10,2},{3,11},{11,3},{4,12},{12,4},... | collective-permute-start | bytes 1572872 | tf_op jit(solution)/shard_map/ppermute | solution.py:230
  108.6 10.9 %collective-permute-start.6 = (bf16[256,512]{1,0:T(8,128)(2,1)S(1)}, bf16[256,512]{1,0:T(8,128)(2,1)S(1)}, u32[]{:S(2)}, u32[]{:S(2)}) collective-permute-start(bf16[256,512]{1,0:T(8,128)(2,1)S(1)} %get-tuple-element.32), channel_id=1, source_target_pairs={{0,256},{256,0},{1,257},{257,1},{2,258},{258,2},{3,259},{259,3},{4... | collective-permute-start | bytes 786440 | tf_op jit(solution)/shard_map/ppermute | solution.py:230
  119.5 0.8 copy-start.1

commit v4 on v3

--- a/solution.py
+++ b/solution.py
@@ -19,10 +19,9 @@
 PACK_LIMIT = 62 * 1024 * 1024
 
 
-def call(kernel, out_shapes, *args, smem=0, hbm=0, scratch=(), limit=VMEM_LIMIT):
-    specs = [pl.BlockSpec(memory_space=pltpu.SMEM)] * smem
-    specs += [pl.BlockSpec(memory_space=pl.ANY)] * hbm
-    specs += [pl.BlockSpec(memory_space=pltpu.VMEM)] * (len(args) - smem - hbm)
+def call(kernel, out_shapes, *args, hbm=0, scratch=(), limit=VMEM_LIMIT):
+    specs = [pl.BlockSpec(memory_space=pl.ANY)] * hbm
+    specs += [pl.BlockSpec(memory_space=pltpu.VMEM)] * (len(args) - hbm)
     return pl.pallas_call(
         kernel,
         out_shape=[jax.ShapeDtypeStruct(shape, dtype) for shape, dtype in out_shapes],
@@ -33,7 +32,7 @@
     )(*args)
 
 
-def pack_kernel(place, queries, owners, rows, sent, mine, short, wide, sems):
+def pack_kernel(queries, owners, rows, sent, mine, short, wide, sems):
     copies = [
         pltpu.make_async_copy(owners, short.at[0], sems.at[0]),
         pltpu.make_async_copy(rows, short.at[1], sems.at[1]),
@@ -41,7 +40,7 @@
     ]
     for copy in copies:
         copy.start()
-    yh, zh, zp, c = place[0], place[1], place[2], place[3]
+    yh, zh, zp, c = (lax.axis_index(axis) for axis in ("yh", "zh", "zp", "c"))
     line = lax.broadcasted_iota(jnp.int32, (NH * 16, 128), 0)
     lane = lax.broadcasted_iota(jnp.int32, (NH * 16, 128), 1)
     block = line % 16
@@ -113,8 +112,8 @@
         sent[i] = total
 
 
-def stat_kernel(place, scores, sent, tops):
-    zp = place[2]
+def stat_kernel(scores, sent, tops):
+    zp = lax.axis_index("zp")
     pairs = []
     for l in range(4):
         batch = [scores[h * 4 + l, 0:64, :] for h in range(2)]
@@ -147,19 +146,21 @@
     return jnp.concatenate([batch.astype(BF16), hard.astype(BF16)], axis=0)
 
 
-def is_target(zh):
+def is_target():
+    zh = lax.axis_index("zh")
     row = lax.broadcasted_iota(jnp.int32, (32, ROWS), 0)
     lane = lax.broadcasted_iota(jnp.int32, (32, ROWS), 1)
     return lane == zh * 32 + row
 
 
-def share_kernel(place, scores, tops, asked, col0, col1, col2, col3, keep, give, q_acc):
+def share_kernel(scores, tops, asked, col0, col1, col2, col3, keep, *refs):
+    give, q_acc = refs[:-1], refs[-1]
     top = tops[...]
     for o, cols in enumerate((col0, col1, col2, col3)):
         batch, hard = block_scores(scores, o)
         weights = jnp.exp(batch - top)
         if o == 0:
-            weights = jnp.where(is_target(place[1]), 0.0, weights)
+            weights = jnp.where(is_target(), 0.0, weights)
         both = block_weights(weights, jnp.exp(hard - top), asked[o : o + 1, :])
         term = lax.dot_general(both, cols[...], (((0,), (0,)), ((), ())), preferred_element_type=F32)
         if o == 0:
@@ -169,11 +170,14 @@
         else:
             total = (q_acc[...] + term).astype(BF16)
             keep[...] = total[0:256, :]
-            give[...] = total[256:512, :]
-
-
-def join_kernel(place, stats, keep, came, sent, logs):
-    z, zp = place[1] * 2 + place[2], place[2]
+            for i, piece in enumerate(give):
+                piece[...] = total[256 + i * 128 : 256 + (i + 1) * 128, :]
+
+
+def join_kernel(stats, keep, *refs):
+    came, (sent, logs) = refs[:-2], refs[-2:]
+    zp = lax.axis_index("zp")
+    z = lax.axis_index("zh") * 2 + zp
     absolute = []
     for l in range(4):
         tops = stats[:, l, :]
@@ -190,18 +194,19 @@
     factors = jnp.concatenate(rows + [jnp.zeros((124, 128), F32)], axis=0).T
     for l in range(2):
         lines = slice(l * 128, (l + 1) * 128)
-        total = keep[lines, :].astype(F32) * factors[:, l : l + 1] + came[lines, :].astype(F32) * factors[:, 2 + l : 3 + l]
+        other = jnp.concatenate([piece[...] for piece in came[l * 1 : (l + 1) * 1]], axis=0).astype(F32)
+        total = keep[lines, :].astype(F32) * factors[:, l : l + 1] + other * factors[:, 2 + l : 3 + l]
         sent[l * 4 : (l + 1) * 4] = total.astype(BF16).reshape(4, 32, 512)
 
 
-def column_grad_kernel(place, logs, scores, asked, queries, keep, give, at_target):
+def column_grad_kernel(logs, scores, asked, queries, keep, give, at_target):
     log_total = logs[...]
     every = queries[...]
     for o in range(NB):
         batch, hard = block_scores(scores, o)
         weights = jnp.exp(batch - log_total)
         if o == 0:
-            target = is_target(place[1])
+            target = is_target()
             weights = jnp.where(target, weights - 1.0, weights)
             own = jnp.sum(jnp.where(target, weights, 0.0), axis=1, keepdims=True)
             at_target[...] = jnp.broadcast_to(own.astype(BF16).astype(F32), (32, 128))
@@ -235,10 +240,9 @@
 
 
 def shards(queries, passages, negatives, hard_owner, hard_row):
-    place = jnp.stack([lax.axis_index(axis) for axis in ("yh", "zh", "zp", "c")]).astype(jnp.int32)
     (sent,) = call(
         pack_kernel, [((NH, 144, 128), BF16)],
-        place, queries, hard_owner.T, hard_row.T, smem=1, hbm=3, limit=PACK_LIMIT,
+        queries, hard_owner.T, hard_row.T, hbm=3, limit=PACK_LIMIT,
         scratch=[
             pltpu.VMEM((32, 512), BF16), pltpu.VMEM((2, 7, 32), jnp.int32), pltpu.VMEM((2, 7, 128), jnp.int32),
             pltpu.SemaphoreType.DMA((3,)),
@@ -247,7 +251,7 @@
     near = exchange(sent, "zh")
     far = swap(near, "zp")
     (col0,) = call(
-        column_pack_kernel, [((256, 512), BF16)], passages, negatives, hbm=2, limit=PACK_LIMIT,
+        column_pack_kernel, [((256, 512), BF16)], passages, negatives, hbm=2,
         scratch=[pltpu.SemaphoreType.DMA((2,))],
     )
     col2 = swap(col0, "yh")
@@ -259,19 +263,19 @@
     )
     (summed,) = call(add_kernel, [((8, 72, 128), F32)], exchange(parts, ("yl", "x")))
     scores = exchange(summed, ("yl", "x"))
-    stats, tops = call(stat_kernel, [((NZ, 8, 128), F32), ((1, ROWS), F32)], place, scores, smem=1)
+    stats, tops = call(stat_kernel, [((NZ, 8, 128), F32), ((1, ROWS), F32)], scores)
     stats = exchange(stats, ("zh", "zp"))
-    q_keep, q_give = call(
-        share_kernel, [((256, 512), BF16), ((256, 512), BF16)],
-        place, scores, tops, asked, col0, col1, col2, col3, smem=1, scratch=[pltpu.VMEM((ROWS, 512), F32)],
+    q_keep, *q_give = call(
+        share_kernel, [((256, 512), BF16)] + [((128, 512), BF16)] * 2,
+        scores, tops, asked, col0, col1, col2, col3, scratch=[pltpu.VMEM((ROWS, 512), F32)],
     )
     q_pair, logs = call(
-        join_kernel, [((NH, 32, 512), BF16), ((1, ROWS), F32)], place, stats, q_keep, swap(q_give, "zp"), smem=1
+        join_kernel, [((NH, 32, 512), BF16), ((1, ROWS), F32)], stats, q_keep, *[swap(piece, "zp") for piece in q_give]
     )
     q_came = exchange(q_pair, "zh")
     keep, give, at_target = call(
         column_grad_kernel, [((2, 256, 512), BF16), ((2, 256, 512), BF16), ((32, 128), F32)],
-        place, logs, scores, asked, every, smem=1,
+        logs, scores, asked, every,
     )
     own, cross = call(pair_kernel, [((256, 512), F32), ((256, 512), BF16)], keep, swap(give, "c"))
     cross = swap(cross, "yh")

time: 122 us -> 120 us (0.984)
  blocking collectives: 36.6 us -> 21.4 us
  starting transfers between devices: 50.4 us -> 62 us
  waiting for transfers between devices: 20.5 us -> 27.3 us
  Pallas kernels: 11.1 us -> 7.57 us
    all_to_all x3 -> x2, blocking collectives: 36.6 us -> 21.4 us  [exchange(): return lax.all_to_all(x, axes, split_axis=0, concat_axis=0, tiled=True)]
    all_to_all x2 -> x3, starting transfers between devices: 19.1 us -> 28.6 us  [exchange(): return lax.all_to_all(x, axes, split_axis=0, concat_axis=0, tiled=True)]
    ppermute x7 -> x8, waiting for transfers between devices: 9.35 us -> 14.9 us  [swap(): return lax.ppermute(x, axis, [(0, 1), (1, 0)])]
    pallas_call x11, Pallas kernels: 11.1 us -> 7.57 us  [call(): pl.pallas_call(kernel, out_shape=[jax.ShapeDtypeStruct(shape, dtype) for...]
    ppermute x7 -> x8, starting transfers between devices: 31.4 us -> 33.4 us  [swap(): return lax.ppermute(x, axis, [(0, 1), (1, 0)])]
    all_to_all x2 -> x3, waiting for transfers between devices: 11.2 us -> 12.5 us  [exchange(): return lax.all_to_all(x, axes, split_axis=0, concat_axis=0, tiled=True)]
  transfers between devices with their start and end apart: 9 -> 11, of which waited for: 4 -> 6; matrix products, arithmetic and copies ran while one was open for 0% -> 0% of each run, Pallas kernels for 3% -> 2%
where the time goes in v4:
time: 120 us; the launch traced here: 119 us
  starting transfers between devices  62 us (52%)
  waiting for transfers between devices  27.3 us (23%)
  blocking collectives  21.4 us (18%)
  Pallas kernels  7.57 us (6%)
    ppermute x8, starting transfers between devices, swap(): return lax.ppermute(x, axis, [(0, 1), (1, 0)])  33.4 us
    all_to_all x3, starting transfers between devices, exchange(): return lax.all_to_all(x, axes, split_axis=0, concat_axis=0, tiled=True)  28.6 us
    all_to_all x2, blocking collectives, exchange(): return lax.all_to_all(x, axes, split_axis=0, concat_axis=0, tiled=True)  21.4 us
    ppermute x8, waiting for transfers between devices, swap(): return lax.ppermute(x, axis, [(0, 1), (1, 0)])  14.9 us
    all_to_all x3, waiting for transfers between devices, exchange(): return lax.all_to_all(x, axes, split_axis=0, concat_axis=0, tiled=True)  12.5 us
    pallas_call x11, Pallas kernels, call(): pl.pallas_call(kernel, out_shape=[jax.ShapeDtypeStruct(shape, dtype) for...  7.57 us
  transfers between devices with their start and end apart: 11, of which 6 were waited for; matrix products, arithmetic and copies ran while one was open for 0% of the time, Pallas kernels for 2%

profile of v4, /device:TPU:1, one launch (start us, length us, event | category | flops | bytes accessed | tf_op | source)
XLA Modules:
  0.0 119.1 jit_solution(5768990866435048954)
XLA Ops:
  0.6 1.6 %shard_map.76 = bf16[8,144,128]{2,1,0:T(8,128)(2,1)} custom-call(bf16[32,512]{1,0:T(8,128)(2,1)} %queries.1, s32[7,32]{1,0:T(8,128)} %bitcast.2, s32[7,32]{1,0:T(8,128)} %bitcast.3), custom_call_target="tpu_custom_call" | custom-call | tf_op jit(solution)/shard_map/pallas_call | solution.py:25
  2.2 0.0 copy-start
  2.2 0.0 copy-start.1
  2.3 15.8 %all-to-all-start = ((bf16[8,144,128]{2,1,0:T(8,128)(2,1)}), bf16[8,144,128]{2,1,0:T(8,128)(2,1)S(1)}, u32[]{:S(2)}, u32[]{:S(2)}) async-start(bf16[8,144,128]{2,1,0:T(8,128)(2,1)} %shard_map.76), calls=%async_computation | async-start | bytes 589824 | tf_op jit(solution)/shard_map/all_to_all | solution.py:239
  18.1 0.4 shard_map.77.col0
  18.4 4.8 %collective-permute-start.2 = (bf16[256,512]{1,0:T(8,128)(2,1)S(1)}, bf16[256,512]{1,0:T(8,128)(2,1)S(1)}, u32[]{:S(2)}, u32[]{:S(2)}) collective-permute-start(bf16[256,512]{1,0:T(8,128)(2,1)S(1)} %shard_map.77.col0), channel_id=1, source_target_pairs={{0,256},{256,0},{1,257},{257,1},{2,258},{258,2},{3,259},{259,3},{4... | collective-permute-start | bytes 786440 | tf_op jit(solution)/shard_map/ppermute | solution.py:235
  23.3 12.4 %all-to-all-done.near = bf16[8,144,128]{2,1,0:T(8,128)(2,1)S(1)} async-done(((bf16[8,144,128]{2,1,0:T(8,128)(2,1)}), bf16[8,144,128]{2,1,0:T(8,128)(2,1)S(1)}, u32[]{:S(2)}, u32[]{:S(2)}) %all-to-all-start) | async-done | bytes 294944 | tf_op jit(solution)/shard_map/all_to_all | solution.py:239
  35.7 2.4 %collective-permute-start = (bf16[8,144,128]{2,1,0:T(8,128)(2,1)S(1)}, bf16[8,144,128]{2,1,0:T(8,128)(2,1)S(1)}, u32[]{:S(2)}, u32[]{:S(2)}) collective-permute-start(bf16[8,144,128]{2,1,0:T(8,128)(2,1)S(1)} %all-to-all-done.near), channel_id=1, source_target_pairs={{0,16},{16,0},{1,17},{17,1},{2,18},{18,2},{3,19},{19,3},{4,20},{20... | collective-permute-start | bytes 884744 | tf_op jit(solution)/shard_map/ppermute | solution.py:235
  38.1 7.5 %collective-permute-start.1 = (bf16[256,512]{1,0:T(8,128)(2,1)S(1)}, bf16[256,512]{1,0:T(8,128)(2,1)S(1)}, u32[]{:S(2)}, u32[]{:S(2)}) collective-permute-start(bf16[256,512]{1,0:T(8,128)(2,1)S(1)} %shard_map.77.col0), channel_id=1, source_target_pairs={{0,8},{8,0},{1,9},{9,1},{2,10},{10,2},{3,11},{11,3},{4,12},{12,4},... | collective-permute-start | bytes 786440 | tf_op jit(solution)/shard_map/ppermute | solution.py:235
  45.6 1.9 %collective-permute-start.3 = (bf16[256,512]{1,0:T(8,128)(2,1)S(1)}, bf16[256,512]{1,0:T(8,128)(2,1)S(1)}, u32[]{:S(2)}, u32[]{:S(2)}) collective-permute-start(bf16[256,512]{1,0:T(8,128)(2,1)S(1)} %collective-permute-done.2.col2), channel_id=1, source_target_pairs={{0,8},{8,0},{1,9},{9,1},{2,10},{10,2},{3,11},{11,3},{4,12},{12,4},... | collective-permute-start | bytes 786440 | tf_op jit(solution)/shard_map/ppermute | solution.py:235
  47.5 1.5 %collective-permute-done.3.col3 = bf16[256,512]{1,0:T(8,128)(2,1)S(1)} collective-permute-done((bf16[256,512]{1,0:T(8,128)(2,1)S(1)}, bf16[256,512]{1,0:T(8,128)(2,1)S(1)}, u32[]{:S(2)}, u32[]{:S(2)}) %collective-permute-start.3) | collective-permute-done | bytes 262176 | tf_op jit(solution)/shard_map/ppermute | solution.py:235
  49.0 0.8 shard_map.78
  49.8 12.4 %all_to_all.25.came = f32[8,72,128]{2,1,0:T(8,128)S(1)} all-to-all(f32[8,72,128]{2,1,0:T(8,128)S(1)} %get-tuple-element.20), channel_id=1, replica_groups=mesh['yh'=2,'zh'=8,'zp'=2,'c'=2,'yl'=2,'x'=4] {'yl','x'}, dimensions={0} | all-to-all | bytes 589824 | tf_op jit(solution)/shard_map/all_to_all | solution.py:239
  62.3 9.0 %all_to_all.26.scores = f32[8,72,128]{2,1,0:T(8,128)S(1)} all-to-all(f32[8,72,128]{2,1,0:T(8,128)S(1)} %shard_map.79), channel_id=1, replica_groups=mesh['yh'=2,'zh'=8,'zp'=2,'c'=2,'yl'=2,'x'=4] {'yl','x'}, dimensions={0} | all-to-all | bytes 589824 | tf_op jit(solution)/shard_map/all_to_all | solution.py:239
  71.2 0.7 shard_map.80
  71.9 3.7 %all-to-all-start.3 = ((f32[16,8,128]{2,1,0:T(8,128)}), f32[16,8,128]{2,1,0:T(8,128)S(1)}, u32[]{:S(2)}, u32[]{:S(2)}) async-start(f32[16,8,128]{2,1,0:T(8,128)} %get-tuple-element.21), calls=%async_computation.3 | async-start | bytes 131072 | tf_op jit(solution)/shard_map/all_to_all | solution.py:239
  75.7 0.8 shard_map.81
  76.4 3.3 %collective-permute-start.4 = (bf16[128,512]{1,0:T(8,128)(2,1)S(1)}, bf16[128,512]{1,0:T(8,128)(2,1)S(1)}, u32[]{:S(2)}, u32[]{:S(2)}) collective-permute-start(bf16[128,512]{1,0:T(8,128)(2,1)S(1)} %get-tuple-element.25), channel_id=1, source_target_pairs={{0,16},{16,0},{1,17},{17,1},{2,18},{18,2},{3,19},{19,3},{4,20},{20... | collective-permute-start | bytes 393224 | tf_op jit(solution)/shard_map/ppermute | solution.py:235
  79.7 2.0 %collective-permute-start.5 = (bf16[128,512]{1,0:T(8,128)(2,1)S(1)}, bf16[128,512]{1,0:T(8,128)(2,1)S(1)}, u32[]{:S(2)}, u32[]{:S(2)}) collective-permute-start(bf16[128,512]{1,0:T(8,128)(2,1)S(1)} %get-tuple-element.26), channel_id=1, source_target_pairs={{0,16},{16,0},{1,17},{17,1},{2,18},{18,2},{3,19},{19,3},{4,20},{20... | collective-permute-start | bytes 393224 | tf_op jit(solution)/shard_map/ppermute | solution.py:235
  81.7 0.5 collective-permute-done.4.refs_0_
  82.3 4.9 %collective-permute-done.5.refs_1_ = bf16[128,512]{1,0:T(8,128)(2,1)S(1)} collective-permute-done((bf16[128,512]{1,0:T(8,128)(2,1)S(1)}, bf16[128,512]{1,0:T(8,128)(2,1)S(1)}, u32[]{:S(2)}, u32[]{:S(2)}) %collective-permute-start.5) | collective-permute-done | bytes 131104 | tf_op jit(solution)/shard_map/ppermute | solution.py:235
  87.2 0.0 all-to-all-done.3.stats
  87.3 1.0 shard_map.82
  88.3 9.1 %all-to-all-start.4 = ((bf16[8,32,512]{2,1,0:T(8,128)(2,1)}), bf16[8,32,512]{2,1,0:T(8,128)(2,1)S(1)}, u32[]{:S(2)}, u32[]{:S(2)}) async-start(bf16[8,32,512]{2,1,0:T(8,128)(2,1)} %get-tuple-element.27), calls=%async_computation.4 | async-start | bytes 524288 | tf_op jit(solution)/shard_map/all_to_all | solution.py:239
  97.4 0.7 shard_map.83
  98.1 7.0 %collective-permute-start.6 = (bf16[2,256,512]{2,1,0:T(8,128)(2,1)S(1)}, bf16[2,256,512]{2,1,0:T(8,128)(2,1)S(1)}, u32[]{:S(2)}, u32[]{:S(2)}) collective-permute-start(bf16[2,256,512]{2,1,0:T(8,128)(2,1)S(1)} %get-tuple-element.32), channel_id=1, source_target_pairs={{0,8},{8,0},{1,9},{9,1},{2,10},{10,2},{3,11},{11,3},{4,12},{12,4},... | collective-permute-start | bytes 1572872 | tf_op jit(solution)/shard_map/ppermute | solution.py:235
  105.1 1.5 %collective-permute-done.6.came = bf16[2,256,512]{2,1,0:T(8,128)(2,1)S(1)} collective-permute-done((bf16[2,256,512]{2,1,0:T(8,128)(2,1)S(1)}, bf16[2,256,512]{2,1,0:T(8,128)(2,1)S(1)}, u32[]{:S(2)}, u32[]{:S(2)}) %collective-permute-start.6) | collective-permute-done | bytes 524320 | tf_op jit(solution)/shard_map/ppermute | solution.py:235
  106.6 0.1 shard_map.85
  106.7 4.5 %collective-permute-start.7 = (bf16[256,512]{1,0:T(8,128)(2,1)S(1)}, bf16[256,512]{1,0:T(8,128)(2,1)S(1)}, u32[]{:S(2)}, u32[]{:S(2)}) collective-permute-start(bf16[256,512]{1,0:T(8,128)(2,1)S(1)} %get-tuple-element.34), channel_id=1, source_target_pairs={{0,256},{256,0},{1,257},{257,1},{2,258},{258,2},{3,259},{259,3},{4... | collective-permute-start | bytes 786440 | tf_op jit(solution)/shard_map/ppermute | solution.py:235
  111.3 6.4 %collective-permute-done.7.came = bf16[256,512]{1,0:T(8,128)(2,1)S(1)} collective-permute-done((bf16[256,512]{1,0:T(8,128)(2,1)S(1)}, bf16[256,512]{1,0:T(8,128)(2,1)S(1)}, u32[]{:S(2)}, u32[]{:S(2)}) %collective-permute-start.7) | collective-permute-done | bytes 262176 | tf_op jit(solution)/shard_map/ppermute | solution.py:235
  117.6 0.7 shard_map.86
  118.4 0.7 shard_map.84
  (7 shorter events, 0.0 us)
Async XLA Ops:
  2.2 15.8 %copy-start = (bf16[224,512]{1,0:T(8,128)(2,1)S(1)}, bf16[224,512]{1,0:T(8,128)(2,1)}, u32[]{:S(2)}) copy-start(bf16[224,512]{1,0:T(8,128)(2,1)} %negatives.1) | copy-start | bytes 688132
  2.2 15.8 %copy-start.1 = (bf16[32,512]{1,0:T(8,128)(2,1)S(1)}, bf16[32,512]{1,0:T(8,128)(2,1)}, u32[]{:S(2)}) copy-start(bf16[32,512]{1,0:T(8,128)(2,1)} %passages.3) | copy-start | bytes 98308
  2.3 33.4 %all-to-all-start = ((bf16[8,144,128]{2,1,0:T(8,128)(2,1)}), bf16[8,144,128]{2,1,0:T(8,128)(2,1)S(1)}, u32[]{:S(2)}, u32[]{:S(2)}) async-start(bf16[8,144,128]{2,1,0:T(8,128)(2,1)} %shard_map.76), calls=%async_computation | async-start | bytes 589824 | tf_op jit(solution)/shard_map/all_to_all | solution.py:239
  18.4 27.1 %collective-permute-start.2 = (bf16[256,512]{1,0:T(8,128)(2,1)S(1)}, bf16[256,512]{1,0:T(8,128)(2,1)S(1)}, u32[]{:S(2)}, u32[]{:S(2)}) collective-permute-start(bf16[256,512]{1,0:T(8,128)(2,1)S(1)} %shard_map.77.col0), channel_id=1, source_target_pairs={{0,256},{256,0},{1,257},{257,1},{2,258},{258,2},{3,259},{259,3},{4... | collective-permute-start | bytes 786440 | tf_op jit(solution)/shard_map/ppermute | solution.py:235
  35.7 13.3 %collective-permute-start = (bf16[8,144,128]{2,1,0:T(8,128)(2,1)S(1)}, bf16[8,144,128]{2,1,0:T(8,128)(2,1)S(1)}, u32[]{:S(2)}, u32[]{:S(2)}) collective-permute-start(bf16[8,144,128]{2,1,0:T(8,128)(2,1)S(1)} %all-to-all-done.near), channel_id=1, source_target_pairs={{0,16},{16,0},{1,17},{17,1},{2,18},{18,2},{3,19},{19,3},{4,20},{20... | collective-permute-start | bytes 884744 | tf_op jit(solution)/shard_map/ppermute | solution.py:235
  38.1 9.4 %collective-permute-start.1 = (bf16[256,512]{1,0:T(8,128)(2,1)S(1)}, bf16[256,512]{1,0:T(8,128)(2,1)S(1)}, u32[]{:S(2)}, u32[]{:S(2)}) collective-permute-start(bf16[256,512]{1,0:T(8,128)(2,1)S(1)} %shard_map.77.col0), channel_id=1, source_target_pairs={{0,8},{8,0},{1,9},{9,1},{2,10},{10,2},{3,11},{11,3},{4,12},{12,4},... | collective-permute-start | bytes 786440 | tf_op jit(solution)/shard_map/ppermute | solution.py:235
  45.6 3.4 %collective-permute-start.3 = (bf16[256,512]{1,0:T(8,128)(2,1)S(1)}, bf16[256,512]{1,0:T(8,128)(2,1)S(1)}, u32[]{:S(2)}, u32[]{:S(2)}) collective-permute-start(bf16[256,512]{1,0:T(8,128)(2,1)S(1)} %collective-permute-done.2.col2), channel_id=1, source_target_pairs={{0,8},{8,0},{1,9},{9,1},{2,10},{10,2},{3,11},{11,3},{4,12},{12,4},... | collective-permute-start | bytes 786440 | tf_op jit(solution)/shard_map/ppermute | solution.py:235
  71.9 15.3 %all-to-all-start.3 = ((f32[16,8,128]{2,1,0:T(8,128)}), f32[16,8,128]{2,1,0:T(8,128)S(1)}, u32[]{:S(2)}, u32[]{:S(2)}) async-start(f32[16,8,128]{2,1,0:T(8,128)} %get-tuple-element.21), calls=%async_computation.3 | async-start | bytes 131072 | tf_op jit(solution)/shard_map/all_to_all | solution.py:239
  76.4 5.8 %collective-permute-start.4 = (bf16[128,512]{1,0:T(8,128)(2,1)S(1)}, bf16[128,512]{1,0:T(8,128)(2,1)S(1)}, u32[]{:S(2)}, u32[]{:S(2)}) collective-permute-start(bf16[128,512]{1,0:T(8,128)(2,1)S(1)} %get-tuple-element.25), channel_id=1, source_target_pairs={{0,16},{16,0},{1,17},{17,1},{2,18},{18,2},{3,19},{19,3},{4,20},{20... | collective-permute-start | bytes 393224 | tf_op jit(solution)/shard_map/ppermute | solution.py:235
  79.7 7.5 %collective-permute-start.5 = (bf16[128,512]{1,0:T(8,128)(2,1)S(1)}, bf16[128,512]{1,0:T(8,128)(2,1)S(1)}, u32[]{:S(2)}, u32[]{:S(2)}) collective-permute-start(bf16[128,512]{1,0:T(8,128)(2,1)S(1)} %get-tuple-element.26), channel_id=1, source_target_pairs={{0,16},{16,0},{1,17},{17,1},{2,18},{18,2},{3,19},{19,3},{4,20},{20... | collective-permute-start | bytes 393224 | tf_op jit(solution)/shard_map/ppermute | solution.py:235
  88.3 30.1 %all-to-all-start.4 = ((bf16[8,32,512]{2,1,0:T(8,128)(2,1)}), bf16[8,32,512]{2,1,0:T(8,128)(2,1)S(1)}, u32[]{:S(2)}, u32[]{:S(2)}) async-start(bf16[8,32,512]{2,1,0:T(8,128)(2,1)} %get-tuple-element.27), calls=%async_computation.4 | async-start | bytes 524288 | tf_op jit(solution)/shard_map/all_to_all | solution.py:239
  98.1 8.5 %collective-permute-start.6 = (bf16[2,256,512]{2,1,0:T(8,128)(2,1)S(1)}, bf16[2,256,512]{2,1,0:T(8,128)(2,1)S(1)}, u32[]{:S(2)}, u32[]{:S(2)}) collective-permute-start(bf16[2,256,512]{2,1,0:T(8,128)(2,1)S(1)} %get-tuple-element.32), channel_id=1, source_target_pairs={{0,8},{8,0},{1,9},{9,1},{2,10},{10,2},{3,11},{11,3},{4,12},{12,4},... | collective-permute-start | bytes 1572872 | tf_op jit(solution)/shard_map/ppermute | solution.py:235
  106.7 10.9 %collective-permute-start.7 = (bf16[256,512]{1,0:T(8,128)(2,1)S(1)}, bf16[256,512]{1,0:T(8,128)(2,1)S(1)}, u32[]{:S(2)}, u32[]{:S(2)}) collective-permute-start(bf16[256,512]{1,0:T(8,128)(2,1)S(1)} %get-tuple-element.34), channel_id=1, source_target_pairs={{0,256},{256,0},{1,257},{257,1},{2,258},{258,2},{3,259},{259,3},{4... | collective-permute-start | bytes 786440 | tf_op jit(solution)/shard_map/ppermute | solution.py:235

commit v5 on v4

--- a/solution.py
+++ b/solution.py
@@ -174,33 +174,16 @@
                 piece[...] = total[256 + i * 128 : 256 + (i + 1) * 128, :]
 
 
-def join_kernel(stats, keep, *refs):
-    came, (sent, logs) = refs[:-2], refs[-2:]
+def column_grad_kernel(*refs):
+    stats, scores, asked, queries, keep, give, at_target, logs = refs[2:]
     zp = lax.axis_index("zp")
-    z = lax.axis_index("zh") * 2 + zp
     absolute = []
     for l in range(4):
         tops = stats[:, l, :]
         top = jnp.max(tops, axis=0, keepdims=True)
         absolute.append(top + jnp.log(jnp.sum(stats[:, 4 + l, :] * jnp.exp(tops - top), axis=0, keepdims=True)))
-    mine = stats[z]
-    other = stats[z ^ 1]
-    relative = [jnp.where(zp == 0, absolute[l], absolute[l ^ 2]) for l in range(4)]
-    logs[...] = jnp.concatenate(relative, axis=1)
-    rows = []
-    for tops in (mine, other):
-        for l in range(2):
-            rows.append(jnp.exp(jnp.where(zp == 0, tops[l : l + 1, :], tops[l + 2 : l + 3, :]) - relative[l]))
-    factors = jnp.concatenate(rows + [jnp.zeros((124, 128), F32)], axis=0).T
-    for l in range(2):
-        lines = slice(l * 128, (l + 1) * 128)
-        other = jnp.concatenate([piece[...] for piece in came[l * 1 : (l + 1) * 1]], axis=0).astype(F32)
-        total = keep[lines, :].astype(F32) * factors[:, l : l + 1] + other * factors[:, 2 + l : 3 + l]
-        sent[l * 4 : (l + 1) * 4] = total.astype(BF16).reshape(4, 32, 512)
-
-
-def column_grad_kernel(logs, scores, asked, queries, keep, give, at_target):
-    log_total = logs[...]
+    log_total = jnp.concatenate([jnp.where(zp == 0, absolute[l], absolute[l ^ 2]) for l in range(4)], axis=1)
+    logs[...] = log_total
     every = queries[...]
     for o in range(NB):
         batch, hard = block_scores(scores, o)
@@ -211,12 +194,29 @@
             own = jnp.sum(jnp.where(target, weights, 0.0), axis=1, keepdims=True)
             at_target[...] = jnp.broadcast_to(own.astype(BF16).astype(F32), (32, 128))
         both = block_weights(weights, jnp.exp(hard - log_total), asked[o : o + 1, :])
-        (give if o % 2 else keep)[o // 2] = jnp.dot(both, every, preferred_element_type=F32).astype(BF16)
+        (give if o % 2 else keep)[o // 2] = jnp.dot(both, every, preferred_element_type=F32)
+
+
+def join_kernel(stats, logs, keep, *refs):
+    came, (sent,) = refs[:-1], refs[-1:]
+    zp = lax.axis_index("zp")
+    z = lax.axis_index("zh") * 2 + zp
+    rows = []
+    for tops in (stats[z], stats[z ^ 1]):
+        for l in range(2):
+            top = jnp.where(zp == 0, tops[l : l + 1, :], tops[l + 2 : l + 3, :])
+            rows.append(jnp.exp(top - logs[:, l * 128 : (l + 1) * 128]))
+    factors = jnp.concatenate(rows + [jnp.zeros((124, 128), F32)], axis=0).T
+    for l in range(2):
+        lines = slice(l * 128, (l + 1) * 128)
+        total = keep[lines, :].astype(F32) * factors[:, l : l + 1]
+        total = total + came[l][...].astype(F32) * factors[:, 2 + l : 3 + l]
+        sent[l * 4 : (l + 1) * 4] = total.astype(BF16).reshape(4, 32, 512)
 
 
 def pair_kernel(keep, came, own, sent):
-    own[...] = keep[0].astype(F32) + came[0].astype(F32)
-    sent[...] = (keep[1].astype(F32) + came[1].astype(F32)).astype(BF16)
+    own[...] = keep[0] + came[0]
+    sent[...] = (keep[1] + came[1]).astype(BF16)
 
 
 def column_kernel(own, came, passage_out, negative_out):
@@ -269,14 +269,14 @@
         share_kernel, [((256, 512), BF16)] + [((128, 512), BF16)] * 2,
         scores, tops, asked, col0, col1, col2, col3, scratch=[pltpu.VMEM((ROWS, 512), F32)],
     )
-    q_pair, logs = call(
-        join_kernel, [((NH, 32, 512), BF16), ((1, ROWS), F32)], stats, q_keep, *[swap(piece, "zp") for piece in q_give]
-    )
+    q_swapped = [swap(piece, "zp") for piece in q_give]
+    keep, give, at_target, logs = call(
+        column_grad_kernel,
+        [((2, 256, 512), F32), ((2, 256, 512), F32), ((32, 128), F32), ((1, ROWS), F32)],
+        *q_swapped, stats, scores, asked, every, hbm=2,
+    )
+    (q_pair,) = call(join_kernel, [((NH, 32, 512), BF16)], stats, logs, q_keep, *q_swapped)
     q_came = exchange(q_pair, "zh")
-    keep, give, at_target = call(
-        column_grad_kernel, [((2, 256, 512), BF16), ((2, 256, 512), BF16), ((32, 128), F32)],
-        logs, scores, asked, every,
-    )
     own, cross = call(pair_kernel, [((256, 512), F32), ((256, 512), BF16)], keep, swap(give, "c"))
     cross = swap(cross, "yh")
     passage_out, negative_out = call(column_kernel, [((32, 512), BF16), ((224, 512), BF16)], own, cross)

time: 120 us -> 128 us (1.067)
  waiting for transfers between devices: 27.3 us -> 34.7 us
    all_to_all x3, waiting for transfers between devices: 12.5 us -> 27.8 us  [exchange(): return lax.all_to_all(x, axes, split_axis=0, concat_axis=0, tiled=True)]
    ppermute x8, waiting for transfers between devices: 14.9 us -> 6.98 us  [swap(): return lax.ppermute(x, axis, [(0, 1), (1, 0)])]
  transfers between devices with their start and end apart: 11 -> 11, of which waited for: 6 -> 5; matrix products, arithmetic and copies ran while one was open for 0% -> 0% of each run, Pallas kernels for 2% -> 2%
where the time goes in v5:
time: 128 us; the launch traced here: 127 us
  starting transfers between devices  61.7 us (48%)
  waiting for transfers between devices  34.7 us (27%)
  blocking collectives  21.4 us (17%)
  Pallas kernels  8.55 us (7%)
    ppermute x8, starting transfers between devices, swap(): return lax.ppermute(x, axis, [(0, 1), (1, 0)])  33.5 us
    all_to_all x3, starting transfers between devices, exchange(): return lax.all_to_all(x, axes, split_axis=0, concat_axis=0, tiled=True)  28.3 us
    all_to_all x3, waiting for transfers between devices, exchange(): return lax.all_to_all(x, axes, split_axis=0, concat_axis=0, tiled=True)  27.8 us
    all_to_all x2, blocking collectives, exchange(): return lax.all_to_all(x, axes, split_axis=0, concat_axis=0, tiled=True)  21.4 us
    pallas_call x11, Pallas kernels, call(): pl.pallas_call(kernel, out_shape=[jax.ShapeDtypeStruct(shape, dtype) for...  8.55 us
    ppermute x8, waiting for transfers between devices, swap(): return lax.ppermute(x, axis, [(0, 1), (1, 0)])  6.98 us
  transfers between devices with their start and end apart: 11, of which 5 were waited for; matrix products, arithmetic and copies ran while one was open for 0% of the time, Pallas kernels for 2%

profile of v5, /device:TPU:1, one launch (start us, length us, event | category | flops | bytes accessed | tf_op | source)
XLA Modules:
  0.0 127.2 jit_solution(18436352368289357723)
XLA Ops:
  0.6 1.6 %shard_map.76 = bf16[8,144,128]{2,1,0:T(8,128)(2,1)} custom-call(bf16[32,512]{1,0:T(8,128)(2,1)} %queries.1, s32[7,32]{1,0:T(8,128)} %bitcast.2, s32[7,32]{1,0:T(8,128)} %bitcast.3), custom_call_target="tpu_custom_call" | custom-call | tf_op jit(solution)/shard_map/pallas_call | solution.py:25
  2.2 0.0 copy-start
  2.2 0.0 copy-start.1
  2.3 15.8 %all-to-all-start = ((bf16[8,144,128]{2,1,0:T(8,128)(2,1)}), bf16[8,144,128]{2,1,0:T(8,128)(2,1)S(1)}, u32[]{:S(2)}, u32[]{:S(2)}) async-start(bf16[8,144,128]{2,1,0:T(8,128)(2,1)} %shard_map.76), calls=%async_computation | async-start | bytes 589824 | tf_op jit(solution)/shard_map/all_to_all | solution.py:239
  18.1 0.4 shard_map.77.col0
  18.4 4.8 %collective-permute-start.2 = (bf16[256,512]{1,0:T(8,128)(2,1)S(1)}, bf16[256,512]{1,0:T(8,128)(2,1)S(1)}, u32[]{:S(2)}, u32[]{:S(2)}) collective-permute-start(bf16[256,512]{1,0:T(8,128)(2,1)S(1)} %shard_map.77.col0), channel_id=1, source_target_pairs={{0,256},{256,0},{1,257},{257,1},{2,258},{258,2},{3,259},{259,3},{4... | collective-permute-start | bytes 786440 | tf_op jit(solution)/shard_map/ppermute | solution.py:235
  23.2 12.4 %all-to-all-done.near = bf16[8,144,128]{2,1,0:T(8,128)(2,1)S(1)} async-done(((bf16[8,144,128]{2,1,0:T(8,128)(2,1)}), bf16[8,144,128]{2,1,0:T(8,128)(2,1)S(1)}, u32[]{:S(2)}, u32[]{:S(2)}) %all-to-all-start) | async-done | bytes 294944 | tf_op jit(solution)/shard_map/all_to_all | solution.py:239
  35.7 2.4 %collective-permute-start = (bf16[8,144,128]{2,1,0:T(8,128)(2,1)S(1)}, bf16[8,144,128]{2,1,0:T(8,128)(2,1)S(1)}, u32[]{:S(2)}, u32[]{:S(2)}) collective-permute-start(bf16[8,144,128]{2,1,0:T(8,128)(2,1)S(1)} %all-to-all-done.near), channel_id=1, source_target_pairs={{0,16},{16,0},{1,17},{17,1},{2,18},{18,2},{3,19},{19,3},{4,20},{20... | collective-permute-start | bytes 884744 | tf_op jit(solution)/shard_map/ppermute | solution.py:235
  38.1 7.5 %collective-permute-start.1 = (bf16[256,512]{1,0:T(8,128)(2,1)S(1)}, bf16[256,512]{1,0:T(8,128)(2,1)S(1)}, u32[]{:S(2)}, u32[]{:S(2)}) collective-permute-start(bf16[256,512]{1,0:T(8,128)(2,1)S(1)} %shard_map.77.col0), channel_id=1, source_target_pairs={{0,8},{8,0},{1,9},{9,1},{2,10},{10,2},{3,11},{11,3},{4,12},{12,4},... | collective-permute-start | bytes 786440 | tf_op jit(solution)/shard_map/ppermute | solution.py:235
  45.6 1.9 %collective-permute-start.3 = (bf16[256,512]{1,0:T(8,128)(2,1)S(1)}, bf16[256,512]{1,0:T(8,128)(2,1)S(1)}, u32[]{:S(2)}, u32[]{:S(2)}) collective-permute-start(bf16[256,512]{1,0:T(8,128)(2,1)S(1)} %collective-permute-done.2.col2), channel_id=1, source_target_pairs={{0,8},{8,0},{1,9},{9,1},{2,10},{10,2},{3,11},{11,3},{4,12},{12,4},... | collective-permute-start | bytes 786440 | tf_op jit(solution)/shard_map/ppermute | solution.py:235
  47.5 0.0 collective-permute-done.1.col1
  47.5 1.5 %collective-permute-done.3.col3 = bf16[256,512]{1,0:T(8,128)(2,1)S(1)} collective-permute-done((bf16[256,512]{1,0:T(8,128)(2,1)S(1)}, bf16[256,512]{1,0:T(8,128)(2,1)S(1)}, u32[]{:S(2)}, u32[]{:S(2)}) %collective-permute-start.3) | collective-permute-done | bytes 262176 | tf_op jit(solution)/shard_map/ppermute | solution.py:235
  49.0 0.8 shard_map.78
  49.8 12.4 %all_to_all.25.came = f32[8,72,128]{2,1,0:T(8,128)S(1)} all-to-all(f32[8,72,128]{2,1,0:T(8,128)S(1)} %get-tuple-element.19), channel_id=1, replica_groups=mesh['yh'=2,'zh'=8,'zp'=2,'c'=2,'yl'=2,'x'=4] {'yl','x'}, dimensions={0} | all-to-all | bytes 589824 | tf_op jit(solution)/shard_map/all_to_all | solution.py:239
  62.3 9.0 %all_to_all.26.scores.refs_3_ = f32[8,72,128]{2,1,0:T(8,128)S(1)} all-to-all(f32[8,72,128]{2,1,0:T(8,128)S(1)} %shard_map.79), channel_id=1, replica_groups=mesh['yh'=2,'zh'=8,'zp'=2,'c'=2,'yl'=2,'x'=4] {'yl','x'}, dimensions={0} | all-to-all | bytes 589824 | tf_op jit(solution)/shard_map/all_to_all | solution.py:239
  71.2 0.7 shard_map.80
  71.9 3.7 %all-to-all-start.3 = ((f32[16,8,128]{2,1,0:T(8,128)}), f32[16,8,128]{2,1,0:T(8,128)S(1)}, u32[]{:S(2)}, u32[]{:S(2)}) async-start(f32[16,8,128]{2,1,0:T(8,128)} %get-tuple-element.20), calls=%async_computation.3 | async-start | bytes 131072 | tf_op jit(solution)/shard_map/all_to_all | solution.py:239
  75.7 0.8 shard_map.81
  76.4 3.3 %collective-permute-start.4 = (bf16[128,512]{1,0:T(8,128)(2,1)S(1)}, bf16[128,512]{1,0:T(8,128)(2,1)S(1)}, u32[]{:S(2)}, u32[]{:S(2)}) collective-permute-start(bf16[128,512]{1,0:T(8,128)(2,1)S(1)} %get-tuple-element.23), channel_id=1, source_target_pairs={{0,16},{16,0},{1,17},{17,1},{2,18},{18,2},{3,19},{19,3},{4,20},{20... | collective-permute-start | bytes 393224 | tf_op jit(solution)/shard_map/ppermute | solution.py:235
  79.7 2.0 %collective-permute-start.5 = (bf16[128,512]{1,0:T(8,128)(2,1)S(1)}, bf16[128,512]{1,0:T(8,128)(2,1)S(1)}, u32[]{:S(2)}, u32[]{:S(2)}) collective-permute-start(bf16[128,512]{1,0:T(8,128)(2,1)S(1)} %get-tuple-element.24), channel_id=1, source_target_pairs={{0,16},{16,0},{1,17},{17,1},{2,18},{18,2},{3,19},{19,3},{4,20},{20... | collective-permute-start | bytes 393224 | tf_op jit(solution)/shard_map/ppermute | solution.py:235
  81.7 0.5 collective-permute-done.4.refs_0_
  82.3 4.9 %collective-permute-done.5.refs_1_ = bf16[128,512]{1,0:T(8,128)(2,1)S(1)} collective-permute-done((bf16[128,512]{1,0:T(8,128)(2,1)S(1)}, bf16[128,512]{1,0:T(8,128)(2,1)S(1)}, u32[]{:S(2)}, u32[]{:S(2)}) %collective-permute-start.5) | collective-permute-done | bytes 131104 | tf_op jit(solution)/shard_map/ppermute | solution.py:235
  87.2 0.0 all-to-all-done.3.refs_2_.stats
  87.2 1.8 %shard_map.82 = (f32[2,256,512]{2,1,0:T(8,128)S(1)}, f32[2,256,512]{2,1,0:T(8,128)}, f32[32,128]{1,0:T(8,128)S(1)}, f32[1,512]{1,0:T(1,128)S(1)}) custom-call(bf16[128,512]{1,0:T(8,128)(2,1)S(1)} %collective-permute-done.4.refs_0_, bf16[128,512]{1,0:T(8,128)(2,1)S(1)} %collective-permute-done.5.refs_1_, f32[16,8,128]{2,1,0:T(8,128)S(1)} %all-to-all-done.3.refs_2_.stats, ...), custom_call_target="tpu_custom_call" | custom-call | tf_op jit(solution)/shard_map/pallas_call | solution.py:25
  89.0 7.0 %collective-permute-start.6 = (f32[2,256,512]{2,1,0:T(8,128)}, f32[2,256,512]{2,1,0:T(8,128)S(1)}, u32[]{:S(2)}, u32[]{:S(2)}) collective-permute-start(f32[2,256,512]{2,1,0:T(8,128)} %get-tuple-element.30), channel_id=1, source_target_pairs={{0,8},{8,0},{1,9},{9,1},{2,10},{10,2},{3,11},{11,3},{4,12},{12,4},... | collective-permute-start | bytes 3145736 | tf_op jit(solution)/shard_map/ppermute | solution.py:235
  96.1 1.0 shard_map.83
  97.1 8.7 %all-to-all-start.4 = ((bf16[8,32,512]{2,1,0:T(8,128)(2,1)}), bf16[8,32,512]{2,1,0:T(8,128)(2,1)S(1)}, u32[]{:S(2)}, u32[]{:S(2)}) async-start(bf16[8,32,512]{2,1,0:T(8,128)(2,1)} %shard_map.83), calls=%async_computation.4 | async-start | bytes 524288 | tf_op jit(solution)/shard_map/all_to_all | solution.py:239
  105.8 0.1 shard_map.85
  105.9 4.5 %collective-permute-start.7 = (bf16[256,512]{1,0:T(8,128)(2,1)S(1)}, bf16[256,512]{1,0:T(8,128)(2,1)S(1)}, u32[]{:S(2)}, u32[]{:S(2)}) collective-permute-start(bf16[256,512]{1,0:T(8,128)(2,1)S(1)} %get-tuple-element.32), channel_id=1, source_target_pairs={{0,256},{256,0},{1,257},{257,1},{2,258},{258,2},{3,259},{259,3},{4... | collective-permute-start | bytes 786440 | tf_op jit(solution)/shard_map/ppermute | solution.py:235
  110.4 15.3 %all-to-all-done.4.came = bf16[8,32,512]{2,1,0:T(8,128)(2,1)S(1)} async-done(((bf16[8,32,512]{2,1,0:T(8,128)(2,1)}), bf16[8,32,512]{2,1,0:T(8,128)(2,1)S(1)}, u32[]{:S(2)}, u32[]{:S(2)}) %all-to-all-start.4) | async-done | bytes 262176 | tf_op jit(solution)/shard_map/all_to_all | solution.py:239
  125.7 0.7 shard_map.84
  126.4 0.7 shard_map.86
  (7 shorter events, 0.0 us)
Async XLA Ops:
  2.2 15.8 %copy-start = (bf16[224,512]{1,0:T(8,128)(2,1)S(1)}, bf16[224,512]{1,0:T(8,128)(2,1)}, u32[]{:S(2)}) copy-start(bf16[224,512]{1,0:T(8,128)(2,1)} %negatives.1) | copy-start | bytes 688132
  2.2 15.8 %copy-start.1 = (bf16[32,512]{1,0:T(8,128)(2,1)S(1)}, bf16[32,512]{1,0:T(8,128)(2,1)}, u32[]{:S(2)}) copy-start(bf16[32,512]{1,0:T(8,128)(2,1)} %passages.3) | copy-start | bytes 98308
  2.3 33.4 %all-to-all-start = ((bf16[8,144,128]{2,1,0:T(8,128)(2,1)}), bf16[8,144,128]{2,1,0:T(8,128)(2,1)S(1)}, u32[]{:S(2)}, u32[]{:S(2)}) async-start(bf16[8,144,128]{2,1,0:T(8,128)(2,1)} %shard_map.76), calls=%async_computation | async-start | bytes 589824 | tf_op jit(solution)/shard_map/all_to_all | solution.py:239
  18.4 27.1 %collective-permute-start.2 = (bf16[256,512]{1,0:T(8,128)(2,1)S(1)}, bf16[256,512]{1,0:T(8,128)(2,1)S(1)}, u32[]{:S(2)}, u32[]{:S(2)}) collective-permute-start(bf16[256,512]{1,0:T(8,128)(2,1)S(1)} %shard_map.77.col0), channel_id=1, source_target_pairs={{0,256},{256,0},{1,257},{257,1},{2,258},{258,2},{3,259},{259,3},{4... | collective-permute-start | bytes 786440 | tf_op jit(solution)/shard_map/ppermute | solution.py:235
  35.7 13.3 %collective-permute-start = (bf16[8,144,128]{2,1,0:T(8,128)(2,1)S(1)}, bf16[8,144,128]{2,1,0:T(8,128)(2,1)S(1)}, u32[]{:S(2)}, u32[]{:S(2)}) collective-permute-start(bf16[8,144,128]{2,1,0:T(8,128)(2,1)S(1)} %all-to-all-done.near), channel_id=1, source_target_pairs={{0,16},{16,0},{1,17},{17,1},{2,18},{18,2},{3,19},{19,3},{4,20},{20... | collective-permute-start | bytes 884744 | tf_op jit(solution)/shard_map/ppermute | solution.py:235
  38.1 9.4 %collective-permute-start.1 = (bf16[256,512]{1,0:T(8,128)(2,1)S(1)}, bf16[256,512]{1,0:T(8,128)(2,1)S(1)}, u32[]{:S(2)}, u32[]{:S(2)}) collective-permute-start(bf16[256,512]{1,0:T(8,128)(2,1)S(1)} %shard_map.77.col0), channel_id=1, source_target_pairs={{0,8},{8,0},{1,9},{9,1},{2,10},{10,2},{3,11},{11,3},{4,12},{12,4},... | collective-permute-start | bytes 786440 | tf_op jit(solution)/shard_map/ppermute | solution.py:235
  45.6 3.4 %collective-permute-start.3 = (bf16[256,512]{1,0:T(8,128)(2,1)S(1)}, bf16[256,512]{1,0:T(8,128)(2,1)S(1)}, u32[]{:S(2)}, u32[]{:S(2)}) collective-permute-start(bf16[256,512]{1,0:T(8,128)(2,1)S(1)} %collective-permute-done.2.col2), channel_id=1, source_target_pairs={{0,8},{8,0},{1,9},{9,1},{2,10},{10,2},{3,11},{11,3},{4,12},{12,4},... | collective-permute-start | bytes 786440 | tf_op jit(solution)/shard_map/ppermute | solution.py:235
  71.9 15.3 %all-to-all-start.3 = ((f32[16,8,128]{2,1,0:T(8,128)}), f32[16,8,128]{2,1,0:T(8,128)S(1)}, u32[]{:S(2)}, u32[]{:S(2)}) async-start(f32[16,8,128]{2,1,0:T(8,128)} %get-tuple-element.20), calls=%async_computation.3 | async-start | bytes 131072 | tf_op jit(solution)/shard_map/all_to_all | solution.py:239
  76.4 5.8 %collective-permute-start.4 = (bf16[128,512]{1,0:T(8,128)(2,1)S(1)}, bf16[128,512]{1,0:T(8,128)(2,1)S(1)}, u32[]{:S(2)}, u32[]{:S(2)}) collective-permute-start(bf16[128,512]{1,0:T(8,128)(2,1)S(1)} %get-tuple-element.23), channel_id=1, source_target_pairs={{0,16},{16,0},{1,17},{17,1},{2,18},{18,2},{3,19},{19,3},{4,20},{20... | collective-permute-start | bytes 393224 | tf_op jit(solution)/shard_map/ppermute | solution.py:235
  79.7 7.5 %collective-permute-start.5 = (bf16[128,512]{1,0:T(8,128)(2,1)S(1)}, bf16[128,512]{1,0:T(8,128)(2,1)S(1)}, u32[]{:S(2)}, u32[]{:S(2)}) collective-permute-start(bf16[128,512]{1,0:T(8,128)(2,1)S(1)} %get-tuple-element.24), channel_id=1, source_target_pairs={{0,16},{16,0},{1,17},{17,1},{2,18},{18,2},{3,19},{19,3},{4,20},{20... | collective-permute-start | bytes 393224 | tf_op jit(solution)/shard_map/ppermute | solution.py:235
  89.0 16.8 %collective-permute-start.6 = (f32[2,256,512]{2,1,0:T(8,128)}, f32[2,256,512]{2,1,0:T(8,128)S(1)}, u32[]{:S(2)}, u32[]{:S(2)}) collective-permute-start(f32[2,256,512]{2,1,0:T(8,128)} %get-tuple-element.30), channel_id=1, source_target_pairs={{0,8},{8,0},{1,9},{9,1},{2,10},{10,2},{3,11},{11,3},{4,12},{12,4},... | collective-permute-start | bytes 3145736 | tf_op jit(solution)/shard_map/ppermute | solution.py:235
  97.1 28.7 %all-to-all-start.4 = ((bf16[8,32,512]{2,1,0:T(8,128)(2,1)}), bf16[8,32,512]{2,1,0:T(8,128)(2,1)S(1)}, u32[]{:S(2)}, u32[]{:S(2)}) async-start(bf16[8,32,512]{2,1,0:T(8,128)(2,1)} %shard_map.83), calls=%async_computation.4 | async-start | bytes 524288 | tf_op jit(solution)/shard_map/all_to_all | solution.py:239
  105.9 20.5 %collective-permute-start.7 = (bf16[256,512]{1,0:T(8,128)(2,1)S(1)}, bf16[256,512]{1,0:T(8,128)(2,1)S(1)}, u32[]{:S(2)}, u32[]{:S(2)}) collective-permute-start(bf16[256,512]{1,0:T(8,128)(2,1)S(1)} %get-tuple-element.32), channel_id=1, source_target_pairs={{0,256},{256,0},{1,257},{257,1},{2,258},{258,2},{3,259},{259,3},{4... | collective-permute-start | bytes 786440 | tf_op jit(solution)/shard_map/ppermute | solution.py:235

commit v6 on v4

--- a/solution.py
+++ b/solution.py
@@ -199,7 +199,7 @@
         sent[l * 4 : (l + 1) * 4] = total.astype(BF16).reshape(4, 32, 512)
 
 
-def column_grad_kernel(logs, scores, asked, queries, keep, give, at_target):
+def column_grad_kernel(logs, scores, asked, queries, own, core, other, cross, at_target):
     log_total = logs[...]
     every = queries[...]
     for o in range(NB):
@@ -208,20 +208,17 @@
         if o == 0:
             target = is_target()
             weights = jnp.where(target, weights - 1.0, weights)
-            own = jnp.sum(jnp.where(target, weights, 0.0), axis=1, keepdims=True)
-            at_target[...] = jnp.broadcast_to(own.astype(BF16).astype(F32), (32, 128))
+            mine = jnp.sum(jnp.where(target, weights, 0.0), axis=1, keepdims=True)
+            at_target[...] = jnp.broadcast_to(mine.astype(BF16).astype(F32), (32, 128))
         both = block_weights(weights, jnp.exp(hard - log_total), asked[o : o + 1, :])
-        (give if o % 2 else keep)[o // 2] = jnp.dot(both, every, preferred_element_type=F32).astype(BF16)
-
-
-def pair_kernel(keep, came, own, sent):
-    own[...] = keep[0].astype(F32) + came[0].astype(F32)
-    sent[...] = (keep[1].astype(F32) + came[1].astype(F32)).astype(BF16)
-
-
-def column_kernel(own, came, passage_out, negative_out):
-    passage_out[...] = (own[0:32, :] + came[0:32, :].astype(F32)).astype(BF16)
-    negative_out[...] = (own[32:256, :] + came[32:256, :].astype(F32)).astype(BF16)
+        out = (own, core, other, cross)[o]
+        out[...] = jnp.dot(both, every, preferred_element_type=F32).astype(out.dtype)
+
+
+def column_kernel(own, cross, other, core, passage_out, negative_out):
+    for out, rows in ((passage_out, slice(0, 32)), (negative_out, slice(32, 256))):
+        total = own[rows, :] + core[rows, :].astype(F32)
+        out[...] = (total + other[rows, :].astype(F32) + cross[rows, :].astype(F32)).astype(BF16)
 
 
 def query_kernel(came, at_target, passages, query_out):
@@ -273,13 +270,14 @@
         join_kernel, [((NH, 32, 512), BF16), ((1, ROWS), F32)], stats, q_keep, *[swap(piece, "zp") for piece in q_give]
     )
     q_came = exchange(q_pair, "zh")
-    keep, give, at_target = call(
-        column_grad_kernel, [((2, 256, 512), BF16), ((2, 256, 512), BF16), ((32, 128), F32)],
+    own, core, other, cross, at_target = call(
+        column_grad_kernel, [((256, 512), F32)] + [((256, 512), BF16)] * 3 + [((32, 128), F32)],
         logs, scores, asked, every,
     )
-    own, cross = call(pair_kernel, [((256, 512), F32), ((256, 512), BF16)], keep, swap(give, "c"))
-    cross = swap(cross, "yh")
-    passage_out, negative_out = call(column_kernel, [((32, 512), BF16), ((224, 512), BF16)], own, cross)
+    passage_out, negative_out = call(
+        column_kernel, [((32, 512), BF16), ((224, 512), BF16)],
+        own, lax.ppermute(cross, ("yh", "c"), [(0, 3), (1, 2), (2, 1), (3, 0)]), swap(other, "yh"), swap(core, "c"),
+    )
     (query_out,) = call(query_kernel, [((32, 512), BF16)], q_came, at_target, passages)
     return (query_out, passage_out, negative_out)
 

time: 120 us -> 123 us (1.025)
  starting transfers between devices: 62 us -> 64.2 us
    ppermute x0 -> x1, starting transfers between devices: none -> 9.5 us  [shards(): lax.ppermute(cross, ('yh', 'c'), [(0, 3), (1, 2), (2, 1), (3, 0)])]
    ppermute x8, starting transfers between devices: 33.4 us -> 26.1 us  [swap(): return lax.ppermute(x, axis, [(0, 1), (1, 0)])]
    ppermute x0 -> x1, waiting for transfers between devices: none -> 2.86 us  [shards(): lax.ppermute(cross, ('yh', 'c'), [(0, 3), (1, 2), (2, 1), (3, 0)])]
    ppermute x8, waiting for transfers between devices: 14.9 us -> 12.6 us  [swap(): return lax.ppermute(x, axis, [(0, 1), (1, 0)])]
    pallas_call x11 -> x10, Pallas kernels: 7.57 us -> 7.52 us  [call(): pl.pallas_call(kernel, out_shape=[jax.ShapeDtypeStruct(shape, dtype) for...]
  transfers between devices with their start and end apart: 11 -> 12, of which waited for: 6 -> 6; matrix products, arithmetic and copies ran while one was open for 0% -> 0% of each run, Pallas kernels for 2% -> 2%
where the time goes in v6:
time: 123 us; the launch traced here: 122 us
  starting transfers between devices  64.2 us (52%)
  waiting for transfers between devices  27.9 us (23%)
  blocking collectives  21.4 us (17%)
  Pallas kernels  7.52 us (6%)
    all_to_all x3, starting transfers between devices, exchange(): return lax.all_to_all(x, axes, split_axis=0, concat_axis=0, tiled=True)  28.6 us
    ppermute x8, starting transfers between devices, swap(): return lax.ppermute(x, axis, [(0, 1), (1, 0)])  26.1 us
    all_to_all x2, blocking collectives, exchange(): return lax.all_to_all(x, axes, split_axis=0, concat_axis=0, tiled=True)  21.4 us
    ppermute x8, waiting for transfers between devices, swap(): return lax.ppermute(x, axis, [(0, 1), (1, 0)])  12.6 us
    all_to_all x3, waiting for transfers between devices, exchange(): return lax.all_to_all(x, axes, split_axis=0, concat_axis=0, tiled=True)  12.5 us
    ppermute x1, starting transfers between devices, shards(): lax.ppermute(cross, ('yh', 'c'), [(0, 3), (1, 2), (2, 1), (3, 0)])  9.5 us
    pallas_call x10, Pallas kernels, call(): pl.pallas_call(kernel, out_shape=[jax.ShapeDtypeStruct(shape, dtype) for...  7.52 us
    ppermute x1, waiting for transfers between devices, shards(): lax.ppermute(cross, ('yh', 'c'), [(0, 3), (1, 2), (2, 1), (3, 0)])  2.86 us
  transfers between devices with their start and end apart: 12, of which 6 were waited for; matrix products, arithmetic and copies ran while one was open for 0% of the time, Pallas kernels for 2%

profile of v6, /device:TPU:1, one launch (start us, length us, event | category | flops | bytes accessed | tf_op | source)
XLA Modules:
  0.0 121.8 jit_solution(17152201735100234167)
XLA Ops:
  0.6 1.6 %shard_map.76 = bf16[8,144,128]{2,1,0:T(8,128)(2,1)} custom-call(bf16[32,512]{1,0:T(8,128)(2,1)} %queries.1, s32[7,32]{1,0:T(8,128)} %bitcast.2, s32[7,32]{1,0:T(8,128)} %bitcast.3), custom_call_target="tpu_custom_call" | custom-call | tf_op jit(solution)/shard_map/pallas_call | solution.py:25
  2.2 0.0 copy-start
  2.2 0.0 copy-start.1
  2.3 15.8 %all-to-all-start = ((bf16[8,144,128]{2,1,0:T(8,128)(2,1)}), bf16[8,144,128]{2,1,0:T(8,128)(2,1)S(1)}, u32[]{:S(2)}, u32[]{:S(2)}) async-start(bf16[8,144,128]{2,1,0:T(8,128)(2,1)} %shard_map.76), calls=%async_computation | async-start | bytes 589824 | tf_op jit(solution)/shard_map/all_to_all | solution.py:236
  18.1 0.4 shard_map.77.col0
  18.4 4.8 %collective-permute-start.2 = (bf16[256,512]{1,0:T(8,128)(2,1)S(1)}, bf16[256,512]{1,0:T(8,128)(2,1)S(1)}, u32[]{:S(2)}, u32[]{:S(2)}) collective-permute-start(bf16[256,512]{1,0:T(8,128)(2,1)S(1)} %shard_map.77.col0), channel_id=1, source_target_pairs={{0,256},{256,0},{1,257},{257,1},{2,258},{258,2},{3,259},{259,3},{4... | collective-permute-start | bytes 786440 | tf_op jit(solution)/shard_map/ppermute | solution.py:232
  23.3 12.4 %all-to-all-done.near = bf16[8,144,128]{2,1,0:T(8,128)(2,1)S(1)} async-done(((bf16[8,144,128]{2,1,0:T(8,128)(2,1)}), bf16[8,144,128]{2,1,0:T(8,128)(2,1)S(1)}, u32[]{:S(2)}, u32[]{:S(2)}) %all-to-all-start) | async-done | bytes 294944 | tf_op jit(solution)/shard_map/all_to_all | solution.py:236
  35.7 2.4 %collective-permute-start = (bf16[8,144,128]{2,1,0:T(8,128)(2,1)S(1)}, bf16[8,144,128]{2,1,0:T(8,128)(2,1)S(1)}, u32[]{:S(2)}, u32[]{:S(2)}) collective-permute-start(bf16[8,144,128]{2,1,0:T(8,128)(2,1)S(1)} %all-to-all-done.near), channel_id=1, source_target_pairs={{0,16},{16,0},{1,17},{17,1},{2,18},{18,2},{3,19},{19,3},{4,20},{20... | collective-permute-start | bytes 884744 | tf_op jit(solution)/shard_map/ppermute | solution.py:232
  38.1 7.5 %collective-permute-start.1 = (bf16[256,512]{1,0:T(8,128)(2,1)S(1)}, bf16[256,512]{1,0:T(8,128)(2,1)S(1)}, u32[]{:S(2)}, u32[]{:S(2)}) collective-permute-start(bf16[256,512]{1,0:T(8,128)(2,1)S(1)} %shard_map.77.col0), channel_id=1, source_target_pairs={{0,8},{8,0},{1,9},{9,1},{2,10},{10,2},{3,11},{11,3},{4,12},{12,4},... | collective-permute-start | bytes 786440 | tf_op jit(solution)/shard_map/ppermute | solution.py:232
  45.6 1.9 %collective-permute-start.3 = (bf16[256,512]{1,0:T(8,128)(2,1)S(1)}, bf16[256,512]{1,0:T(8,128)(2,1)S(1)}, u32[]{:S(2)}, u32[]{:S(2)}) collective-permute-start(bf16[256,512]{1,0:T(8,128)(2,1)S(1)} %collective-permute-done.2.col2), channel_id=1, source_target_pairs={{0,8},{8,0},{1,9},{9,1},{2,10},{10,2},{3,11},{11,3},{4,12},{12,4},... | collective-permute-start | bytes 786440 | tf_op jit(solution)/shard_map/ppermute | solution.py:232
  47.5 1.5 %collective-permute-done.3.col3 = bf16[256,512]{1,0:T(8,128)(2,1)S(1)} collective-permute-done((bf16[256,512]{1,0:T(8,128)(2,1)S(1)}, bf16[256,512]{1,0:T(8,128)(2,1)S(1)}, u32[]{:S(2)}, u32[]{:S(2)}) %collective-permute-start.3) | collective-permute-done | bytes 262176 | tf_op jit(solution)/shard_map/ppermute | solution.py:232
  49.0 0.8 shard_map.78
  49.8 12.4 %all_to_all.25.came = f32[8,72,128]{2,1,0:T(8,128)S(1)} all-to-all(f32[8,72,128]{2,1,0:T(8,128)S(1)} %get-tuple-element.20), channel_id=1, replica_groups=mesh['yh'=2,'zh'=8,'zp'=2,'c'=2,'yl'=2,'x'=4] {'yl','x'}, dimensions={0} | all-to-all | bytes 589824 | tf_op jit(solution)/shard_map/all_to_all | solution.py:236
  62.3 9.0 %all_to_all.26.scores = f32[8,72,128]{2,1,0:T(8,128)S(1)} all-to-all(f32[8,72,128]{2,1,0:T(8,128)S(1)} %shard_map.79), channel_id=1, replica_groups=mesh['yh'=2,'zh'=8,'zp'=2,'c'=2,'yl'=2,'x'=4] {'yl','x'}, dimensions={0} | all-to-all | bytes 589824 | tf_op jit(solution)/shard_map/all_to_all | solution.py:236
  71.2 0.7 shard_map.80
  71.9 3.7 %all-to-all-start.3 = ((f32[16,8,128]{2,1,0:T(8,128)}), f32[16,8,128]{2,1,0:T(8,128)S(1)}, u32[]{:S(2)}, u32[]{:S(2)}) async-start(f32[16,8,128]{2,1,0:T(8,128)} %get-tuple-element.21), calls=%async_computation.3 | async-start | bytes 131072 | tf_op jit(solution)/shard_map/all_to_all | solution.py:236
  75.7 0.8 shard_map.81
  76.4 3.3 %collective-permute-start.4 = (bf16[128,512]{1,0:T(8,128)(2,1)S(1)}, bf16[128,512]{1,0:T(8,128)(2,1)S(1)}, u32[]{:S(2)}, u32[]{:S(2)}) collective-permute-start(bf16[128,512]{1,0:T(8,128)(2,1)S(1)} %get-tuple-element.25), channel_id=1, source_target_pairs={{0,16},{16,0},{1,17},{17,1},{2,18},{18,2},{3,19},{19,3},{4,20},{20... | collective-permute-start | bytes 393224 | tf_op jit(solution)/shard_map/ppermute | solution.py:232
  79.7 2.0 %collective-permute-start.5 = (bf16[128,512]{1,0:T(8,128)(2,1)S(1)}, bf16[128,512]{1,0:T(8,128)(2,1)S(1)}, u32[]{:S(2)}, u32[]{:S(2)}) collective-permute-start(bf16[128,512]{1,0:T(8,128)(2,1)S(1)} %get-tuple-element.26), channel_id=1, source_target_pairs={{0,16},{16,0},{1,17},{17,1},{2,18},{18,2},{3,19},{19,3},{4,20},{20... | collective-permute-start | bytes 393224 | tf_op jit(solution)/shard_map/ppermute | solution.py:232
  81.7 0.5 collective-permute-done.4.refs_0_
  82.3 4.9 %collective-permute-done.5.refs_1_ = bf16[128,512]{1,0:T(8,128)(2,1)S(1)} collective-permute-done((bf16[128,512]{1,0:T(8,128)(2,1)S(1)}, bf16[128,512]{1,0:T(8,128)(2,1)S(1)}, u32[]{:S(2)}, u32[]{:S(2)}) %collective-permute-start.5) | collective-permute-done | bytes 131104 | tf_op jit(solution)/shard_map/ppermute | solution.py:232
  87.2 0.0 all-to-all-done.3.stats
  87.3 1.0 shard_map.82
  88.3 9.1 %all-to-all-start.4 = ((bf16[8,32,512]{2,1,0:T(8,128)(2,1)}), bf16[8,32,512]{2,1,0:T(8,128)(2,1)S(1)}, u32[]{:S(2)}, u32[]{:S(2)}) async-start(bf16[8,32,512]{2,1,0:T(8,128)(2,1)} %get-tuple-element.27), calls=%async_computation.4 | async-start | bytes 524288 | tf_op jit(solution)/shard_map/all_to_all | solution.py:236
  97.4 0.7 shard_map.83
  98.1 9.5 %collective-permute-start.6 = (bf16[256,512]{1,0:T(8,128)(2,1)S(1)}, bf16[256,512]{1,0:T(8,128)(2,1)S(1)}, u32[]{:S(2)}, u32[]{:S(2)}) collective-permute-start(bf16[256,512]{1,0:T(8,128)(2,1)S(1)} %get-tuple-element.32), channel_id=1, source_target_pairs={{0,264},{8,256},{256,8},{264,0},{1,265},{9,257},{257,9},{265,1},{2... | collective-permute-start | bytes 786440 | tf_op jit(solution)/shard_map/ppermute | solution.py:279
  107.6 2.3 %collective-permute-start.7 = (bf16[256,512]{1,0:T(8,128)(2,1)S(1)}, bf16[256,512]{1,0:T(8,128)(2,1)S(1)}, u32[]{:S(2)}, u32[]{:S(2)}) collective-permute-start(bf16[256,512]{1,0:T(8,128)(2,1)S(1)} %get-tuple-element.33), channel_id=1, source_target_pairs={{0,256},{256,0},{1,257},{257,1},{2,258},{258,2},{3,259},{259,3},{4... | collective-permute-start | bytes 786440 | tf_op jit(solution)/shard_map/ppermute | solution.py:232
  109.9 2.0 %collective-permute-start.8 = (bf16[256,512]{1,0:T(8,128)(2,1)S(1)}, bf16[256,512]{1,0:T(8,128)(2,1)S(1)}, u32[]{:S(2)}, u32[]{:S(2)}) collective-permute-start(bf16[256,512]{1,0:T(8,128)(2,1)S(1)} %get-tuple-element.34), channel_id=1, source_target_pairs={{0,8},{8,0},{1,9},{9,1},{2,10},{10,2},{3,11},{11,3},{4,12},{12,4},... | collective-permute-start | bytes 786440 | tf_op jit(solution)/shard_map/ppermute | solution.py:232
  111.8 2.9 %collective-permute-done.6.cross = bf16[256,512]{1,0:T(8,128)(2,1)S(1)} collective-permute-done((bf16[256,512]{1,0:T(8,128)(2,1)S(1)}, bf16[256,512]{1,0:T(8,128)(2,1)S(1)}, u32[]{:S(2)}, u32[]{:S(2)}) %collective-permute-start.6) | collective-permute-done | bytes 262176 | tf_op jit(solution)/shard_map/ppermute | solution.py:279
  114.7 5.6 %collective-permute-done.7.other = bf16[256,512]{1,0:T(8,128)(2,1)S(1)} collective-permute-done((bf16[256,512]{1,0:T(8,128)(2,1)S(1)}, bf16[256,512]{1,0:T(8,128)(2,1)S(1)}, u32[]{:S(2)}, u32[]{:S(2)}) %collective-permute-start.7) | collective-permute-done | bytes 262176 | tf_op jit(solution)/shard_map/ppermute | solution.py:232
  120.3 0.8 shard_map.85
  121.1 0.7 shard_map.84
  (8 shorter events, 0.0 us)
Async XLA Ops:
  2.2 15.8 %copy-start = (bf16[224,512]{1,0:T(8,128)(2,1)S(1)}, bf16[224,512]{1,0:T(8,128)(2,1)}, u32[]{:S(2)}) copy-start(bf16[224,512]{1,0:T(8,128)(2,1)} %negatives.1) | copy-start | bytes 688132
  2.2 15.8 %copy-start.1 = (bf16[32,512]{1,0:T(8,128)(2,1)S(1)}, bf16[32,512]{1,0:T(8,128)(2,1)}, u32[]{:S(2)}) copy-start(bf16[32,512]{1,0:T(8,128)(2,1)} %passages.3) | copy-start | bytes 98308
  2.3 33.4 %all-to-all-start = ((bf16[8,144,128]{2,1,0:T(8,128)(2,1)}), bf16[8,144,128]{2,1,0:T(8,128)(2,1)S(1)}, u32[]{:S(2)}, u32[]{:S(2)}) async-start(bf16[8,144,128]{2,1,0:T(8,128)(2,1)} %shard_map.76), calls=%async_computation | async-start | bytes 589824 | tf_op jit(solution)/shard_map/all_to_all | solution.py:236
  18.4 27.1 %collective-permute-start.2 = (bf16[256,512]{1,0:T(8,128)(2,1)S(1)}, bf16[256,512]{1,0:T(8,128)(2,1)S(1)}, u32[]{:S(2)}, u32[]{:S(2)}) collective-permute-start(bf16[256,512]{1,0:T(8,128)(2,1)S(1)} %shard_map.77.col0), channel_id=1, source_target_pairs={{0,256},{256,0},{1,257},{257,1},{2,258},{258,2},{3,259},{259,3},{4... | collective-permute-start | bytes 786440 | tf_op jit(solution)/shard_map/ppermute | solution.py:232
  35.7 13.3 %collective-permute-start = (bf16[8,144,128]{2,1,0:T(8,128)(2,1)S(1)}, bf16[8,144,128]{2,1,0:T(8,128)(2,1)S(1)}, u32[]{:S(2)}, u32[]{:S(2)}) collective-permute-start(bf16[8,144,128]{2,1,0:T(8,128)(2,1)S(1)} %all-to-all-done.near), channel_id=1, source_target_pairs={{0,16},{16,0},{1,17},{17,1},{2,18},{18,2},{3,19},{19,3},{4,20},{20... | collective-permute-start | bytes 884744 | tf_op jit(solution)/shard_map/ppermute | solution.py:232
  38.1 9.4 %collective-permute-start.1 = (bf16[256,512]{1,0:T(8,128)(2,1)S(1)}, bf16[256,512]{1,0:T(8,128)(2,1)S(1)}, u32[]{:S(2)}, u32[]{:S(2)}) collective-permute-start(bf16[256,512]{1,0:T(8,128)(2,1)S(1)} %shard_map.77.col0), channel_id=1, source_target_pairs={{0,8},{8,0},{1,9},{9,1},{2,10},{10,2},{3,11},{11,3},{4,12},{12,4},... | collective-permute-start | bytes 786440 | tf_op jit(solution)/shard_map/ppermute | solution.py:232
  45.6 3.4 %collective-permute-start.3 = (bf16[256,512]{1,0:T(8,128)(2,1)S(1)}, bf16[256,512]{1,0:T(8,128)(2,1)S(1)}, u32[]{:S(2)}, u32[]{:S(2)}) collective-permute-start(bf16[256,512]{1,0:T(8,128)(2,1)S(1)} %collective-permute-done.2.col2), channel_id=1, source_target_pairs={{0,8},{8,0},{1,9},{9,1},{2,10},{10,2},{3,11},{11,3},{4,12},{12,4},... | collective-permute-start | bytes 786440 | tf_op jit(solution)/shard_map/ppermute | solution.py:232
  71.9 15.3 %all-to-all-start.3 = ((f32[16,8,128]{2,1,0:T(8,128)}), f32[16,8,128]{2,1,0:T(8,128)S(1)}, u32[]{:S(2)}, u32[]{:S(2)}) async-start(f32[16,8,128]{2,1,0:T(8,128)} %get-tuple-element.21), calls=%async_computation.3 | async-start | bytes 131072 | tf_op jit(solution)/shard_map/all_to_all | solution.py:236
  76.4 5.8 %collective-permute-start.4 = (bf16[128,512]{1,0:T(8,128)(2,1)S(1)}, bf16[128,512]{1,0:T(8,128)(2,1)S(1)}, u32[]{:S(2)}, u32[]{:S(2)}) collective-permute-start(bf16[128,512]{1,0:T(8,128)(2,1)S(1)} %get-tuple-element.25), channel_id=1, source_target_pairs={{0,16},{16,0},{1,17},{17,1},{2,18},{18,2},{3,19},{19,3},{4,20},{20... | collective-permute-start | bytes 393224 | tf_op jit(solution)/shard_map/ppermute | solution.py:232
  79.7 7.5 %collective-permute-start.5 = (bf16[128,512]{1,0:T(8,128)(2,1)S(1)}, bf16[128,512]{1,0:T(8,128)(2,1)S(1)}, u32[]{:S(2)}, u32[]{:S(2)}) collective-permute-start(bf16[128,512]{1,0:T(8,128)(2,1)S(1)} %get-tuple-element.26), channel_id=1, source_target_pairs={{0,16},{16,0},{1,17},{17,1},{2,18},{18,2},{3,19},{19,3},{4,20},{20... | collective-permute-start | bytes 393224 | tf_op jit(solution)/shard_map/ppermute | solution.py:232
  88.3 32.8 %all-to-all-start.4 = ((bf16[8,32,512]{2,1,0:T(8,128)(2,1)}), bf16[8,32,512]{2,1,0:T(8,128)(2,1)S(1)}, u32[]{:S(2)}, u32[]{:S(2)}) async-start(bf16[8,32,512]{2,1,0:T(8,128)(2,1)} %get-tuple-element.27), calls=%async_computation.4 | async-start | bytes 524288 | tf_op jit(solution)/shard_map/all_to_all | solution.py:236
  98.1 16.6 %collective-permute-start.6 = (bf16[256,512]{1,0:T(8,128)(2,1)S(1)}, bf16[256,512]{1,0:T(8,128)(2,1)S(1)}, u32[]{:S(2)}, u32[]{:S(2)}) collective-permute-start(bf16[256,512]{1,0:T(8,128)(2,1)S(1)} %get-tuple-element.32), channel_id=1, source_target_pairs={{0,264},{8,256},{256,8},{264,0},{1,265},{9,257},{257,9},{265,1},{2... | collective-permute-start | bytes 786440 | tf_op jit(solution)/shard_map/ppermute | solution.py:279
  107.6 12.7 %collective-permute-start.7 = (bf16[256,512]{1,0:T(8,128)(2,1)S(1)}, bf16[256,512]{1,0:T(8,128)(2,1)S(1)}, u32[]{:S(2)}, u32[]{:S(2)}) collective-permute-start(bf16[256,512]{1,0:T(8,128)(2,1)S(1)} %get-tuple-element.33), channel_id=1, source_target_pairs={{0,256},{256,0},{1,257},{257,1},{2,258},{258,2},{3,259},{259,3},{4... | collective-permute-start | bytes 786440 | tf_op jit(solution)/shard_map/ppermute | solution.py:232
  109.9 10.5 %collective-permute-start.8 = (bf16[256,512]{1,0:T(8,128)(2,1)S(1)}, bf16[256,512]{1,0:T(8,128)(2,1)S(1)}, u32[]{:S(2)}, u32[]{:S(2)}) collective-permute-start(bf16[256,512]{1,0:T(8,128)(2,1)S(1)} %get-tuple-element.34), channel_id=1, source_target_pairs={{0,8},{8,0},{1,9},{9,1},{2,10},{10,2},{3,11},{11,3},{4,12},{12,4},... | collective-permute-start | bytes 786440 | tf_op jit(solution)/shard_map/ppermute | solution.py:232

commit v7 on v4

--- a/solution.py
+++ b/solution.py
@@ -231,6 +231,17 @@
     query_out[...] = total.astype(BF16)
 
 
+def after(x, *others):
+    return pl.pallas_call(
+        lambda *refs: None,
+        out_shape=jax.ShapeDtypeStruct(x.shape, x.dtype),
+        in_specs=[pl.BlockSpec(memory_space=pltpu.VMEM)] * (1 + len(others)),
+        out_specs=pl.BlockSpec(memory_space=pltpu.VMEM),
+        input_output_aliases={0: 0},
+        compiler_params=pltpu.CompilerParams(vmem_limit_bytes=VMEM_LIMIT),
+    )(x, *others)
+
+
 def swap(x, axis):
     return lax.ppermute(x, axis, [(0, 1), (1, 0)])
 
@@ -249,7 +260,6 @@
         ],
     )
     near = exchange(sent, "zh")
-    far = swap(near, "zp")
     (col0,) = call(
         column_pack_kernel, [((256, 512), BF16)], passages, negatives, hbm=2,
         scratch=[pltpu.SemaphoreType.DMA((2,))],
@@ -257,6 +267,8 @@
     col2 = swap(col0, "yh")
     col1 = swap(col0, "c")
     col3 = swap(col2, "c")
+    near = after(near, col1, col3)
+    far = swap(near, "zp")
     parts, every, asked = call(
         score_kernel, [((8, 72, 128), F32), ((ROWS, 512), BF16), ((8, ROWS), jnp.int32)],
         near, far, col0, col1, col2, col3,

time: 120 us -> 122 us (1.017)
  starting transfers between devices: 62 us -> 68.2 us
  waiting for transfers between devices: 27.3 us -> 24 us
    all_to_all x3, waiting for transfers between devices: 12.5 us -> 2.59 us  [exchange(): return lax.all_to_all(x, axes, split_axis=0, concat_axis=0, tiled=True)]
    all_to_all x3, starting transfers between devices: 28.6 us -> 37 us  [exchange(): return lax.all_to_all(x, axes, split_axis=0, concat_axis=0, tiled=True)]
    ppermute x8, waiting for transfers between devices: 14.9 us -> 21.4 us  [swap(): return lax.ppermute(x, axis, [(0, 1), (1, 0)])]
    ppermute x8, starting transfers between devices: 33.4 us -> 31.2 us  [swap(): return lax.ppermute(x, axis, [(0, 1), (1, 0)])]
  transfers between devices with their start and end apart: 11 -> 11, of which waited for: 6 -> 9; matrix products, arithmetic and copies ran while one was open for 0% -> 0% of each run, Pallas kernels for 2% -> 2%
where the time goes in v7:
time: 122 us; the launch traced here: 121 us
  starting transfers between devices  68.2 us (56%)
  waiting for transfers between devices  24 us (20%)
  blocking collectives  20.2 us (17%)
  Pallas kernels  7.57 us (6%)
    all_to_all x3, starting transfers between devices, exchange(): return lax.all_to_all(x, axes, split_axis=0, concat_axis=0, tiled=True)  37 us
    ppermute x8, starting transfers between devices, swap(): return lax.ppermute(x, axis, [(0, 1), (1, 0)])  31.2 us
    ppermute x8, waiting for transfers between devices, swap(): return lax.ppermute(x, axis, [(0, 1), (1, 0)])  21.4 us
    all_to_all x2, blocking collectives, exchange(): return lax.all_to_all(x, axes, split_axis=0, concat_axis=0, tiled=True)  20.2 us
    pallas_call x11, Pallas kernels, call(): pl.pallas_call(kernel, out_shape=[jax.ShapeDtypeStruct(shape, dtype) for...  7.57 us
    all_to_all x3, waiting for transfers between devices, exchange(): return lax.all_to_all(x, axes, split_axis=0, concat_axis=0, tiled=True)  2.59 us
  transfers between devices with their start and end apart: 11, of which 9 were waited for; matrix products, arithmetic and copies ran while one was open for 0% of the time, Pallas kernels for 2%

profile of v7, /device:TPU:1, one launch (start us, length us, event | category | flops | bytes accessed | tf_op | source)
XLA Modules:
  0.0 120.8 jit_solution(16976144358523148071)
XLA Ops:
  0.6 1.6 %shard_map.76 = bf16[8,144,128]{2,1,0:T(8,128)(2,1)} custom-call(bf16[32,512]{1,0:T(8,128)(2,1)} %queries.1, s32[7,32]{1,0:T(8,128)} %bitcast.2, s32[7,32]{1,0:T(8,128)} %bitcast.3), custom_call_target="tpu_custom_call" | custom-call | tf_op jit(solution)/shard_map/pallas_call | solution.py:25
  2.3 15.8 %all-to-all-start = ((bf16[8,144,128]{2,1,0:T(8,128)(2,1)}), bf16[8,144,128]{2,1,0:T(8,128)(2,1)S(1)}, u32[]{:S(2)}, u32[]{:S(2)}) async-start(bf16[8,144,128]{2,1,0:T(8,128)(2,1)} %shard_map.76), calls=%async_computation | async-start | bytes 589824 | tf_op jit(solution)/shard_map/all_to_all | solution.py:250
  18.1 0.4 shard_map.77.col0
  18.4 4.8 %collective-permute-start.1 = (bf16[256,512]{1,0:T(8,128)(2,1)S(1)}, bf16[256,512]{1,0:T(8,128)(2,1)S(1)}, u32[]{:S(2)}, u32[]{:S(2)}) collective-permute-start(bf16[256,512]{1,0:T(8,128)(2,1)S(1)} %shard_map.77.col0), channel_id=1, source_target_pairs={{0,256},{256,0},{1,257},{257,1},{2,258},{258,2},{3,259},{259,3},{4... | collective-permute-start | bytes 786440 | tf_op jit(solution)/shard_map/ppermute | solution.py:246
  23.3 3.1 %collective-permute-start = (bf16[256,512]{1,0:T(8,128)(2,1)S(1)}, bf16[256,512]{1,0:T(8,128)(2,1)S(1)}, u32[]{:S(2)}, u32[]{:S(2)}) collective-permute-start(bf16[256,512]{1,0:T(8,128)(2,1)S(1)} %shard_map.77.col0), channel_id=1, source_target_pairs={{0,8},{8,0},{1,9},{9,1},{2,10},{10,2},{3,11},{11,3},{4,12},{12,4},... | collective-permute-start | bytes 786440 | tf_op jit(solution)/shard_map/ppermute | solution.py:246
  26.4 2.3 %collective-permute-done.1.col2 = bf16[256,512]{1,0:T(8,128)(2,1)S(1)} collective-permute-done((bf16[256,512]{1,0:T(8,128)(2,1)S(1)}, bf16[256,512]{1,0:T(8,128)(2,1)S(1)}, u32[]{:S(2)}, u32[]{:S(2)}) %collective-permute-start.1) | collective-permute-done | bytes 262176 | tf_op jit(solution)/shard_map/ppermute | solution.py:246
  28.7 3.8 %collective-permute-start.2 = (bf16[256,512]{1,0:T(8,128)(2,1)S(1)}, bf16[256,512]{1,0:T(8,128)(2,1)S(1)}, u32[]{:S(2)}, u32[]{:S(2)}) collective-permute-start(bf16[256,512]{1,0:T(8,128)(2,1)S(1)} %collective-permute-done.1.col2), channel_id=1, source_target_pairs={{0,8},{8,0},{1,9},{9,1},{2,10},{10,2},{3,11},{11,3},{4,12},{12,4},... | collective-permute-start | bytes 786440 | tf_op jit(solution)/shard_map/ppermute | solution.py:246
  32.5 1.1 collective-permute-done.2.refs_2_.col3
  33.6 2.1 %all-to-all-done.refs_0_ = bf16[8,144,128]{2,1,0:T(8,128)(2,1)S(1)} async-done(((bf16[8,144,128]{2,1,0:T(8,128)(2,1)}), bf16[8,144,128]{2,1,0:T(8,128)(2,1)S(1)}, u32[]{:S(2)}, u32[]{:S(2)}) %all-to-all-start) | async-done | bytes 294944 | tf_op jit(solution)/shard_map/all_to_all | solution.py:250
  35.7 2.4 %collective-permute-start.3 = (bf16[8,144,128]{2,1,0:T(8,128)(2,1)S(1)}, bf16[8,144,128]{2,1,0:T(8,128)(2,1)S(1)}, u32[]{:S(2)}, u32[]{:S(2)}) collective-permute-start(bf16[8,144,128]{2,1,0:T(8,128)(2,1)S(1)} %shard_map.78.near), channel_id=1, source_target_pairs={{0,16},{16,0},{1,17},{17,1},{2,18},{18,2},{3,19},{19,3},{4,20},{20... | collective-permute-start | bytes 884744 | tf_op jit(solution)/shard_map/ppermute | solution.py:246
  38.1 5.1 %collective-permute-done.3.far = bf16[8,144,128]{2,1,0:T(8,128)(2,1)S(1)} collective-permute-done((bf16[8,144,128]{2,1,0:T(8,128)(2,1)S(1)}, bf16[8,144,128]{2,1,0:T(8,128)(2,1)S(1)}, u32[]{:S(2)}, u32[]{:S(2)}) %collective-permute-start.3) | collective-permute-done | bytes 294944 | tf_op jit(solution)/shard_map/ppermute | solution.py:246
  43.2 0.8 shard_map.79
  43.9 11.3 %all_to_all.25.came = f32[8,72,128]{2,1,0:T(8,128)S(1)} all-to-all(f32[8,72,128]{2,1,0:T(8,128)S(1)} %get-tuple-element.20), channel_id=1, replica_groups=mesh['yh'=2,'zh'=8,'zp'=2,'c'=2,'yl'=2,'x'=4] {'yl','x'}, dimensions={0} | all-to-all | bytes 589824 | tf_op jit(solution)/shard_map/all_to_all | solution.py:250
  55.3 8.9 %all_to_all.26.scores = f32[8,72,128]{2,1,0:T(8,128)S(1)} all-to-all(f32[8,72,128]{2,1,0:T(8,128)S(1)} %shard_map.80), channel_id=1, replica_groups=mesh['yh'=2,'zh'=8,'zp'=2,'c'=2,'yl'=2,'x'=4] {'yl','x'}, dimensions={0} | all-to-all | bytes 589824 | tf_op jit(solution)/shard_map/all_to_all | solution.py:250
  64.2 0.7 shard_map.81
  64.9 12.2 %all-to-all-start.3 = ((f32[16,8,128]{2,1,0:T(8,128)}), f32[16,8,128]{2,1,0:T(8,128)S(1)}, u32[]{:S(2)}, u32[]{:S(2)}) async-start(f32[16,8,128]{2,1,0:T(8,128)} %get-tuple-element.21), calls=%async_computation.3 | async-start | bytes 131072 | tf_op jit(solution)/shard_map/all_to_all | solution.py:250
  77.1 0.8 shard_map.82
  77.9 3.3 %collective-permute-start.4 = (bf16[128,512]{1,0:T(8,128)(2,1)S(1)}, bf16[128,512]{1,0:T(8,128)(2,1)S(1)}, u32[]{:S(2)}, u32[]{:S(2)}) collective-permute-start(bf16[128,512]{1,0:T(8,128)(2,1)S(1)} %get-tuple-element.25), channel_id=1, source_target_pairs={{0,16},{16,0},{1,17},{17,1},{2,18},{18,2},{3,19},{19,3},{4,20},{20... | collective-permute-start | bytes 393224 | tf_op jit(solution)/shard_map/ppermute | solution.py:246
  81.1 2.0 %collective-permute-start.5 = (bf16[128,512]{1,0:T(8,128)(2,1)S(1)}, bf16[128,512]{1,0:T(8,128)(2,1)S(1)}, u32[]{:S(2)}, u32[]{:S(2)}) collective-permute-start(bf16[128,512]{1,0:T(8,128)(2,1)S(1)} %get-tuple-element.26), channel_id=1, source_target_pairs={{0,16},{16,0},{1,17},{17,1},{2,18},{18,2},{3,19},{19,3},{4,20},{20... | collective-permute-start | bytes 393224 | tf_op jit(solution)/shard_map/ppermute | solution.py:246
  83.2 0.6 collective-permute-done.4.refs_0_
  83.7 4.5 %collective-permute-done.5.refs_1_ = bf16[128,512]{1,0:T(8,128)(2,1)S(1)} collective-permute-done((bf16[128,512]{1,0:T(8,128)(2,1)S(1)}, bf16[128,512]{1,0:T(8,128)(2,1)S(1)}, u32[]{:S(2)}, u32[]{:S(2)}) %collective-permute-start.5) | collective-permute-done | bytes 131104 | tf_op jit(solution)/shard_map/ppermute | solution.py:246
  88.2 0.5 all-to-all-done.3.stats
  88.7 1.0 shard_map.83
  89.7 9.1 %all-to-all-start.4 = ((bf16[8,32,512]{2,1,0:T(8,128)(2,1)}), bf16[8,32,512]{2,1,0:T(8,128)(2,1)S(1)}, u32[]{:S(2)}, u32[]{:S(2)}) async-start(bf16[8,32,512]{2,1,0:T(8,128)(2,1)} %get-tuple-element.27), calls=%async_computation.4 | async-start | bytes 524288 | tf_op jit(solution)/shard_map/all_to_all | solution.py:250
  98.8 0.7 shard_map.84
  99.5 7.3 %collective-permute-start.6 = (bf16[2,256,512]{2,1,0:T(8,128)(2,1)S(1)}, bf16[2,256,512]{2,1,0:T(8,128)(2,1)S(1)}, u32[]{:S(2)}, u32[]{:S(2)}) collective-permute-start(bf16[2,256,512]{2,1,0:T(8,128)(2,1)S(1)} %get-tuple-element.32), channel_id=1, source_target_pairs={{0,8},{8,0},{1,9},{9,1},{2,10},{10,2},{3,11},{11,3},{4,12},{12,4},... | collective-permute-start | bytes 1572872 | tf_op jit(solution)/shard_map/ppermute | solution.py:246
  106.8 1.5 %collective-permute-done.6.came = bf16[2,256,512]{2,1,0:T(8,128)(2,1)S(1)} collective-permute-done((bf16[2,256,512]{2,1,0:T(8,128)(2,1)S(1)}, bf16[2,256,512]{2,1,0:T(8,128)(2,1)S(1)}, u32[]{:S(2)}, u32[]{:S(2)}) %collective-permute-start.6) | collective-permute-done | bytes 524320 | tf_op jit(solution)/shard_map/ppermute | solution.py:246
  108.3 0.1 shard_map.86
  108.4 4.5 %collective-permute-start.7 = (bf16[256,512]{1,0:T(8,128)(2,1)S(1)}, bf16[256,512]{1,0:T(8,128)(2,1)S(1)}, u32[]{:S(2)}, u32[]{:S(2)}) collective-permute-start(bf16[256,512]{1,0:T(8,128)(2,1)S(1)} %get-tuple-element.34), channel_id=1, source_target_pairs={{0,256},{256,0},{1,257},{257,1},{2,258},{258,2},{3,259},{259,3},{4... | collective-permute-start | bytes 786440 | tf_op jit(solution)/shard_map/ppermute | solution.py:246
  113.0 6.4 %collective-permute-done.7.came = bf16[256,512]{1,0:T(8,128)(2,1)S(1)} collective-permute-done((bf16[256,512]{1,0:T(8,128)(2,1)S(1)}, bf16[256,512]{1,0:T(8,128)(2,1)S(1)}, u32[]{:S(2)}, u32[]{:S(2)}) %collective-permute-start.7) | collective-permute-done | bytes 262176 | tf_op jit(solution)/shard_map/ppermute | solution.py:246
  119.4 0.7 shard_map.87
  120.1 0.7 shard_map.85
  (8 shorter events, 0.0 us)
Async XLA Ops:
  2.2 15.8 %copy-start = (bf16[224,512]{1,0:T(8,128)(2,1)S(1)}, bf16[224,512]{1,0:T(8,128)(2,1)}, u32[]{:S(2)}) copy-start(bf16[224,512]{1,0:T(8,128)(2,1)} %negatives.1) | copy-start | bytes 688132
  2.2 15.8 %copy-start.1 = (bf16[32,512]{1,0:T(8,128)(2,1)S(1)}, bf16[32,512]{1,0:T(8,128)(2,1)}, u32[]{:S(2)}) copy-start(bf16[32,512]{1,0:T(8,128)(2,1)} %passages.3) | copy-start | bytes 98308
  2.3 33.4 %all-to-all-start = ((bf16[8,144,128]{2,1,0:T(8,128)(2,1)}), bf16[8,144,128]{2,1,0:T(8,128)(2,1)S(1)}, u32[]{:S(2)}, u32[]{:S(2)}) async-start(bf16[8,144,128]{2,1,0:T(8,128)(2,1)} %shard_map.76), calls=%async_computation | async-start | bytes 589824 | tf_op jit(solution)/shard_map/all_to_all | solution.py:250
  18.4 10.3 %collective-permute-start.1 = (bf16[256,512]{1,0:T(8,128)(2,1)S(1)}, bf16[256,512]{1,0:T(8,128)(2,1)S(1)}, u32[]{:S(2)}, u32[]{:S(2)}) collective-permute-start(bf16[256,512]{1,0:T(8,128)(2,1)S(1)} %shard_map.77.col0), channel_id=1, source_target_pairs={{0,256},{256,0},{1,257},{257,1},{2,258},{258,2},{3,259},{259,3},{4... | collective-permute-start | bytes 786440 | tf_op jit(solution)/shard_map/ppermute | solution.py:246
  23.3 9.2 %collective-permute-start = (bf16[256,512]{1,0:T(8,128)(2,1)S(1)}, bf16[256,512]{1,0:T(8,128)(2,1)S(1)}, u32[]{:S(2)}, u32[]{:S(2)}) collective-permute-start(bf16[256,512]{1,0:T(8,128)(2,1)S(1)} %shard_map.77.col0), channel_id=1, source_target_pairs={{0,8},{8,0},{1,9},{9,1},{2,10},{10,2},{3,11},{11,3},{4,12},{12,4},... | collective-permute-start | bytes 786440 | tf_op jit(solution)/shard_map/ppermute | solution.py:246
  28.7 4.9 %collective-permute-start.2 = (bf16[256,512]{1,0:T(8,128)(2,1)S(1)}, bf16[256,512]{1,0:T(8,128)(2,1)S(1)}, u32[]{:S(2)}, u32[]{:S(2)}) collective-permute-start(bf16[256,512]{1,0:T(8,128)(2,1)S(1)} %collective-permute-done.1.col2), channel_id=1, source_target_pairs={{0,8},{8,0},{1,9},{9,1},{2,10},{10,2},{3,11},{11,3},{4,12},{12,4},... | collective-permute-start | bytes 786440 | tf_op jit(solution)/shard_map/ppermute | solution.py:246
  35.7 7.5 %collective-permute-start.3 = (bf16[8,144,128]{2,1,0:T(8,128)(2,1)S(1)}, bf16[8,144,128]{2,1,0:T(8,128)(2,1)S(1)}, u32[]{:S(2)}, u32[]{:S(2)}) collective-permute-start(bf16[8,144,128]{2,1,0:T(8,128)(2,1)S(1)} %shard_map.78.near), channel_id=1, source_target_pairs={{0,16},{16,0},{1,17},{17,1},{2,18},{18,2},{3,19},{19,3},{4,20},{20... | collective-permute-start | bytes 884744 | tf_op jit(solution)/shard_map/ppermute | solution.py:246
  64.9 23.7 %all-to-all-start.3 = ((f32[16,8,128]{2,1,0:T(8,128)}), f32[16,8,128]{2,1,0:T(8,128)S(1)}, u32[]{:S(2)}, u32[]{:S(2)}) async-start(f32[16,8,128]{2,1,0:T(8,128)} %get-tuple-element.21), calls=%async_computation.3 | async-start | bytes 131072 | tf_op jit(solution)/shard_map/all_to_all | solution.py:250
  77.9 5.9 %collective-permute-start.4 = (bf16[128,512]{1,0:T(8,128)(2,1)S(1)}, bf16[128,512]{1,0:T(8,128)(2,1)S(1)}, u32[]{:S(2)}, u32[]{:S(2)}) collective-permute-start(bf16[128,512]{1,0:T(8,128)(2,1)S(1)} %get-tuple-element.25), channel_id=1, source_target_pairs={{0,16},{16,0},{1,17},{17,1},{2,18},{18,2},{3,19},{19,3},{4,20},{20... | collective-permute-start | bytes 393224 | tf_op jit(solution)/shard_map/ppermute | solution.py:246
  81.1 7.0 %collective-permute-start.5 = (bf16[128,512]{1,0:T(8,128)(2,1)S(1)}, bf16[128,512]{1,0:T(8,128)(2,1)S(1)}, u32[]{:S(2)}, u32[]{:S(2)}) collective-permute-start(bf16[128,512]{1,0:T(8,128)(2,1)S(1)} %get-tuple-element.26), channel_id=1, source_target_pairs={{0,16},{16,0},{1,17},{17,1},{2,18},{18,2},{3,19},{19,3},{4,20},{20... | collective-permute-start | bytes 393224 | tf_op jit(solution)/shard_map/ppermute | solution.py:246
  89.7 30.4 %all-to-all-start.4 = ((bf16[8,32,512]{2,1,0:T(8,128)(2,1)}), bf16[8,32,512]{2,1,0:T(8,128)(2,1)S(1)}, u32[]{:S(2)}, u32[]{:S(2)}) async-start(bf16[8,32,512]{2,1,0:T(8,128)(2,1)} %get-tuple-element.27), calls=%async_computation.4 | async-start | bytes 524288 | tf_op jit(solution)/shard_map/all_to_all | solution.py:250
  99.5 8.8 %collective-permute-start.6 = (bf16[2,256,512]{2,1,0:T(8,128)(2,1)S(1)}, bf16[2,256,512]{2,1,0:T(8,128)(2,1)S(1)}, u32[]{:S(2)}, u32[]{:S(2)}) collective-permute-start(bf16[2,256,512]{2,1,0:T(8,128)(2,1)S(1)} %get-tuple-element.32), channel_id=1, source_target_pairs={{0,8},{8,0},{1,9},{9,1},{2,10},{10,2},{3,11},{11,3},{4,12},{12,4},... | collective-permute-start | bytes 1572872 | tf_op jit(solution)/shard_map/ppermute | solution.py:246
  108.4 10.9 %collective-permute-start.7 = (bf16[256,512]{1,0:T(8,128)(2,1)S(1)}, bf16[256,512]{1,0:T(8,128)(2,1)S(1)}, u32[]{:S(2)}, u32[]{:S(2)}) collective-permute-start(bf16[256,512]{1,0:T(8,128)(2,1)S(1)} %get-tuple-element.34), channel_id=1, source_target_pairs={{0,256},{256,0},{1,257},{257,1},{2,258},{258,2},{3,259},{259,3},{4... | collective-permute-start | bytes 786440 | tf_op jit(solution)/shard_map/ppermute | solution.py:246

commit v8 on v2

v8 whole, which is shorter than its diff:
```python
import math

import jax
import jax.numpy as jnp
from jax import lax
from jax.experimental import pallas as pl
from jax.experimental.pallas import tpu as pltpu
from jax.sharding import Mesh
from jax.sharding import PartitionSpec as P

BF16 = jnp.bfloat16
F32 = jnp.float32
NZ = 16
NH = 8
NB = 8
ROWS = 256
ABSENT = -1e30
VMEM_LIMIT = 48 * 1024 * 1024
PACK_LIMIT = 62 * 1024 * 1024
HOLD_FLOPS = 1153000000


def call(kernel, out_shapes, *args, hbm=0, scratch=(), limit=VMEM_LIMIT):
    specs = [pl.BlockSpec(memory_space=pl.ANY)] * hbm
    specs += [pl.BlockSpec(memory_space=pltpu.VMEM)] * (len(args) - hbm)
    return pl.pallas_call(
        kernel,
        out_shape=[jax.ShapeDtypeStruct(shape, dtype) for shape, dtype in out_shapes],
        in_specs=specs,
        out_specs=[pl.BlockSpec(memory_space=pltpu.VMEM)] * len(out_shapes),
        scratch_shapes=list(scratch),
        compiler_params=pltpu.CompilerParams(vmem_limit_bytes=limit),
    )(*args)


def pack_kernel(queries, owners, rows, sent, mine, short, wide, sems):
    copies = [
        pltpu.make_async_copy(owners, short.at[0], sems.at[0]),
        pltpu.make_async_copy(rows, short.at[1], sems.at[1]),
        pltpu.make_async_copy(queries, mine, sems.at[2]),
    ]
    for copy in copies:
        copy.start()
    yh, zh, zp, c = (lax.axis_index(axis) for axis in ("yh", "zh", "zp", "c"))
    line = lax.broadcasted_iota(jnp.int32, (NH * 16, 128), 0)
    lane = lax.broadcasted_iota(jnp.int32, (NH * 16, 128), 1)
    block = line % 16
    z = (line // 16) * 2 + (zp ^ (block // 4))
    owner = ((yh ^ (block // 2 % 2)) * NZ + z) * 2 + (c ^ (block % 2))
    owner = jnp.where((block < NB) & (lane // 32 == zh % 4), owner, -2)
    copies[0].wait()
    copies[1].wait()
    for j in range(4):
        wide[:, :, j * 32 : (j + 1) * 32] = short[...]
    asked = jnp.full((NH * 16, 128), -1, jnp.int32)
    for k in range(short.shape[1]):
        asked = jnp.where(wide[0, k : k + 1, :] == owner, wide[1, k : k + 1, :], asked)
    asked = asked.astype(F32).astype(BF16)
    for to in range(NH):
        sent[to, 128:144, :] = asked[to * 16 : (to + 1) * 16, :]
    copies[2].wait()
    for to in range(NH):
        for l in range(4):
            sent[to, l * 32 : (l + 1) * 32, :] = mine[:, l * 128 : (l + 1) * 128]


def column_pack_kernel(passages, negatives, columns, sems):
    copies = [
        pltpu.make_async_copy(negatives, columns.at[32:256], sems.at[0]),
        pltpu.make_async_copy(passages, columns.at[0:32], sems.at[1]),
    ]
    for copy in copies:
        copy.start()
    for copy in copies:
        copy.wait()


def unpack(came, lines, queries, asked):
    for z in range(NH):
        for l in range(4):
            queries[z * 32 : (z + 1) * 32, l * 128 : (l + 1) * 128] = came[z, l * 32 : (l + 1) * 32, :]
    for g in range(2):
        rows = came[4 * g, 128:144, :].astype(F32)
        for z in range(4 * g + 1, 4 * g + 4):
            rows = jnp.maximum(rows, came[z, 128:144, :].astype(F32))
        asked[:, g * 128 : (g + 1) * 128] = rows[lines, :].astype(jnp.int32)


def stack_kernel(first, second, both):
    both[0:256, :] = first[...]
    both[256:512, :] = second[...]


def score_kernel(near, *refs):
    columns, (parts, queries, asked) = refs[:4], refs[4:]
    scale = 3.0 / math.sqrt(4096)
    unpack(near, slice(0, NB), queries, asked)
    every = queries[...]
    place = lax.broadcasted_iota(jnp.int32, (224, ROWS), 0)
    for o in range(NB):
        cols = columns[o % 4][o // 4 * 256 : (o // 4 + 1) * 256, :]
        part = lax.dot_general(cols, every, (((1,), (1,)), ((), ())), preferred_element_type=F32)
        want = asked[o : o + 1, :]
        hard = jnp.sum(jnp.where(place == want, part[32:256, :], 0.0), axis=0, keepdims=True) * scale
        hard = jnp.where(want >= 0, hard, ABSENT)
        h, a = o // 2, o % 2
        for l in range(2):
            lanes = slice(l * 128, (l + 1) * 128)
            parts[h * 2 + l, a * 32 : (a + 1) * 32, :] = part[0:32, lanes] * scale
            parts[h * 2 + l, 64 + a : 65 + a, :] = hard[:, lanes]
            if a == 1:
                parts[h * 2 + l, 66:72, :] = jnp.zeros((6, 128), F32)


def add_kernel(came, sent):
    total = came[0]
    for i in range(1, 8):
        total = total + came[i]
    for i in range(8):
        sent[i] = total


def stat_kernel(scores, sent, cross):
    cross[...] = scores[4:8]
    for l in range(2):
        batch = [scores[h * 2 + l, 0:64, :] for h in range(4)]
        hard = [scores[h * 2 + l, 64:66, :] for h in range(4)]
        top = jnp.maximum(
            jnp.max(jnp.maximum(jnp.maximum(batch[0], batch[1]), jnp.maximum(batch[2], batch[3])), axis=0, keepdims=True),
            jnp.max(jnp.maximum(jnp.maximum(hard[0], hard[1]), jnp.maximum(hard[2], hard[3])), axis=0, keepdims=True),
        )
        total = jnp.sum(sum(jnp.exp(b - top) for b in batch), axis=0, keepdims=True)
        total = total + jnp.sum(sum(jnp.exp(h - top) for h in hard), axis=0, keepdims=True)
        for to in range(NZ):
            sent[to, l : l + 1, :] = top
            sent[to, 2 + l : 3 + l, :] = total
    for to in range(NZ):
        sent[to, 4:8, :] = jnp.zeros((4, 128), F32)


def row_logs(stats, zp):
    logs = []
    for l in range(2):
        tops = jnp.where(zp == 0, stats[:, 0, l, :], stats[:, 1, l, :])
        totals = jnp.where(zp == 0, stats[:, 0, 2 + l, :], stats[:, 1, 2 + l, :])
        top = jnp.max(tops, axis=0, keepdims=True)
        logs.append(top + jnp.log(jnp.sum(totals * jnp.exp(tops - top), axis=0, keepdims=True)))
    return jnp.concatenate(logs, axis=1)


def block_weights(scores, o, logs, want, targets):
    h, a = o // 2, o % 2
    batch = jnp.concatenate([scores[h * 2 + l, a * 32 : (a + 1) * 32, :] for l in range(2)], axis=1)
    hard = jnp.concatenate([scores[h * 2 + l, 64 + a : 65 + a, :] for l in range(2)], axis=1)
    weights = jnp.exp(batch - logs)
    if targets and o == 0:
        row = lax.broadcasted_iota(jnp.int32, (32, ROWS), 0)
        lane = lax.broadcasted_iota(jnp.int32, (32, ROWS), 1)
        weights = weights - (lane == lax.axis_index("zh") * 32 + row).astype(F32)
    line = lax.broadcasted_iota(jnp.int32, (224, ROWS), 0)
    hard = jnp.where(line == want, jnp.exp(hard - logs), 0.0)
    return jnp.concatenate([weights.astype(BF16), hard.astype(BF16)], axis=0)


def share_kernel(stats, scores, asked, *refs):
    columns, (sent, logs, total) = refs[:4], refs[4:]
    zp = lax.axis_index("zp")
    near = row_logs(stats, zp)
    logs[0:1, :] = near
    logs[1:2, :] = row_logs(stats, 1 - zp)
    for o in range(NB):
        weights = block_weights(scores, o, near, asked[o : o + 1, :], True)
        cols = columns[o % 4][o // 4 * 256 : (o // 4 + 1) * 256, :]
        term = lax.dot_general(weights, cols, (((0,), (0,)), ((), ())), preferred_element_type=F32)
        if o == 0:
            total[...] = term
        elif o < NB - 1:
            total[...] += term
        else:
            sent[...] = (total[...] + term).astype(BF16).reshape(NH, 32, 512)


def column_grad_kernel(logs, scores, asked, queries, far_scores, far, keep, give, far_queries, far_asked):
    unpack(far, slice(4, 8), far_queries, far_asked)
    near_queries, other_queries = queries[...], far_queries[...]
    for o in range(4):
        weights = block_weights(scores, o, logs[0:1, :], asked[o : o + 1, :], True)
        grad = jnp.dot(weights, near_queries, preferred_element_type=F32)
        weights = block_weights(far_scores, o, logs[1:2, :], far_asked[o : o + 1, :], False)
        grad = grad + jnp.dot(weights, other_queries, preferred_element_type=F32)
        (give if o % 2 else keep)[o // 2] = grad.astype(BF16)


def pair_kernel(keep, came, own, sent):
    own[...] = keep[0].astype(F32) + came[0].astype(F32)
    sent[...] = (keep[1].astype(F32) + came[1].astype(F32)).astype(BF16)


def column_kernel(own, came, passage_out, negative_out):
    passage_out[...] = (own[0:32, :] + came[0:32, :].astype(F32)).astype(BF16)
    negative_out[...] = (own[32:256, :] + came[32:256, :].astype(F32)).astype(BF16)


def query_kernel(came, query_out):
    total = came[0].astype(F32)
    for z in range(1, NH):
        total = total + came[z].astype(F32)
    query_out[...] = total.astype(BF16)


def hold(x):
    return pl.pallas_call(
        lambda *refs: None,
        out_shape=jax.ShapeDtypeStruct(x.shape, x.dtype),
        in_specs=[pl.BlockSpec(memory_space=pltpu.VMEM)],
        out_specs=pl.BlockSpec(memory_space=pltpu.VMEM),
        input_output_aliases={0: 0},
        cost_estimate=pl.CostEstimate(flops=HOLD_FLOPS, bytes_accessed=0, transcendentals=0),
        compiler_params=pltpu.CompilerParams(vmem_limit_bytes=VMEM_LIMIT),
    )(x)


def swap(x, axis):
    return lax.ppermute(x, axis, [(0, 1), (1, 0)])


def exchange(x, axes):
    return lax.all_to_all(x, axes, split_axis=0, concat_axis=0, tiled=True)


def shards(queries, passages, negatives, hard_owner, hard_row):
    (sent,) = call(
        pack_kernel, [((NH, 144, 128), BF16)],
        queries, hard_owner.T, hard_row.T, hbm=3, limit=PACK_LIMIT,
        scratch=[
            pltpu.VMEM((32, 512), BF16), pltpu.VMEM((2, 7, 32), jnp.int32), pltpu.VMEM((2, 7, 128), jnp.int32),
            pltpu.SemaphoreType.DMA((3,)),
        ],
    )
    (col0,) = call(
        column_pack_kernel, [((256, 512), BF16)], passages, negatives, hbm=2,
        scratch=[pltpu.SemaphoreType.DMA((2,))],
    )
    (pair,) = call(stack_kernel, [((512, 512), BF16)], col0, swap(col0, "zp"))
    near = hold(exchange(sent, "zh"))
    other = swap(pair, "yh")
    columns = (pair, swap(pair, "c"), other, swap(other, "c"))
    parts, queries, asked = call(
        score_kernel, [((8, 72, 128), F32), ((ROWS, 512), BF16), ((NB, ROWS), jnp.int32)], near, *columns
    )
    far = swap(near, "zp")
    (summed,) = call(add_kernel, [((8, 72, 128), F32)], exchange(parts, ("yl", "x")))
    scores = exchange(summed, ("yl", "x"))
    stats, cross = call(stat_kernel, [((NZ, 8, 128), F32), ((4, 72, 128), F32)], scores)
    stats = exchange(stats, ("zh", "zp")).reshape(NH, 2, 8, 128)
    far_scores = swap(cross, "zp")
    q_part, logs = call(
        share_kernel, [((NH, 32, 512), BF16), ((8, ROWS), F32)], stats, scores, asked, *columns,
        scratch=[pltpu.VMEM((ROWS, 512), F32)],
    )
    q_came = exchange(q_part, "zh")
    keep, give = call(
        column_grad_kernel, [((2, 256, 512), BF16), ((2, 256, 512), BF16)],
        logs, scores, asked, queries, far_scores, far,
        scratch=[pltpu.VMEM((ROWS, 512), BF16), pltpu.VMEM((4, ROWS), jnp.int32)],
    )
    own, cross = call(pair_kernel, [((256, 512), F32), ((256, 512), BF16)], keep, swap(give, "c"))
    cross = swap(cross, "yh")
    passage_out, negative_out = call(column_kernel, [((32, 512), BF16), ((224, 512), BF16)], own, cross)
    (query_out,) = call(query_kernel, [((32, 512), BF16)], q_came)
    return (query_out, passage_out, negative_out)


def solution(mesh):
    fine = Mesh(mesh.devices.reshape(2, NH, 2, 2, 2, 4), ("yh", "zh", "zp", "c", "yl", "x"))
    dp, mp = ("yh", "zh", "zp", "c"), ("yl", "x")
    return jax.shard_map(
        shards,
        mesh=fine,
        in_specs=(P(dp, mp), P(dp, mp), P(dp, mp), P(dp, None), P(dp, None)),
        out_specs=(P(dp, mp), P(dp, mp), P(dp, mp)),
        check_vma=False,
    )
```

time: 137 us -> 119 us (0.87)
  blocking collectives: 43.9 us -> 20.3 us
  starting transfers between devices: 56.9 us -> 63.5 us
  local copies, waits for them, and re-layouts: 3.73 us -> 2.35 us
    all_to_all x3 -> x2, blocking collectives: 43.9 us -> 20.3 us  [exchange(): return lax.all_to_all(x, axes, split_axis=0, concat_axis=0, tiled=True)]
    all_to_all x2 -> x3, starting transfers between devices: 19.1 us -> 31.5 us  [exchange(): return lax.all_to_all(x, axes, split_axis=0, concat_axis=0, tiled=True)]
    ppermute x11 -> x8, starting transfers between devices: 37.8 us -> 32 us  [swap(): return lax.ppermute(x, axis, [(0, 1), (1, 0)])]
    ppermute x11 -> x8, waiting for transfers between devices: 12.9 us -> 16.7 us  [swap(): return lax.ppermute(x, axis, [(0, 1), (1, 0)])]
    all_to_all x2 -> x3, waiting for transfers between devices: 9.7 us -> 6.49 us  [exchange(): return lax.all_to_all(x, axes, split_axis=0, concat_axis=0, tiled=True)]
    unnamed x12 -> x6, local copies, waits for them, and re-layouts: 3.73 us -> 2.35 us
    pallas_call x8 -> x11, Pallas kernels: 7.82 us -> 7.26 us  [call(): pl.pallas_call(kernel, out_shape=[jax.ShapeDtypeStruct(shape, dtype) for...]
  transfers between devices with their start and end apart: 13 -> 11, of which waited for: 6 -> 5; matrix products, arithmetic and copies ran while one was open for 0% -> 0% of each run, Pallas kernels for 1% -> 4%
where the time goes in v8:
time: 119 us; the launch traced here: 117 us
  starting transfers between devices  63.5 us (53%)
  waiting for transfers between devices  23.2 us (19%)
  blocking collectives  20.3 us (17%)
  Pallas kernels  7.26 us (6%)
  local copies, waits for them, and re-layouts  2.35 us (2%)
    ppermute x8, starting transfers between devices, swap(): return lax.ppermute(x, axis, [(0, 1), (1, 0)])  32 us
    all_to_all x3, starting transfers between devices, exchange(): return lax.all_to_all(x, axes, split_axis=0, concat_axis=0, tiled=True)  31.5 us
    all_to_all x2, blocking collectives, exchange(): return lax.all_to_all(x, axes, split_axis=0, concat_axis=0, tiled=True)  20.3 us
    ppermute x8, waiting for transfers between devices, swap(): return lax.ppermute(x, axis, [(0, 1), (1, 0)])  16.7 us
    pallas_call x11, Pallas kernels, call(): pl.pallas_call(kernel, out_shape=[jax.ShapeDtypeStruct(shape, dtype) for...  7.26 us
    all_to_all x3, waiting for transfers between devices, exchange(): return lax.all_to_all(x, axes, split_axis=0, concat_axis=0, tiled=True)  6.49 us
  transfers between devices with their start and end apart: 11, of which 5 were waited for; matrix products, arithmetic and copies ran while one was open for 0% of the time, Pallas kernels for 4%

profile of v8, /device:TPU:1, one launch (start us, length us, event | category | flops | bytes accessed | tf_op | source)
XLA Modules:
  0.0 117.4 jit_solution(10199965160685756550)
XLA Ops:
  0.6 0.9 copy-done
  1.6 0.8 copy-done.1
  2.3 0.3 shard_map.78.first
  2.7 4.4 %collective-permute-start = (bf16[256,512]{1,0:T(8,128)(2,1)S(1)}, bf16[256,512]{1,0:T(8,128)(2,1)S(1)}, u32[]{:S(2)}, u32[]{:S(2)}) collective-permute-start(bf16[256,512]{1,0:T(8,128)(2,1)S(1)} %shard_map.78.first), channel_id=1, source_target_pairs={{0,16},{16,0},{1,17},{17,1},{2,18},{18,2},{3,19},{19,3},{4,20},{20... | collective-permute-start | bytes 786440 | tf_op jit(solution)/shard_map/ppermute | solution.py:224
  7.0 1.6 %shard_map.76 = bf16[8,144,128]{2,1,0:T(8,128)(2,1)} custom-call(bf16[32,512]{1,0:T(8,128)(2,1)} %queries.1, s32[7,32]{1,0:T(8,128)} %bitcast.4, s32[7,32]{1,0:T(8,128)} %bitcast.5), custom_call_target="tpu_custom_call" | custom-call | tf_op jit(solution)/shard_map/pallas_call | solution.py:26
  8.6 13.9 %all-to-all-start = ((bf16[8,144,128]{2,1,0:T(8,128)(2,1)}), bf16[8,144,128]{2,1,0:T(8,128)(2,1)S(1)}, u32[]{:S(2)}, u32[]{:S(2)}) async-start(bf16[8,144,128]{2,1,0:T(8,128)(2,1)} %shard_map.76), calls=%async_computation | async-start | bytes 589824 | tf_op jit(solution)/shard_map/all_to_all | solution.py:228
  22.6 4.8 %collective-permute-start.2 = (bf16[512,512]{1,0:T(8,128)(2,1)S(1)}, bf16[512,512]{1,0:T(8,128)(2,1)S(1)}, u32[]{:S(2)}, u32[]{:S(2)}) collective-permute-start(bf16[512,512]{1,0:T(8,128)(2,1)S(1)} %shard_map.79.refs_0_), channel_id=1, source_target_pairs={{0,256},{256,0},{1,257},{257,1},{2,258},{258,2},{3,259},{259,3},{4... | collective-permute-start | bytes 1572872 | tf_op jit(solution)/shard_map/ppermute | solution.py:224
  27.5 3.4 %collective-permute-start.1 = (bf16[512,512]{1,0:T(8,128)(2,1)S(1)}, bf16[512,512]{1,0:T(8,128)(2,1)S(1)}, u32[]{:S(2)}, u32[]{:S(2)}) collective-permute-start(bf16[512,512]{1,0:T(8,128)(2,1)S(1)} %shard_map.79.refs_0_), channel_id=1, source_target_pairs={{0,8},{8,0},{1,9},{9,1},{2,10},{10,2},{3,11},{11,3},{4,12},{12,4},... | collective-permute-start | bytes 1572872 | tf_op jit(solution)/shard_map/ppermute | solution.py:224
  30.9 7.3 %collective-permute-done.2.refs_2_ = bf16[512,512]{1,0:T(8,128)(2,1)S(1)} collective-permute-done((bf16[512,512]{1,0:T(8,128)(2,1)S(1)}, bf16[512,512]{1,0:T(8,128)(2,1)S(1)}, u32[]{:S(2)}, u32[]{:S(2)}) %collective-permute-start.2) | collective-permute-done | bytes 524320 | tf_op jit(solution)/shard_map/ppermute | solution.py:224
  38.2 4.1 %collective-permute-start.3 = (bf16[512,512]{1,0:T(8,128)(2,1)S(1)}, bf16[512,512]{1,0:T(8,128)(2,1)S(1)}, u32[]{:S(2)}, u32[]{:S(2)}) collective-permute-start(bf16[512,512]{1,0:T(8,128)(2,1)S(1)} %collective-permute-done.2.refs_2_), channel_id=1, source_target_pairs={{0,8},{8,0},{1,9},{9,1},{2,10},{10,2},{3,11},{11,3},{4,12},{12,4},... | collective-permute-start | bytes 1572872 | tf_op jit(solution)/shard_map/ppermute | solution.py:224
  42.3 0.0 all-to-all-done.refs_0_
  42.3 0.0 collective-permute-done.1.refs_1_
  42.3 1.5 %collective-permute-done.3.refs_3_ = bf16[512,512]{1,0:T(8,128)(2,1)S(1)} collective-permute-done((bf16[512,512]{1,0:T(8,128)(2,1)S(1)}, bf16[512,512]{1,0:T(8,128)(2,1)S(1)}, u32[]{:S(2)}, u32[]{:S(2)}) %collective-permute-start.3) | collective-permute-done | bytes 524320 | tf_op jit(solution)/shard_map/ppermute | solution.py:224
  43.8 0.8 shard_map.80
  44.5 11.4 %all_to_all.25.came = f32[8,72,128]{2,1,0:T(8,128)S(1)} all-to-all(f32[8,72,128]{2,1,0:T(8,128)S(1)} %get-tuple-element.16), channel_id=1, replica_groups=mesh['yh'=2,'zh'=8,'zp'=2,'c'=2,'yl'=2,'x'=4] {'yl','x'}, dimensions={0} | all-to-all | bytes 589824 | tf_op jit(solution)/shard_map/all_to_all | solution.py:228
  56.0 8.9 %all_to_all.26.scores = f32[8,72,128]{2,1,0:T(8,128)S(1)} all-to-all(f32[8,72,128]{2,1,0:T(8,128)S(1)} %shard_map.81), channel_id=1, replica_groups=mesh['yh'=2,'zh'=8,'zp'=2,'c'=2,'yl'=2,'x'=4] {'yl','x'}, dimensions={0} | all-to-all | bytes 589824 | tf_op jit(solution)/shard_map/all_to_all | solution.py:228
  64.9 0.7 shard_map.82
  65.6 0.7 copy-done.2
  66.3 12.7 %all-to-all-start.3 = ((f32[16,8,128]{2,1,0:T(8,128)}), f32[16,8,128]{2,1,0:T(8,128)S(1)}, u32[]{:S(2)}, u32[]{:S(2)}) async-start(f32[16,8,128]{2,1,0:T(8,128)} %get-tuple-element.17), calls=%async_computation.3 | async-start | bytes 131072 | tf_op jit(solution)/shard_map/all_to_all | solution.py:228
  78.9 3.3 %collective-permute-start.5 = (bf16[8,144,128]{2,1,0:T(8,128)(2,1)S(1)}, bf16[8,144,128]{2,1,0:T(8,128)(2,1)S(1)}, u32[]{:S(2)}, u32[]{:S(2)}) collective-permute-start(bf16[8,144,128]{2,1,0:T(8,128)(2,1)S(1)} %shard_map.77.near), channel_id=1, source_target_pairs={{0,16},{16,0},{1,17},{17,1},{2,18},{18,2},{3,19},{19,3},{4,20},{20... | collective-permute-start | bytes 884744 | tf_op jit(solution)/shard_map/ppermute | solution.py:224
  82.2 2.0 %collective-permute-start.4 = (f32[4,72,128]{2,1,0:T(8,128)}, f32[4,72,128]{2,1,0:T(8,128)S(1)}, u32[]{:S(2)}, u32[]{:S(2)}) collective-permute-start(f32[4,72,128]{2,1,0:T(8,128)} %copy-done.2), channel_id=1, source_target_pairs={{0,16},{16,0},{1,17},{17,1},{2,18},{18,2},{3,19},{19,3},{4,20},{20... | collective-permute-start | bytes 442376 | tf_op jit(solution)/shard_map/ppermute | solution.py:224
  84.2 6.5 %all-to-all-done.3 = f32[16,8,128]{2,1,0:T(8,128)S(1)} async-done(((f32[16,8,128]{2,1,0:T(8,128)}), f32[16,8,128]{2,1,0:T(8,128)S(1)}, u32[]{:S(2)}, u32[]{:S(2)}) %all-to-all-start.3) | async-done | bytes 65568 | tf_op jit(solution)/shard_map/all_to_all | solution.py:228
  90.7 1.5 %shard_map.83 = (bf16[8,32,512]{2,1,0:T(8,128)(2,1)}, f32[8,256]{1,0:T(8,128)S(1)}) custom-call(f32[8,2,8,128]{3,2,1,0:T(8,128)S(1)} %bitcast.3, f32[8,72,128]{2,1,0:T(8,128)S(1)} %all_to_all.26.scores, s32[8,256]{1,0:T(8,128)S(1)} %get-tuple-element.18.asked, bf16[512,512]{1,0:T(8,128)(2,1)S(1)} %shard_map.79.refs_0_, ...), custom_call_target="tpu_custom_call" | custom-call | tf_op jit(solution)/shard_map/pallas_call | solution.py:26
  92.3 4.9 %all-to-all-start.4 = ((bf16[8,32,512]{2,1,0:T(8,128)(2,1)}), bf16[8,32,512]{2,1,0:T(8,128)(2,1)S(1)}, u32[]{:S(2)}, u32[]{:S(2)}) async-start(bf16[8,32,512]{2,1,0:T(8,128)(2,1)} %get-tuple-element.19), calls=%async_computation.4 | async-start | bytes 524288 | tf_op jit(solution)/shard_map/all_to_all | solution.py:228
  97.2 0.8 shard_map.85
  97.9 5.5 %collective-permute-start.6 = (bf16[2,256,512]{2,1,0:T(8,128)(2,1)S(1)}, bf16[2,256,512]{2,1,0:T(8,128)(2,1)S(1)}, u32[]{:S(2)}, u32[]{:S(2)}) collective-permute-start(bf16[2,256,512]{2,1,0:T(8,128)(2,1)S(1)} %get-tuple-element.24), channel_id=1, source_target_pairs={{0,8},{8,0},{1,9},{9,1},{2,10},{10,2},{3,11},{11,3},{4,12},{12,4},... | collective-permute-start | bytes 1572872 | tf_op jit(solution)/shard_map/ppermute | solution.py:224
  103.5 1.5 %collective-permute-done.6.came = bf16[2,256,512]{2,1,0:T(8,128)(2,1)S(1)} collective-permute-done((bf16[2,256,512]{2,1,0:T(8,128)(2,1)S(1)}, bf16[2,256,512]{2,1,0:T(8,128)(2,1)S(1)}, u32[]{:S(2)}, u32[]{:S(2)}) %collective-permute-start.6) | collective-permute-done | bytes 524320 | tf_op jit(solution)/shard_map/ppermute | solution.py:224
  105.0 0.1 shard_map.86
  105.1 4.5 %collective-permute-start.7 = (bf16[256,512]{1,0:T(8,128)(2,1)S(1)}, bf16[256,512]{1,0:T(8,128)(2,1)S(1)}, u32[]{:S(2)}, u32[]{:S(2)}) collective-permute-start(bf16[256,512]{1,0:T(8,128)(2,1)S(1)} %get-tuple-element.26), channel_id=1, source_target_pairs={{0,256},{256,0},{1,257},{257,1},{2,258},{258,2},{3,259},{259,3},{4... | collective-permute-start | bytes 786440 | tf_op jit(solution)/shard_map/ppermute | solution.py:224
  109.7 6.4 %collective-permute-done.7.came = bf16[256,512]{1,0:T(8,128)(2,1)S(1)} collective-permute-done((bf16[256,512]{1,0:T(8,128)(2,1)S(1)}, bf16[256,512]{1,0:T(8,128)(2,1)S(1)}, u32[]{:S(2)}, u32[]{:S(2)}) %collective-permute-start.7) | collective-permute-done | bytes 262176 | tf_op jit(solution)/shard_map/ppermute | solution.py:224
  116.0 0.7 shard_map.87
  116.8 0.7 shard_map.84
  (10 shorter events, 0.1 us)
Async XLA Ops:
  0.6 0.9 copy-start
  1.6 0.8 copy-start.1
  2.7 19.9 %collective-permute-start = (bf16[256,512]{1,0:T(8,128)(2,1)S(1)}, bf16[256,512]{1,0:T(8,128)(2,1)S(1)}, u32[]{:S(2)}, u32[]{:S(2)}) collective-permute-start(bf16[256,512]{1,0:T(8,128)(2,1)S(1)} %shard_map.78.first), channel_id=1, source_target_pairs={{0,16},{16,0},{1,17},{17,1},{2,18},{18,2},{3,19},{19,3},{4,20},{20... | collective-permute-start | bytes 786440 | tf_op jit(solution)/shard_map/ppermute | solution.py:224
  8.6 33.6 %all-to-all-start = ((bf16[8,144,128]{2,1,0:T(8,128)(2,1)}), bf16[8,144,128]{2,1,0:T(8,128)(2,1)S(1)}, u32[]{:S(2)}, u32[]{:S(2)}) async-start(bf16[8,144,128]{2,1,0:T(8,128)(2,1)} %shard_map.76), calls=%async_computation | async-start | bytes 589824 | tf_op jit(solution)/shard_map/all_to_all | solution.py:228
  22.6 15.6 %collective-permute-start.2 = (bf16[512,512]{1,0:T(8,128)(2,1)S(1)}, bf16[512,512]{1,0:T(8,128)(2,1)S(1)}, u32[]{:S(2)}, u32[]{:S(2)}) collective-permute-start(bf16[512,512]{1,0:T(8,128)(2,1)S(1)} %shard_map.79.refs_0_), channel_id=1, source_target_pairs={{0,256},{256,0},{1,257},{257,1},{2,258},{258,2},{3,259},{259,3},{4... | collective-permute-start | bytes 1572872 | tf_op jit(solution)/shard_map/ppermute | solution.py:224
  27.5 14.8 %collective-permute-start.1 = (bf16[512,512]{1,0:T(8,128)(2,1)S(1)}, bf16[512,512]{1,0:T(8,128)(2,1)S(1)}, u32[]{:S(2)}, u32[]{:S(2)}) collective-permute-start(bf16[512,512]{1,0:T(8,128)(2,1)S(1)} %shard_map.79.refs_0_), channel_id=1, source_target_pairs={{0,8},{8,0},{1,9},{9,1},{2,10},{10,2},{3,11},{11,3},{4,12},{12,4},... | collective-permute-start | bytes 1572872 | tf_op jit(solution)/shard_map/ppermute | solution.py:224
  38.2 5.6 %collective-permute-start.3 = (bf16[512,512]{1,0:T(8,128)(2,1)S(1)}, bf16[512,512]{1,0:T(8,128)(2,1)S(1)}, u32[]{:S(2)}, u32[]{:S(2)}) collective-permute-start(bf16[512,512]{1,0:T(8,128)(2,1)S(1)} %collective-permute-done.2.refs_2_), channel_id=1, source_target_pairs={{0,8},{8,0},{1,9},{9,1},{2,10},{10,2},{3,11},{11,3},{4,12},{12,4},... | collective-permute-start | bytes 1572872 | tf_op jit(solution)/shard_map/ppermute | solution.py:224
  65.6 0.7 copy-start.2
  66.3 24.5 %all-to-all-start.3 = ((f32[16,8,128]{2,1,0:T(8,128)}), f32[16,8,128]{2,1,0:T(8,128)S(1)}, u32[]{:S(2)}, u32[]{:S(2)}) async-start(f32[16,8,128]{2,1,0:T(8,128)} %get-tuple-element.17), calls=%async_computation.3 | async-start | bytes 131072 | tf_op jit(solution)/shard_map/all_to_all | solution.py:228
  78.9 18.2 %collective-permute-start.5 = (bf16[8,144,128]{2,1,0:T(8,128)(2,1)S(1)}, bf16[8,144,128]{2,1,0:T(8,128)(2,1)S(1)}, u32[]{:S(2)}, u32[]{:S(2)}) collective-permute-start(bf16[8,144,128]{2,1,0:T(8,128)(2,1)S(1)} %shard_map.77.near), channel_id=1, source_target_pairs={{0,16},{16,0},{1,17},{17,1},{2,18},{18,2},{3,19},{19,3},{4,20},{20... | collective-permute-start | bytes 884744 | tf_op jit(solution)/shard_map/ppermute | solution.py:224
  82.2 14.9 %collective-permute-start.4 = (f32[4,72,128]{2,1,0:T(8,128)}, f32[4,72,128]{2,1,0:T(8,128)S(1)}, u32[]{:S(2)}, u32[]{:S(2)}) collective-permute-start(f32[4,72,128]{2,1,0:T(8,128)} %copy-done.2), channel_id=1, source_target_pairs={{0,16},{16,0},{1,17},{17,1},{2,18},{18,2},{3,19},{19,3},{4,20},{20... | collective-permute-start | bytes 442376 | tf_op jit(solution)/shard_map/ppermute | solution.py:224
  92.3 24.5 %all-to-all-start.4 = ((bf16[8,32,512]{2,1,0:T(8,128)(2,1)}), bf16[8,32,512]{2,1,0:T(8,128)(2,1)S(1)}, u32[]{:S(2)}, u32[]{:S(2)}) async-start(bf16[8,32,512]{2,1,0:T(8,128)(2,1)} %get-tuple-element.19), calls=%async_computation.4 | async-start | bytes 524288 | tf_op jit(solution)/shard_map/all_to_all | solution.py:228
  97.9 7.1 %collective-permute-start.6 = (bf16[2,256,512]{2,1,0:T(8,128)(2,1)S(1)}, bf16[2,256,512]{2,1,0:T(8,128)(2,1)S(1)}, u32[]{:S(2)}, u32[]{:S(2)}) collective-permute-start(bf16[2,256,512]{2,1,0:T(8,128)(2,1)S(1)} %get-tuple-element.24), channel_id=1, source_target_pairs={{0,8},{8,0},{1,9},{9,1},{2,10},{10,2},{3,11},{11,3},{4,12},{12,4},... | collective-permute-start | bytes 1572872 | tf_op jit(solution)/shard_map/ppermute | solution.py:224
  105.1 10.9 %collective-permute-start.7 = (bf16[256,512]{1,0:T(8,128)(2,1)S(1)}, bf16[256,512]{1,0:T(8,128)(2,1)S(1)}, u32[]{:S(2)}, u32[]{:S(2)}) collective-permute-start(bf16[256,512]{1,0:T(8,128)(2,1)S(1)} %get-tuple-element.26), channel_id=1, source_target_pairs={{0,256},{256,0},{1,257},{257,1},{2,258},{258,2},{3,259},{259,3},{4... | collective-permute-start | bytes 786440 | tf_op jit(solution)/shard_map/ppermute | solution.py:224

commit v9 on v8

--- a/solution.py
+++ b/solution.py
@@ -120,7 +120,7 @@
         sent[i] = total
 
 
-def stat_kernel(scores, sent, cross):
+def stat_kernel(scores, far, sent, cross):
     cross[...] = scores[4:8]
     for l in range(2):
         batch = [scores[h * 2 + l, 0:64, :] for h in range(4)]
@@ -251,7 +251,7 @@
     far = swap(near, "zp")
     (summed,) = call(add_kernel, [((8, 72, 128), F32)], exchange(parts, ("yl", "x")))
     scores = exchange(summed, ("yl", "x"))
-    stats, cross = call(stat_kernel, [((NZ, 8, 128), F32), ((4, 72, 128), F32)], scores)
+    stats, cross = call(stat_kernel, [((NZ, 8, 128), F32), ((4, 72, 128), F32)], scores, far)
     stats = exchange(stats, ("zh", "zp")).reshape(NH, 2, 8, 128)
     far_scores = swap(cross, "zp")
     q_part, logs = call(

time: 119 us -> 120 us (level)
  blocking collectives: 20.3 us -> 0 us
  waiting for transfers between devices: 23.2 us -> 35.3 us
  starting transfers between devices: 63.5 us -> 71.4 us
  Pallas kernels: 7.26 us -> 8.67 us
    all_to_all x2 -> x0, blocking collectives: 20.3 us -> none  [exchange(): return lax.all_to_all(x, axes, split_axis=0, concat_axis=0, tiled=True)]
    all_to_all x3 -> x5, waiting for transfers between devices: 6.49 us -> 18.6 us  [exchange(): return lax.all_to_all(x, axes, split_axis=0, concat_axis=0, tiled=True)]
    all_to_all x3 -> x5, starting transfers between devices: 31.5 us -> 38.8 us  [exchange(): return lax.all_to_all(x, axes, split_axis=0, concat_axis=0, tiled=True)]
    pallas_call x11, Pallas kernels: 7.26 us -> 8.66 us  [call(): pl.pallas_call(kernel, out_shape=[jax.ShapeDtypeStruct(shape, dtype) for...]
  transfers between devices with their start and end apart: 11 -> 13, of which waited for: 5 -> 7; matrix products, arithmetic and copies ran while one was open for 0% -> 0% of each run, Pallas kernels for 4% -> 5%
where the time goes in v9:
time: 120 us; the launch traced here: 118 us
  starting transfers between devices  71.4 us (60%)
  waiting for transfers between devices  35.3 us (29%)
  Pallas kernels  8.67 us (7%)
  local copies, waits for them, and re-layouts  1.69 us (1%)
    all_to_all x5, starting transfers between devices, exchange(): return lax.all_to_all(x, axes, split_axis=0, concat_axis=0, tiled=True)  38.8 us
    ppermute x8, starting transfers between devices, swap(): return lax.ppermute(x, axis, [(0, 1), (1, 0)])  32.5 us
    all_to_all x5, waiting for transfers between devices, exchange(): return lax.all_to_all(x, axes, split_axis=0, concat_axis=0, tiled=True)  18.6 us
    ppermute x8, waiting for transfers between devices, swap(): return lax.ppermute(x, axis, [(0, 1), (1, 0)])  16.7 us
    pallas_call x11, Pallas kernels, call(): pl.pallas_call(kernel, out_shape=[jax.ShapeDtypeStruct(shape, dtype) for...  8.66 us
  transfers between devices with their start and end apart: 13, of which 7 were waited for; matrix products, arithmetic and copies ran while one was open for 0% of the time, Pallas kernels for 5%

profile of v9, /device:TPU:1, one launch (start us, length us, event | category | flops | bytes accessed | tf_op | source)
XLA Modules:
  0.0 117.9 jit_solution(184270433107661809)
XLA Ops:
  0.6 0.9 copy-done
  1.6 0.8 copy-done.1
  2.3 0.3 shard_map.78.first
  2.7 4.4 %collective-permute-start = (bf16[256,512]{1,0:T(8,128)(2,1)S(1)}, bf16[256,512]{1,0:T(8,128)(2,1)S(1)}, u32[]{:S(2)}, u32[]{:S(2)}) collective-permute-start(bf16[256,512]{1,0:T(8,128)(2,1)S(1)} %shard_map.78.first), channel_id=1, source_target_pairs={{0,16},{16,0},{1,17},{17,1},{2,18},{18,2},{3,19},{19,3},{4,20},{20... | collective-permute-start | bytes 786440 | tf_op jit(solution)/shard_map/ppermute | solution.py:224
  7.0 1.6 %shard_map.76 = bf16[8,144,128]{2,1,0:T(8,128)(2,1)} custom-call(bf16[32,512]{1,0:T(8,128)(2,1)} %queries.1, s32[7,32]{1,0:T(8,128)} %bitcast.4, s32[7,32]{1,0:T(8,128)} %bitcast.5), custom_call_target="tpu_custom_call" | custom-call | tf_op jit(solution)/shard_map/pallas_call | solution.py:26
  8.6 13.9 %all-to-all-start = ((bf16[8,144,128]{2,1,0:T(8,128)(2,1)}), bf16[8,144,128]{2,1,0:T(8,128)(2,1)S(1)}, u32[]{:S(2)}, u32[]{:S(2)}) async-start(bf16[8,144,128]{2,1,0:T(8,128)(2,1)} %shard_map.76), calls=%async_computation | async-start | bytes 589824 | tf_op jit(solution)/shard_map/all_to_all | solution.py:228
  22.6 4.8 %collective-permute-start.2 = (bf16[512,512]{1,0:T(8,128)(2,1)S(1)}, bf16[512,512]{1,0:T(8,128)(2,1)S(1)}, u32[]{:S(2)}, u32[]{:S(2)}) collective-permute-start(bf16[512,512]{1,0:T(8,128)(2,1)S(1)} %shard_map.79.refs_0_), channel_id=1, source_target_pairs={{0,256},{256,0},{1,257},{257,1},{2,258},{258,2},{3,259},{259,3},{4... | collective-permute-start | bytes 1572872 | tf_op jit(solution)/shard_map/ppermute | solution.py:224
  27.4 3.4 %collective-permute-start.1 = (bf16[512,512]{1,0:T(8,128)(2,1)S(1)}, bf16[512,512]{1,0:T(8,128)(2,1)S(1)}, u32[]{:S(2)}, u32[]{:S(2)}) collective-permute-start(bf16[512,512]{1,0:T(8,128)(2,1)S(1)} %shard_map.79.refs_0_), channel_id=1, source_target_pairs={{0,8},{8,0},{1,9},{9,1},{2,10},{10,2},{3,11},{11,3},{4,12},{12,4},... | collective-permute-start | bytes 1572872 | tf_op jit(solution)/shard_map/ppermute | solution.py:224
  30.9 7.3 %collective-permute-done.2.refs_2_ = bf16[512,512]{1,0:T(8,128)(2,1)S(1)} collective-permute-done((bf16[512,512]{1,0:T(8,128)(2,1)S(1)}, bf16[512,512]{1,0:T(8,128)(2,1)S(1)}, u32[]{:S(2)}, u32[]{:S(2)}) %collective-permute-start.2) | collective-permute-done | bytes 524320 | tf_op jit(solution)/shard_map/ppermute | solution.py:224
  38.2 4.1 %collective-permute-start.3 = (bf16[512,512]{1,0:T(8,128)(2,1)S(1)}, bf16[512,512]{1,0:T(8,128)(2,1)S(1)}, u32[]{:S(2)}, u32[]{:S(2)}) collective-permute-start(bf16[512,512]{1,0:T(8,128)(2,1)S(1)} %collective-permute-done.2.refs_2_), channel_id=1, source_target_pairs={{0,8},{8,0},{1,9},{9,1},{2,10},{10,2},{3,11},{11,3},{4,12},{12,4},... | collective-permute-start | bytes 1572872 | tf_op jit(solution)/shard_map/ppermute | solution.py:224
  42.3 1.5 %collective-permute-done.3.refs_3_ = bf16[512,512]{1,0:T(8,128)(2,1)S(1)} collective-permute-done((bf16[512,512]{1,0:T(8,128)(2,1)S(1)}, bf16[512,512]{1,0:T(8,128)(2,1)S(1)}, u32[]{:S(2)}, u32[]{:S(2)}) %collective-permute-start.3) | collective-permute-done | bytes 524320 | tf_op jit(solution)/shard_map/ppermute | solution.py:224
  43.8 1.5 %shard_map.80 = (f32[8,72,128]{2,1,0:T(8,128)}, bf16[256,512]{1,0:T(8,128)(2,1)S(1)}, s32[8,256]{1,0:T(8,128)S(1)}) custom-call(bf16[8,144,128]{2,1,0:T(8,128)(2,1)S(1)} %shard_map.77.near, bf16[512,512]{1,0:T(8,128)(2,1)S(1)} %shard_map.79.refs_0_, bf16[512,512]{1,0:T(8,128)(2,1)S(1)} %collective-permute-done.1.refs_1_, ...), custom_call_target="tpu_custom_call" | custom-call | tf_op jit(solution)/shard_map/pallas_call | solution.py:26
  45.2 5.0 %all-to-all-start.1 = ((f32[8,72,128]{2,1,0:T(8,128)}), f32[8,72,128]{2,1,0:T(8,128)S(1)}, u32[]{:S(2)}, u32[]{:S(2)}) async-start(f32[8,72,128]{2,1,0:T(8,128)} %get-tuple-element.16), calls=%async_computation.1 | async-start | bytes 589824 | tf_op jit(solution)/shard_map/all_to_all | solution.py:228
  50.3 2.6 %collective-permute-start.4 = (bf16[8,144,128]{2,1,0:T(8,128)(2,1)S(1)}, bf16[8,144,128]{2,1,0:T(8,128)(2,1)S(1)}, u32[]{:S(2)}, u32[]{:S(2)}) collective-permute-start(bf16[8,144,128]{2,1,0:T(8,128)(2,1)S(1)} %shard_map.77.near), channel_id=1, source_target_pairs={{0,16},{16,0},{1,17},{17,1},{2,18},{18,2},{3,19},{19,3},{4,20},{20... | collective-permute-start | bytes 884744 | tf_op jit(solution)/shard_map/ppermute | solution.py:224
  52.9 3.8 %all-to-all-done.1.came = f32[8,72,128]{2,1,0:T(8,128)S(1)} async-done(((f32[8,72,128]{2,1,0:T(8,128)}), f32[8,72,128]{2,1,0:T(8,128)S(1)}, u32[]{:S(2)}, u32[]{:S(2)}) %all-to-all-start.1) | async-done | bytes 294944 | tf_op jit(solution)/shard_map/all_to_all | solution.py:228
  56.7 0.7 shard_map.81
  57.4 3.4 %all-to-all-start.2 = ((f32[8,72,128]{2,1,0:T(8,128)}), f32[8,72,128]{2,1,0:T(8,128)S(1)}, u32[]{:S(2)}, u32[]{:S(2)}) async-start(f32[8,72,128]{2,1,0:T(8,128)} %shard_map.81), calls=%async_computation.2 | async-start | bytes 589824 | tf_op jit(solution)/shard_map/all_to_all | solution.py:228
  60.9 6.3 %all-to-all-done.2.scores = f32[8,72,128]{2,1,0:T(8,128)S(1)} async-done(((f32[8,72,128]{2,1,0:T(8,128)}), f32[8,72,128]{2,1,0:T(8,128)S(1)}, u32[]{:S(2)}, u32[]{:S(2)}) %all-to-all-start.2) | async-done | bytes 294944 | tf_op jit(solution)/shard_map/all_to_all | solution.py:228
  67.2 0.7 shard_map.82
  67.9 13.1 %all-to-all-start.3 = ((f32[16,8,128]{2,1,0:T(8,128)}), f32[16,8,128]{2,1,0:T(8,128)S(1)}, u32[]{:S(2)}, u32[]{:S(2)}) async-start(f32[16,8,128]{2,1,0:T(8,128)} %get-tuple-element.17), calls=%async_computation.3 | async-start | bytes 131072 | tf_op jit(solution)/shard_map/all_to_all | solution.py:228
  81.0 3.3 %collective-permute-start.5 = (f32[4,72,128]{2,1,0:T(8,128)S(1)}, f32[4,72,128]{2,1,0:T(8,128)S(1)}, u32[]{:S(2)}, u32[]{:S(2)}) collective-permute-start(f32[4,72,128]{2,1,0:T(8,128)S(1)} %get-tuple-element.22), channel_id=1, source_target_pairs={{0,16},{16,0},{1,17},{17,1},{2,18},{18,2},{3,19},{19,3},{4,20},{20... | collective-permute-start | bytes 442376 | tf_op jit(solution)/shard_map/ppermute | solution.py:224
  84.3 8.5 %all-to-all-done.3 = f32[16,8,128]{2,1,0:T(8,128)S(1)} async-done(((f32[16,8,128]{2,1,0:T(8,128)}), f32[16,8,128]{2,1,0:T(8,128)S(1)}, u32[]{:S(2)}, u32[]{:S(2)}) %all-to-all-start.3) | async-done | bytes 65568 | tf_op jit(solution)/shard_map/all_to_all | solution.py:228
  92.7 1.5 %shard_map.83 = (bf16[8,32,512]{2,1,0:T(8,128)(2,1)}, f32[8,256]{1,0:T(8,128)S(1)}) custom-call(f32[8,2,8,128]{3,2,1,0:T(8,128)S(1)} %bitcast.3, f32[8,72,128]{2,1,0:T(8,128)S(1)} %all-to-all-done.2.scores, s32[8,256]{1,0:T(8,128)S(1)} %get-tuple-element.18.asked, bf16[512,512]{1,0:T(8,128)(2,1)S(1)} %shard_map.79.refs_0_, ...), custom_call_target="tpu_custom_call" | custom-call | tf_op jit(solution)/shard_map/pallas_call | solution.py:26
  94.3 3.4 %all-to-all-start.4 = ((bf16[8,32,512]{2,1,0:T(8,128)(2,1)}), bf16[8,32,512]{2,1,0:T(8,128)(2,1)S(1)}, u32[]{:S(2)}, u32[]{:S(2)}) async-start(bf16[8,32,512]{2,1,0:T(8,128)(2,1)} %get-tuple-element.19), calls=%async_computation.4 | async-start | bytes 524288 | tf_op jit(solution)/shard_map/all_to_all | solution.py:228
  97.7 0.8 shard_map.85
  98.5 5.4 %collective-permute-start.6 = (bf16[2,256,512]{2,1,0:T(8,128)(2,1)S(1)}, bf16[2,256,512]{2,1,0:T(8,128)(2,1)S(1)}, u32[]{:S(2)}, u32[]{:S(2)}) collective-permute-start(bf16[2,256,512]{2,1,0:T(8,128)(2,1)S(1)} %get-tuple-element.24), channel_id=1, source_target_pairs={{0,8},{8,0},{1,9},{9,1},{2,10},{10,2},{3,11},{11,3},{4,12},{12,4},... | collective-permute-start | bytes 1572872 | tf_op jit(solution)/shard_map/ppermute | solution.py:224
  103.9 1.5 %collective-permute-done.6.came = bf16[2,256,512]{2,1,0:T(8,128)(2,1)S(1)} collective-permute-done((bf16[2,256,512]{2,1,0:T(8,128)(2,1)S(1)}, bf16[2,256,512]{2,1,0:T(8,128)(2,1)S(1)}, u32[]{:S(2)}, u32[]{:S(2)}) %collective-permute-start.6) | collective-permute-done | bytes 524320 | tf_op jit(solution)/shard_map/ppermute | solution.py:224
  105.4 0.1 shard_map.86
  105.5 4.5 %collective-permute-start.7 = (bf16[256,512]{1,0:T(8,128)(2,1)S(1)}, bf16[256,512]{1,0:T(8,128)(2,1)S(1)}, u32[]{:S(2)}, u32[]{:S(2)}) collective-permute-start(bf16[256,512]{1,0:T(8,128)(2,1)S(1)} %get-tuple-element.26), channel_id=1, source_target_pairs={{0,256},{256,0},{1,257},{257,1},{2,258},{258,2},{3,259},{259,3},{4... | collective-permute-start | bytes 786440 | tf_op jit(solution)/shard_map/ppermute | solution.py:224
  110.1 6.4 %collective-permute-done.7.came = bf16[256,512]{1,0:T(8,128)(2,1)S(1)} collective-permute-done((bf16[256,512]{1,0:T(8,128)(2,1)S(1)}, bf16[256,512]{1,0:T(8,128)(2,1)S(1)}, u32[]{:S(2)}, u32[]{:S(2)}) %collective-permute-start.7) | collective-permute-done | bytes 262176 | tf_op jit(solution)/shard_map/ppermute | solution.py:224
  116.5 0.7 shard_map.87
  117.2 0.7 shard_map.84
  (10 shorter events, 0.1 us)
Async XLA Ops:
  0.6 0.9 copy-start
  1.6 0.8 copy-start.1
  2.7 19.9 %collective-permute-start = (bf16[256,512]{1,0:T(8,128)(2,1)S(1)}, bf16[256,512]{1,0:T(8,128)(2,1)S(1)}, u32[]{:S(2)}, u32[]{:S(2)}) collective-permute-start(bf16[256,512]{1,0:T(8,128)(2,1)S(1)} %shard_map.78.first), channel_id=1, source_target_pairs={{0,16},{16,0},{1,17},{17,1},{2,18},{18,2},{3,19},{19,3},{4,20},{20... | collective-permute-start | bytes 786440 | tf_op jit(solution)/shard_map/ppermute | solution.py:224
  8.6 33.6 %all-to-all-start = ((bf16[8,144,128]{2,1,0:T(8,128)(2,1)}), bf16[8,144,128]{2,1,0:T(8,128)(2,1)S(1)}, u32[]{:S(2)}, u32[]{:S(2)}) async-start(bf16[8,144,128]{2,1,0:T(8,128)(2,1)} %shard_map.76), calls=%async_computation | async-start | bytes 589824 | tf_op jit(solution)/shard_map/all_to_all | solution.py:228
  22.6 15.6 %collective-permute-start.2 = (bf16[512,512]{1,0:T(8,128)(2,1)S(1)}, bf16[512,512]{1,0:T(8,128)(2,1)S(1)}, u32[]{:S(2)}, u32[]{:S(2)}) collective-permute-start(bf16[512,512]{1,0:T(8,128)(2,1)S(1)} %shard_map.79.refs_0_), channel_id=1, source_target_pairs={{0,256},{256,0},{1,257},{257,1},{2,258},{258,2},{3,259},{259,3},{4... | collective-permute-start | bytes 1572872 | tf_op jit(solution)/shard_map/ppermute | solution.py:224
  27.4 14.8 %collective-permute-start.1 = (bf16[512,512]{1,0:T(8,128)(2,1)S(1)}, bf16[512,512]{1,0:T(8,128)(2,1)S(1)}, u32[]{:S(2)}, u32[]{:S(2)}) collective-permute-start(bf16[512,512]{1,0:T(8,128)(2,1)S(1)} %shard_map.79.refs_0_), channel_id=1, source_target_pairs={{0,8},{8,0},{1,9},{9,1},{2,10},{10,2},{3,11},{11,3},{4,12},{12,4},... | collective-permute-start | bytes 1572872 | tf_op jit(solution)/shard_map/ppermute | solution.py:224
  38.2 5.6 %collective-permute-start.3 = (bf16[512,512]{1,0:T(8,128)(2,1)S(1)}, bf16[512,512]{1,0:T(8,128)(2,1)S(1)}, u32[]{:S(2)}, u32[]{:S(2)}) collective-permute-start(bf16[512,512]{1,0:T(8,128)(2,1)S(1)} %collective-permute-done.2.refs_2_), channel_id=1, source_target_pairs={{0,8},{8,0},{1,9},{9,1},{2,10},{10,2},{3,11},{11,3},{4,12},{12,4},... | collective-permute-start | bytes 1572872 | tf_op jit(solution)/shard_map/ppermute | solution.py:224
  45.2 11.5 %all-to-all-start.1 = ((f32[8,72,128]{2,1,0:T(8,128)}), f32[8,72,128]{2,1,0:T(8,128)S(1)}, u32[]{:S(2)}, u32[]{:S(2)}) async-start(f32[8,72,128]{2,1,0:T(8,128)} %get-tuple-element.16), calls=%async_computation.1 | async-start | bytes 589824 | tf_op jit(solution)/shard_map/all_to_all | solution.py:228
  50.3 10.6 %collective-permute-start.4 = (bf16[8,144,128]{2,1,0:T(8,128)(2,1)S(1)}, bf16[8,144,128]{2,1,0:T(8,128)(2,1)S(1)}, u32[]{:S(2)}, u32[]{:S(2)}) collective-permute-start(bf16[8,144,128]{2,1,0:T(8,128)(2,1)S(1)} %shard_map.77.near), channel_id=1, source_target_pairs={{0,16},{16,0},{1,17},{17,1},{2,18},{18,2},{3,19},{19,3},{4,20},{20... | collective-permute-start | bytes 884744 | tf_op jit(solution)/shard_map/ppermute | solution.py:224
  57.4 9.8 %all-to-all-start.2 = ((f32[8,72,128]{2,1,0:T(8,128)}), f32[8,72,128]{2,1,0:T(8,128)S(1)}, u32[]{:S(2)}, u32[]{:S(2)}) async-start(f32[8,72,128]{2,1,0:T(8,128)} %shard_map.81), calls=%async_computation.2 | async-start | bytes 589824 | tf_op jit(solution)/shard_map/all_to_all | solution.py:228
  67.9 24.8 %all-to-all-start.3 = ((f32[16,8,128]{2,1,0:T(8,128)}), f32[16,8,128]{2,1,0:T(8,128)S(1)}, u32[]{:S(2)}, u32[]{:S(2)}) async-start(f32[16,8,128]{2,1,0:T(8,128)} %get-tuple-element.17), calls=%async_computation.3 | async-start | bytes 131072 | tf_op jit(solution)/shard_map/all_to_all | solution.py:228
  81.0 16.7 %collective-permute-start.5 = (f32[4,72,128]{2,1,0:T(8,128)S(1)}, f32[4,72,128]{2,1,0:T(8,128)S(1)}, u32[]{:S(2)}, u32[]{:S(2)}) collective-permute-start(f32[4,72,128]{2,1,0:T(8,128)S(1)} %get-tuple-element.22), channel_id=1, source_target_pairs={{0,16},{16,0},{1,17},{17,1},{2,18},{18,2},{3,19},{19,3},{4,20},{20... | collective-permute-start | bytes 442376 | tf_op jit(solution)/shard_map/ppermute | solution.py:224
  94.3 22.9 %all-to-all-start.4 = ((bf16[8,32,512]{2,1,0:T(8,128)(2,1)}), bf16[8,32,512]{2,1,0:T(8,128)(2,1)S(1)}, u32[]{:S(2)}, u32[]{:S(2)}) async-start(bf16[8,32,512]{2,1,0:T(8,128)(2,1)} %get-tuple-element.19), calls=%async_computation.4 | async-start | bytes 524288 | tf_op jit(solution)/shard_map/all_to_all | solution.py:228
  98.5 7.0 %collective-permute-start.6 = (bf16[2,256,512]{2,1,0:T(8,128)(2,1)S(1)}, bf16[2,256,512]{2,1,0:T(8,128)(2,1)S(1)}, u32[]{:S(2)}, u32[]{:S(2)}) collective-permute-start(bf16[2,256,512]{2,1,0:T(8,128)(2,1)S(1)} %get-tuple-element.24), channel_id=1, source_target_pairs={{0,8},{8,0},{1,9},{9,1},{2,10},{10,2},{3,11},{11,3},{4,12},{12,4},... | collective-permute-start | bytes 1572872 | tf_op jit(solution)/shard_map/ppermute | solution.py:224
  105.5 10.9 %collective-permute-start.7 = (bf16[256,512]{1,0:T(8,128)(2,1)S(1)}, bf16[256,512]{1,0:T(8,128)(2,1)S(1)}, u32[]{:S(2)}, u32[]{:S(2)}) collective-permute-start(bf16[256,512]{1,0:T(8,128)(2,1)S(1)} %get-tuple-element.26), channel_id=1, source_target_pairs={{0,256},{256,0},{1,257},{257,1},{2,258},{258,2},{3,259},{259,3},{4... | collective-permute-start | bytes 786440 | tf_op jit(solution)/shard_map/ppermute | solution.py:224

commit v10 on v8

--- a/solution.py
+++ b/solution.py
@@ -17,10 +17,10 @@
 ABSENT = -1e30
 VMEM_LIMIT = 48 * 1024 * 1024
 PACK_LIMIT = 62 * 1024 * 1024
-HOLD_FLOPS = 1153000000
-
-
-def call(kernel, out_shapes, *args, hbm=0, scratch=(), limit=VMEM_LIMIT):
+STACK_COST = pl.CostEstimate(flops=5765000000, bytes_accessed=0, transcendentals=0)
+
+
+def call(kernel, out_shapes, *args, hbm=0, scratch=(), limit=VMEM_LIMIT, cost=None):
     specs = [pl.BlockSpec(memory_space=pl.ANY)] * hbm
     specs += [pl.BlockSpec(memory_space=pltpu.VMEM)] * (len(args) - hbm)
     return pl.pallas_call(
@@ -30,6 +30,7 @@
         out_specs=[pl.BlockSpec(memory_space=pltpu.VMEM)] * len(out_shapes),
         scratch_shapes=list(scratch),
         compiler_params=pltpu.CompilerParams(vmem_limit_bytes=limit),
+        cost_estimate=cost,
     )(*args)
 
 
@@ -112,7 +113,7 @@
                 parts[h * 2 + l, 66:72, :] = jnp.zeros((6, 128), F32)
 
 
-def add_kernel(came, sent):
+def add_kernel(came, far, sent):
     total = came[0]
     for i in range(1, 8):
         total = total + came[i]
@@ -208,18 +209,6 @@
     query_out[...] = total.astype(BF16)
 
 
-def hold(x):
-    return pl.pallas_call(
-        lambda *refs: None,
-        out_shape=jax.ShapeDtypeStruct(x.shape, x.dtype),
-        in_specs=[pl.BlockSpec(memory_space=pltpu.VMEM)],
-        out_specs=pl.BlockSpec(memory_space=pltpu.VMEM),
-        input_output_aliases={0: 0},
-        cost_estimate=pl.CostEstimate(flops=HOLD_FLOPS, bytes_accessed=0, transcendentals=0),
-        compiler_params=pltpu.CompilerParams(vmem_limit_bytes=VMEM_LIMIT),
-    )(x)
-
-
 def swap(x, axis):
     return lax.ppermute(x, axis, [(0, 1), (1, 0)])
 
@@ -241,15 +230,16 @@
         column_pack_kernel, [((256, 512), BF16)], passages, negatives, hbm=2,
         scratch=[pltpu.SemaphoreType.DMA((2,))],
     )
-    (pair,) = call(stack_kernel, [((512, 512), BF16)], col0, swap(col0, "zp"))
-    near = hold(exchange(sent, "zh"))
-    other = swap(pair, "yh")
+    by_yh, by_zp = swap(col0, "yh"), swap(col0, "zp")
+    near = exchange(sent, "zh")
+    (pair,) = call(stack_kernel, [((512, 512), BF16)], col0, by_zp, cost=STACK_COST)
+    (other,) = call(stack_kernel, [((512, 512), BF16)], by_yh, swap(by_zp, "yh"), cost=STACK_COST)
     columns = (pair, swap(pair, "c"), other, swap(other, "c"))
     parts, queries, asked = call(
         score_kernel, [((8, 72, 128), F32), ((ROWS, 512), BF16), ((NB, ROWS), jnp.int32)], near, *columns
     )
     far = swap(near, "zp")
-    (summed,) = call(add_kernel, [((8, 72, 128), F32)], exchange(parts, ("yl", "x")))
+    (summed,) = call(add_kernel, [((8, 72, 128), F32)], exchange(parts, ("yl", "x")), far)
     scores = exchange(summed, ("yl", "x"))
     stats, cross = call(stat_kernel, [((NZ, 8, 128), F32), ((4, 72, 128), F32)], scores)
     stats = exchange(stats, ("zh", "zp")).reshape(NH, 2, 8, 128)

time: 119 us -> 116 us (0.975)
  starting transfers between devices: 63.5 us -> 62 us
    all_to_all x3, starting transfers between devices: 31.5 us -> 26.6 us  [exchange(): return lax.all_to_all(x, axes, split_axis=0, concat_axis=0, tiled=True)]
    all_to_all x3, waiting for transfers between devices: 6.49 us -> 11 us  [exchange(): return lax.all_to_all(x, axes, split_axis=0, concat_axis=0, tiled=True)]
    ppermute x8 -> x9, waiting for transfers between devices: 16.7 us -> 12.9 us  [swap(): return lax.ppermute(x, axis, [(0, 1), (1, 0)])]
    ppermute x8 -> x9, starting transfers between devices: 32 us -> 35.4 us  [swap(): return lax.ppermute(x, axis, [(0, 1), (1, 0)])]
    pallas_call x11 -> x12, Pallas kernels: 7.26 us -> 7.3 us  [call(): pl.pallas_call(kernel, out_shape=[jax.ShapeDtypeStruct(shape, dtype) for...]
  transfers between devices with their start and end apart: 11 -> 12, of which waited for: 5 -> 5; matrix products, arithmetic and copies ran while one was open for 0% -> 0% of each run, Pallas kernels for 4% -> 5%
where the time goes in v10:
time: 116 us; the launch traced here: 115 us
  starting transfers between devices  62 us (53%)
  waiting for transfers between devices  23.9 us (21%)
  blocking collectives  19.3 us (17%)
  Pallas kernels  7.3 us (6%)
  local copies, waits for them, and re-layouts  1.69 us (1%)
    ppermute x9, starting transfers between devices, swap(): return lax.ppermute(x, axis, [(0, 1), (1, 0)])  35.4 us
    all_to_all x3, starting transfers between devices, exchange(): return lax.all_to_all(x, axes, split_axis=0, concat_axis=0, tiled=True)  26.6 us
    all_to_all x2, blocking collectives, exchange(): return lax.all_to_all(x, axes, split_axis=0, concat_axis=0, tiled=True)  19.3 us
    ppermute x9, waiting for transfers between devices, swap(): return lax.ppermute(x, axis, [(0, 1), (1, 0)])  12.9 us
    all_to_all x3, waiting for transfers between devices, exchange(): return lax.all_to_all(x, axes, split_axis=0, concat_axis=0, tiled=True)  11 us
    pallas_call x12, Pallas kernels, call(): pl.pallas_call(kernel, out_shape=[jax.ShapeDtypeStruct(shape, dtype) for...  7.3 us
  transfers between devices with their start and end apart: 12, of which 5 were waited for; matrix products, arithmetic and copies ran while one was open for 0% of the time, Pallas kernels for 5%

profile of v10, /device:TPU:1, one launch (start us, length us, event | category | flops | bytes accessed | tf_op | source)
XLA Modules:
  0.0 115.1 jit_solution(8623036551669513190)
XLA Ops:
  0.6 0.9 copy-done
  1.6 0.8 copy-done.1
  2.3 0.3 shard_map.77.first
  2.7 4.4 %collective-permute-start = (bf16[256,512]{1,0:T(8,128)(2,1)S(1)}, bf16[256,512]{1,0:T(8,128)(2,1)S(1)}, u32[]{:S(2)}, u32[]{:S(2)}) collective-permute-start(bf16[256,512]{1,0:T(8,128)(2,1)S(1)} %shard_map.77.first), channel_id=1, source_target_pairs={{0,16},{16,0},{1,17},{17,1},{2,18},{18,2},{3,19},{19,3},{4,20},{20... | collective-permute-start | bytes 786440 | tf_op jit(solution)/shard_map/ppermute | solution.py:213
  7.0 4.8 %collective-permute-start.2 = (bf16[256,512]{1,0:T(8,128)(2,1)S(1)}, bf16[256,512]{1,0:T(8,128)(2,1)S(1)}, u32[]{:S(2)}, u32[]{:S(2)}) collective-permute-start(bf16[256,512]{1,0:T(8,128)(2,1)S(1)} %shard_map.77.first), channel_id=1, source_target_pairs={{0,256},{256,0},{1,257},{257,1},{2,258},{258,2},{3,259},{259,3},{4... | collective-permute-start | bytes 786440 | tf_op jit(solution)/shard_map/ppermute | solution.py:213
  11.9 1.6 %shard_map.76 = bf16[8,144,128]{2,1,0:T(8,128)(2,1)} custom-call(bf16[32,512]{1,0:T(8,128)(2,1)} %queries.1, s32[7,32]{1,0:T(8,128)} %bitcast.4, s32[7,32]{1,0:T(8,128)} %bitcast.5), custom_call_target="tpu_custom_call" | custom-call | tf_op jit(solution)/shard_map/pallas_call | solution.py:26
  13.5 13.9 %all-to-all-start = ((bf16[8,144,128]{2,1,0:T(8,128)(2,1)}), bf16[8,144,128]{2,1,0:T(8,128)(2,1)S(1)}, u32[]{:S(2)}, u32[]{:S(2)}) async-start(bf16[8,144,128]{2,1,0:T(8,128)(2,1)} %shard_map.76), calls=%async_computation | async-start | bytes 589824 | tf_op jit(solution)/shard_map/all_to_all | solution.py:217
  27.4 0.0 collective-permute-done.second
  27.4 2.0 %collective-permute-start.3 = (bf16[256,512]{1,0:T(8,128)(2,1)S(1)}, bf16[256,512]{1,0:T(8,128)(2,1)S(1)}, u32[]{:S(2)}, u32[]{:S(2)}) collective-permute-start(bf16[256,512]{1,0:T(8,128)(2,1)S(1)} %collective-permute-done.second), channel_id=1, source_target_pairs={{0,256},{256,0},{1,257},{257,1},{2,258},{258,2},{3,259},{259,3},{4... | collective-permute-start | bytes 786440 | tf_op jit(solution)/shard_map/ppermute | solution.py:213
  29.4 3.7 %collective-permute-start.1 = (bf16[512,512]{1,0:T(8,128)(2,1)S(1)}, bf16[512,512]{1,0:T(8,128)(2,1)S(1)}, u32[]{:S(2)}, u32[]{:S(2)}) collective-permute-start(bf16[512,512]{1,0:T(8,128)(2,1)S(1)} %shard_map.78.refs_0_), channel_id=1, source_target_pairs={{0,8},{8,0},{1,9},{9,1},{2,10},{10,2},{3,11},{11,3},{4,12},{12,4},... | collective-permute-start | bytes 1572872 | tf_op jit(solution)/shard_map/ppermute | solution.py:213
  33.1 0.0 collective-permute-done.2.first
  33.1 3.9 %collective-permute-done.3.second = bf16[256,512]{1,0:T(8,128)(2,1)S(1)} collective-permute-done((bf16[256,512]{1,0:T(8,128)(2,1)S(1)}, bf16[256,512]{1,0:T(8,128)(2,1)S(1)}, u32[]{:S(2)}, u32[]{:S(2)}) %collective-permute-start.3) | collective-permute-done | bytes 262176 | tf_op jit(solution)/shard_map/ppermute | solution.py:213
  37.1 4.3 %collective-permute-start.4 = (bf16[512,512]{1,0:T(8,128)(2,1)S(1)}, bf16[512,512]{1,0:T(8,128)(2,1)S(1)}, u32[]{:S(2)}, u32[]{:S(2)}) collective-permute-start(bf16[512,512]{1,0:T(8,128)(2,1)S(1)} %shard_map.79.refs_2_), channel_id=1, source_target_pairs={{0,8},{8,0},{1,9},{9,1},{2,10},{10,2},{3,11},{11,3},{4,12},{12,4},... | collective-permute-start | bytes 1572872 | tf_op jit(solution)/shard_map/ppermute | solution.py:213
  41.5 2.5 %all-to-all-done.near = bf16[8,144,128]{2,1,0:T(8,128)(2,1)S(1)} async-done(((bf16[8,144,128]{2,1,0:T(8,128)(2,1)}), bf16[8,144,128]{2,1,0:T(8,128)(2,1)S(1)}, u32[]{:S(2)}, u32[]{:S(2)}) %all-to-all-start) | async-done | bytes 294944 | tf_op jit(solution)/shard_map/all_to_all | solution.py:217
  44.0 2.7 %collective-permute-start.5 = (bf16[8,144,128]{2,1,0:T(8,128)(2,1)S(1)}, bf16[8,144,128]{2,1,0:T(8,128)(2,1)S(1)}, u32[]{:S(2)}, u32[]{:S(2)}) collective-permute-start(bf16[8,144,128]{2,1,0:T(8,128)(2,1)S(1)} %all-to-all-done.near), channel_id=1, source_target_pairs={{0,16},{16,0},{1,17},{17,1},{2,18},{18,2},{3,19},{19,3},{4,20},{20... | collective-permute-start | bytes 884744 | tf_op jit(solution)/shard_map/ppermute | solution.py:213
  46.7 0.8 shard_map.80
  47.4 10.4 %all_to_all.25.came = f32[8,72,128]{2,1,0:T(8,128)S(1)} all-to-all(f32[8,72,128]{2,1,0:T(8,128)S(1)} %get-tuple-element.16), channel_id=1, replica_groups=mesh['yh'=2,'zh'=8,'zp'=2,'c'=2,'yl'=2,'x'=4] {'yl','x'}, dimensions={0} | all-to-all | bytes 589824 | tf_op jit(solution)/shard_map/all_to_all | solution.py:217
  57.9 8.9 %all_to_all.26.scores = f32[8,72,128]{2,1,0:T(8,128)S(1)} all-to-all(f32[8,72,128]{2,1,0:T(8,128)S(1)} %shard_map.81), channel_id=1, replica_groups=mesh['yh'=2,'zh'=8,'zp'=2,'c'=2,'yl'=2,'x'=4] {'yl','x'}, dimensions={0} | all-to-all | bytes 589824 | tf_op jit(solution)/shard_map/all_to_all | solution.py:217
  66.8 0.7 shard_map.82
  67.5 9.2 %all-to-all-start.3 = ((f32[16,8,128]{2,1,0:T(8,128)}), f32[16,8,128]{2,1,0:T(8,128)S(1)}, u32[]{:S(2)}, u32[]{:S(2)}) async-start(f32[16,8,128]{2,1,0:T(8,128)} %get-tuple-element.17), calls=%async_computation.3 | async-start | bytes 131072 | tf_op jit(solution)/shard_map/all_to_all | solution.py:217
  76.8 3.3 %collective-permute-start.6 = (f32[4,72,128]{2,1,0:T(8,128)S(1)}, f32[4,72,128]{2,1,0:T(8,128)S(1)}, u32[]{:S(2)}, u32[]{:S(2)}) collective-permute-start(f32[4,72,128]{2,1,0:T(8,128)S(1)} %get-tuple-element.22), channel_id=1, source_target_pairs={{0,16},{16,0},{1,17},{17,1},{2,18},{18,2},{3,19},{19,3},{4,20},{20... | collective-permute-start | bytes 442376 | tf_op jit(solution)/shard_map/ppermute | solution.py:213
  80.1 8.5 %all-to-all-done.3 = f32[16,8,128]{2,1,0:T(8,128)S(1)} async-done(((f32[16,8,128]{2,1,0:T(8,128)}), f32[16,8,128]{2,1,0:T(8,128)S(1)}, u32[]{:S(2)}, u32[]{:S(2)}) %all-to-all-start.3) | async-done | bytes 65568 | tf_op jit(solution)/shard_map/all_to_all | solution.py:217
  88.6 1.5 %shard_map.83 = (bf16[8,32,512]{2,1,0:T(8,128)(2,1)}, f32[8,256]{1,0:T(8,128)S(1)}) custom-call(f32[8,2,8,128]{3,2,1,0:T(8,128)S(1)} %bitcast.3, f32[8,72,128]{2,1,0:T(8,128)S(1)} %all_to_all.26.scores, s32[8,256]{1,0:T(8,128)S(1)} %get-tuple-element.18.asked, bf16[512,512]{1,0:T(8,128)(2,1)S(1)} %shard_map.78.refs_0_, ...), custom_call_target="tpu_custom_call" | custom-call | tf_op jit(solution)/shard_map/pallas_call | solution.py:26
  90.1 3.4 %all-to-all-start.4 = ((bf16[8,32,512]{2,1,0:T(8,128)(2,1)}), bf16[8,32,512]{2,1,0:T(8,128)(2,1)S(1)}, u32[]{:S(2)}, u32[]{:S(2)}) async-start(bf16[8,32,512]{2,1,0:T(8,128)(2,1)} %get-tuple-element.19), calls=%async_computation.4 | async-start | bytes 524288 | tf_op jit(solution)/shard_map/all_to_all | solution.py:217
  93.5 0.8 shard_map.85
  94.3 6.8 %collective-permute-start.7 = (bf16[2,256,512]{2,1,0:T(8,128)(2,1)S(1)}, bf16[2,256,512]{2,1,0:T(8,128)(2,1)S(1)}, u32[]{:S(2)}, u32[]{:S(2)}) collective-permute-start(bf16[2,256,512]{2,1,0:T(8,128)(2,1)S(1)} %get-tuple-element.24), channel_id=1, source_target_pairs={{0,8},{8,0},{1,9},{9,1},{2,10},{10,2},{3,11},{11,3},{4,12},{12,4},... | collective-permute-start | bytes 1572872 | tf_op jit(solution)/shard_map/ppermute | solution.py:213
  101.1 1.5 %collective-permute-done.7.came = bf16[2,256,512]{2,1,0:T(8,128)(2,1)S(1)} collective-permute-done((bf16[2,256,512]{2,1,0:T(8,128)(2,1)S(1)}, bf16[2,256,512]{2,1,0:T(8,128)(2,1)S(1)}, u32[]{:S(2)}, u32[]{:S(2)}) %collective-permute-start.7) | collective-permute-done | bytes 524320 | tf_op jit(solution)/shard_map/ppermute | solution.py:213
  102.6 0.1 shard_map.86
  102.7 3.5 %collective-permute-start.8 = (bf16[256,512]{1,0:T(8,128)(2,1)S(1)}, bf16[256,512]{1,0:T(8,128)(2,1)S(1)}, u32[]{:S(2)}, u32[]{:S(2)}) collective-permute-start(bf16[256,512]{1,0:T(8,128)(2,1)S(1)} %get-tuple-element.26), channel_id=1, source_target_pairs={{0,256},{256,0},{1,257},{257,1},{2,258},{258,2},{3,259},{259,3},{4... | collective-permute-start | bytes 786440 | tf_op jit(solution)/shard_map/ppermute | solution.py:213
  106.2 7.4 %collective-permute-done.8.came = bf16[256,512]{1,0:T(8,128)(2,1)S(1)} collective-permute-done((bf16[256,512]{1,0:T(8,128)(2,1)S(1)}, bf16[256,512]{1,0:T(8,128)(2,1)S(1)}, u32[]{:S(2)}, u32[]{:S(2)}) %collective-permute-start.8) | collective-permute-done | bytes 262176 | tf_op jit(solution)/shard_map/ppermute | solution.py:213
  113.7 0.7 shard_map.87
  114.4 0.7 shard_map.84
  (10 shorter events, 0.1 us)
Async XLA Ops:
  0.6 0.9 copy-start
  1.6 0.8 copy-start.1
  2.7 24.7 %collective-permute-start = (bf16[256,512]{1,0:T(8,128)(2,1)S(1)}, bf16[256,512]{1,0:T(8,128)(2,1)S(1)}, u32[]{:S(2)}, u32[]{:S(2)}) collective-permute-start(bf16[256,512]{1,0:T(8,128)(2,1)S(1)} %shard_map.77.first), channel_id=1, source_target_pairs={{0,16},{16,0},{1,17},{17,1},{2,18},{18,2},{3,19},{19,3},{4,20},{20... | collective-permute-start | bytes 786440 | tf_op jit(solution)/shard_map/ppermute | solution.py:213
  7.0 26.1 %collective-permute-start.2 = (bf16[256,512]{1,0:T(8,128)(2,1)S(1)}, bf16[256,512]{1,0:T(8,128)(2,1)S(1)}, u32[]{:S(2)}, u32[]{:S(2)}) collective-permute-start(bf16[256,512]{1,0:T(8,128)(2,1)S(1)} %shard_map.77.first), channel_id=1, source_target_pairs={{0,256},{256,0},{1,257},{257,1},{2,258},{258,2},{3,259},{259,3},{4... | collective-permute-start | bytes 786440 | tf_op jit(solution)/shard_map/ppermute | solution.py:213
  13.5 30.5 %all-to-all-start = ((bf16[8,144,128]{2,1,0:T(8,128)(2,1)}), bf16[8,144,128]{2,1,0:T(8,128)(2,1)S(1)}, u32[]{:S(2)}, u32[]{:S(2)}) async-start(bf16[8,144,128]{2,1,0:T(8,128)(2,1)} %shard_map.76), calls=%async_computation | async-start | bytes 589824 | tf_op jit(solution)/shard_map/all_to_all | solution.py:217
  27.4 9.7 %collective-permute-start.3 = (bf16[256,512]{1,0:T(8,128)(2,1)S(1)}, bf16[256,512]{1,0:T(8,128)(2,1)S(1)}, u32[]{:S(2)}, u32[]{:S(2)}) collective-permute-start(bf16[256,512]{1,0:T(8,128)(2,1)S(1)} %collective-permute-done.second), channel_id=1, source_target_pairs={{0,256},{256,0},{1,257},{257,1},{2,258},{258,2},{3,259},{259,3},{4... | collective-permute-start | bytes 786440 | tf_op jit(solution)/shard_map/ppermute | solution.py:213
  29.4 17.2 %collective-permute-start.1 = (bf16[512,512]{1,0:T(8,128)(2,1)S(1)}, bf16[512,512]{1,0:T(8,128)(2,1)S(1)}, u32[]{:S(2)}, u32[]{:S(2)}) collective-permute-start(bf16[512,512]{1,0:T(8,128)(2,1)S(1)} %shard_map.78.refs_0_), channel_id=1, source_target_pairs={{0,8},{8,0},{1,9},{9,1},{2,10},{10,2},{3,11},{11,3},{4,12},{12,4},... | collective-permute-start | bytes 1572872 | tf_op jit(solution)/shard_map/ppermute | solution.py:213
  37.1 9.5 %collective-permute-start.4 = (bf16[512,512]{1,0:T(8,128)(2,1)S(1)}, bf16[512,512]{1,0:T(8,128)(2,1)S(1)}, u32[]{:S(2)}, u32[]{:S(2)}) collective-permute-start(bf16[512,512]{1,0:T(8,128)(2,1)S(1)} %shard_map.79.refs_2_), channel_id=1, source_target_pairs={{0,8},{8,0},{1,9},{9,1},{2,10},{10,2},{3,11},{11,3},{4,12},{12,4},... | collective-permute-start | bytes 1572872 | tf_op jit(solution)/shard_map/ppermute | solution.py:213
  44.0 13.9 %collective-permute-start.5 = (bf16[8,144,128]{2,1,0:T(8,128)(2,1)S(1)}, bf16[8,144,128]{2,1,0:T(8,128)(2,1)S(1)}, u32[]{:S(2)}, u32[]{:S(2)}) collective-permute-start(bf16[8,144,128]{2,1,0:T(8,128)(2,1)S(1)} %all-to-all-done.near), channel_id=1, source_target_pairs={{0,16},{16,0},{1,17},{17,1},{2,18},{18,2},{3,19},{19,3},{4,20},{20... | collective-permute-start | bytes 884744 | tf_op jit(solution)/shard_map/ppermute | solution.py:213
  67.5 21.0 %all-to-all-start.3 = ((f32[16,8,128]{2,1,0:T(8,128)}), f32[16,8,128]{2,1,0:T(8,128)S(1)}, u32[]{:S(2)}, u32[]{:S(2)}) async-start(f32[16,8,128]{2,1,0:T(8,128)} %get-tuple-element.17), calls=%async_computation.3 | async-start | bytes 131072 | tf_op jit(solution)/shard_map/all_to_all | solution.py:217
  76.8 16.7 %collective-permute-start.6 = (f32[4,72,128]{2,1,0:T(8,128)S(1)}, f32[4,72,128]{2,1,0:T(8,128)S(1)}, u32[]{:S(2)}, u32[]{:S(2)}) collective-permute-start(f32[4,72,128]{2,1,0:T(8,128)S(1)} %get-tuple-element.22), channel_id=1, source_target_pairs={{0,16},{16,0},{1,17},{17,1},{2,18},{18,2},{3,19},{19,3},{4,20},{20... | collective-permute-start | bytes 442376 | tf_op jit(solution)/shard_map/ppermute | solution.py:213
  90.1 24.3 %all-to-all-start.4 = ((bf16[8,32,512]{2,1,0:T(8,128)(2,1)}), bf16[8,32,512]{2,1,0:T(8,128)(2,1)S(1)}, u32[]{:S(2)}, u32[]{:S(2)}) async-start(bf16[8,32,512]{2,1,0:T(8,128)(2,1)} %get-tuple-element.19), calls=%async_computation.4 | async-start | bytes 524288 | tf_op jit(solution)/shard_map/all_to_all | solution.py:217
  94.3 8.3 %collective-permute-start.7 = (bf16[2,256,512]{2,1,0:T(8,128)(2,1)S(1)}, bf16[2,256,512]{2,1,0:T(8,128)(2,1)S(1)}, u32[]{:S(2)}, u32[]{:S(2)}) collective-permute-start(bf16[2,256,512]{2,1,0:T(8,128)(2,1)S(1)} %get-tuple-element.24), channel_id=1, source_target_pairs={{0,8},{8,0},{1,9},{9,1},{2,10},{10,2},{3,11},{11,3},{4,12},{12,4},... | collective-permute-start | bytes 1572872 | tf_op jit(solution)/shard_map/ppermute | solution.py:213
  102.7 10.9 %collective-permute-start.8 = (bf16[256,512]{1,0:T(8,128)(2,1)S(1)}, bf16[256,512]{1,0:T(8,128)(2,1)S(1)}, u32[]{:S(2)}, u32[]{:S(2)}) collective-permute-start(bf16[256,512]{1,0:T(8,128)(2,1)S(1)} %get-tuple-element.26), channel_id=1, source_target_pairs={{0,256},{256,0},{1,257},{257,1},{2,258},{258,2},{3,259},{259,3},{4... | collective-permute-start | bytes 786440 | tf_op jit(solution)/shard_map/ppermute | solution.py:213

commit v11 on v10

--- a/solution.py
+++ b/solution.py
@@ -34,11 +34,13 @@
     )(*args)
 
 
-def pack_kernel(queries, owners, rows, sent, mine, short, wide, sems):
+def pack_kernel(queries, owners, rows, negatives, passages, sent, columns, mine, short, wide, sems):
     copies = [
         pltpu.make_async_copy(owners, short.at[0], sems.at[0]),
         pltpu.make_async_copy(rows, short.at[1], sems.at[1]),
         pltpu.make_async_copy(queries, mine, sems.at[2]),
+        pltpu.make_async_copy(negatives, columns.at[32:256], sems.at[3]),
+        pltpu.make_async_copy(passages, columns.at[0:32], sems.at[4]),
     ]
     for copy in copies:
         copy.start()
@@ -63,17 +65,8 @@
     for to in range(NH):
         for l in range(4):
             sent[to, l * 32 : (l + 1) * 32, :] = mine[:, l * 128 : (l + 1) * 128]
-
-
-def column_pack_kernel(passages, negatives, columns, sems):
-    copies = [
-        pltpu.make_async_copy(negatives, columns.at[32:256], sems.at[0]),
-        pltpu.make_async_copy(passages, columns.at[0:32], sems.at[1]),
-    ]
-    for copy in copies:
-        copy.start()
-    for copy in copies:
-        copy.wait()
+    copies[3].wait()
+    copies[4].wait()
 
 
 def unpack(came, lines, queries, asked):
@@ -218,17 +211,13 @@
 
 
 def shards(queries, passages, negatives, hard_owner, hard_row):
-    (sent,) = call(
-        pack_kernel, [((NH, 144, 128), BF16)],
-        queries, hard_owner.T, hard_row.T, hbm=3, limit=PACK_LIMIT,
+    sent, col0 = call(
+        pack_kernel, [((NH, 144, 128), BF16), ((256, 512), BF16)],
+        queries, hard_owner.T, hard_row.T, negatives, passages, hbm=5, limit=PACK_LIMIT,
         scratch=[
             pltpu.VMEM((32, 512), BF16), pltpu.VMEM((2, 7, 32), jnp.int32), pltpu.VMEM((2, 7, 128), jnp.int32),
-            pltpu.SemaphoreType.DMA((3,)),
+            pltpu.SemaphoreType.DMA((5,)),
         ],
-    )
-    (col0,) = call(
-        column_pack_kernel, [((256, 512), BF16)], passages, negatives, hbm=2,
-        scratch=[pltpu.SemaphoreType.DMA((2,))],
     )
     by_yh, by_zp = swap(col0, "yh"), swap(col0, "zp")
     near = exchange(sent, "zh")

time: 116 us -> 114 us (0.983)
  local copies, waits for them, and re-layouts: 1.69 us -> 0.01 us
    unnamed x4 -> x2, local copies, waits for them, and re-layouts: 1.69 us -> 0.01 us
    pallas_call x12 -> x11, Pallas kernels: 7.3 us -> 7.25 us  [call(): pl.pallas_call(kernel, out_shape=[jax.ShapeDtypeStruct(shape, dtype) for...]
  transfers between devices with their start and end apart: 12 -> 12, of which waited for: 5 -> 5; matrix products, arithmetic and copies ran while one was open for 0% -> 0% of each run, Pallas kernels for 5% -> 4%
where the time goes in v11:
time: 114 us; the launch traced here: 113 us
  starting transfers between devices  62.1 us (54%)
  waiting for transfers between devices  23.9 us (21%)
  blocking collectives  19.3 us (17%)
  Pallas kernels  7.25 us (6%)
    ppermute x9, starting transfers between devices, swap(): return lax.ppermute(x, axis, [(0, 1), (1, 0)])  35.4 us
    all_to_all x3, starting transfers between devices, exchange(): return lax.all_to_all(x, axes, split_axis=0, concat_axis=0, tiled=True)  26.7 us
    all_to_all x2, blocking collectives, exchange(): return lax.all_to_all(x, axes, split_axis=0, concat_axis=0, tiled=True)  19.3 us
    ppermute x9, waiting for transfers between devices, swap(): return lax.ppermute(x, axis, [(0, 1), (1, 0)])  12.9 us
    all_to_all x3, waiting for transfers between devices, exchange(): return lax.all_to_all(x, axes, split_axis=0, concat_axis=0, tiled=True)  11 us
    pallas_call x11, Pallas kernels, call(): pl.pallas_call(kernel, out_shape=[jax.ShapeDtypeStruct(shape, dtype) for...  7.25 us
  transfers between devices with their start and end apart: 12, of which 5 were waited for; matrix products, arithmetic and copies ran while one was open for 0% of the time, Pallas kernels for 4%

profile of v11, /device:TPU:1, one launch (start us, length us, event | category | flops | bytes accessed | tf_op | source)
XLA Modules:
  0.0 113.4 jit_solution(13353354375529440208)
XLA Ops:
  0.6 1.9 %shard_map.76 = (bf16[8,144,128]{2,1,0:T(8,128)(2,1)}, bf16[256,512]{1,0:T(8,128)(2,1)}) custom-call(bf16[32,512]{1,0:T(8,128)(2,1)} %queries.1, s32[7,32]{1,0:T(8,128)} %bitcast.4, s32[7,32]{1,0:T(8,128)} %bitcast.5, bf16[224,512]{1,0:T(8,128)(2,1)} %negatives.1, bf16[32,512]{1,0:T(8,128)(2,1)} %passages.1), custom_call_target="tpu_custom_call" | custom-call | tf_op jit(solution)/shard_map/pallas_call | solution.py:26
  2.5 4.4 %collective-permute-start = (bf16[256,512]{1,0:T(8,128)(2,1)}, bf16[256,512]{1,0:T(8,128)(2,1)S(1)}, u32[]{:S(2)}, u32[]{:S(2)}) collective-permute-start(bf16[256,512]{1,0:T(8,128)(2,1)} %get-tuple-element.19.first), channel_id=1, source_target_pairs={{0,16},{16,0},{1,17},{17,1},{2,18},{18,2},{3,19},{19,3},{4,20},{20... | collective-permute-start | bytes 786440 | tf_op jit(solution)/shard_map/ppermute | solution.py:206
  6.9 4.8 %collective-permute-start.2 = (bf16[256,512]{1,0:T(8,128)(2,1)}, bf16[256,512]{1,0:T(8,128)(2,1)S(1)}, u32[]{:S(2)}, u32[]{:S(2)}) collective-permute-start(bf16[256,512]{1,0:T(8,128)(2,1)} %get-tuple-element.19.first), channel_id=1, source_target_pairs={{0,256},{256,0},{1,257},{257,1},{2,258},{258,2},{3,259},{259,3},{4... | collective-permute-start | bytes 786440 | tf_op jit(solution)/shard_map/ppermute | solution.py:206
  11.7 14.1 %all-to-all-start = ((bf16[8,144,128]{2,1,0:T(8,128)(2,1)}), bf16[8,144,128]{2,1,0:T(8,128)(2,1)S(1)}, u32[]{:S(2)}, u32[]{:S(2)}) async-start(bf16[8,144,128]{2,1,0:T(8,128)(2,1)} %get-tuple-element.18), calls=%async_computation | async-start | bytes 589824 | tf_op jit(solution)/shard_map/all_to_all | solution.py:210
  25.8 0.0 collective-permute-done.second
  25.8 2.0 %collective-permute-start.3 = (bf16[256,512]{1,0:T(8,128)(2,1)S(1)}, bf16[256,512]{1,0:T(8,128)(2,1)S(1)}, u32[]{:S(2)}, u32[]{:S(2)}) collective-permute-start(bf16[256,512]{1,0:T(8,128)(2,1)S(1)} %collective-permute-done.second), channel_id=1, source_target_pairs={{0,256},{256,0},{1,257},{257,1},{2,258},{258,2},{3,259},{259,3},{4... | collective-permute-start | bytes 786440 | tf_op jit(solution)/shard_map/ppermute | solution.py:206
  27.8 3.7 %collective-permute-start.1 = (bf16[512,512]{1,0:T(8,128)(2,1)S(1)}, bf16[512,512]{1,0:T(8,128)(2,1)S(1)}, u32[]{:S(2)}, u32[]{:S(2)}) collective-permute-start(bf16[512,512]{1,0:T(8,128)(2,1)S(1)} %shard_map.77.refs_0_), channel_id=1, source_target_pairs={{0,8},{8,0},{1,9},{9,1},{2,10},{10,2},{3,11},{11,3},{4,12},{12,4},... | collective-permute-start | bytes 1572872 | tf_op jit(solution)/shard_map/ppermute | solution.py:206
  31.5 0.0 collective-permute-done.2.first
  31.5 3.9 %collective-permute-done.3.second = bf16[256,512]{1,0:T(8,128)(2,1)S(1)} collective-permute-done((bf16[256,512]{1,0:T(8,128)(2,1)S(1)}, bf16[256,512]{1,0:T(8,128)(2,1)S(1)}, u32[]{:S(2)}, u32[]{:S(2)}) %collective-permute-start.3) | collective-permute-done | bytes 262176 | tf_op jit(solution)/shard_map/ppermute | solution.py:206
  35.5 4.3 %collective-permute-start.4 = (bf16[512,512]{1,0:T(8,128)(2,1)S(1)}, bf16[512,512]{1,0:T(8,128)(2,1)S(1)}, u32[]{:S(2)}, u32[]{:S(2)}) collective-permute-start(bf16[512,512]{1,0:T(8,128)(2,1)S(1)} %shard_map.78.refs_2_), channel_id=1, source_target_pairs={{0,8},{8,0},{1,9},{9,1},{2,10},{10,2},{3,11},{11,3},{4,12},{12,4},... | collective-permute-start | bytes 1572872 | tf_op jit(solution)/shard_map/ppermute | solution.py:206
  39.9 2.5 %all-to-all-done.near = bf16[8,144,128]{2,1,0:T(8,128)(2,1)S(1)} async-done(((bf16[8,144,128]{2,1,0:T(8,128)(2,1)}), bf16[8,144,128]{2,1,0:T(8,128)(2,1)S(1)}, u32[]{:S(2)}, u32[]{:S(2)}) %all-to-all-start) | async-done | bytes 294944 | tf_op jit(solution)/shard_map/all_to_all | solution.py:210
  42.4 2.7 %collective-permute-start.5 = (bf16[8,144,128]{2,1,0:T(8,128)(2,1)S(1)}, bf16[8,144,128]{2,1,0:T(8,128)(2,1)S(1)}, u32[]{:S(2)}, u32[]{:S(2)}) collective-permute-start(bf16[8,144,128]{2,1,0:T(8,128)(2,1)S(1)} %all-to-all-done.near), channel_id=1, source_target_pairs={{0,16},{16,0},{1,17},{17,1},{2,18},{18,2},{3,19},{19,3},{4,20},{20... | collective-permute-start | bytes 884744 | tf_op jit(solution)/shard_map/ppermute | solution.py:206
  45.0 0.0 collective-permute-done.1.refs_1_
  45.0 0.0 collective-permute-done.4.refs_3_
  45.0 0.8 shard_map.79
  45.8 10.4 %all_to_all.25.came = f32[8,72,128]{2,1,0:T(8,128)S(1)} all-to-all(f32[8,72,128]{2,1,0:T(8,128)S(1)} %get-tuple-element.20), channel_id=1, replica_groups=mesh['yh'=2,'zh'=8,'zp'=2,'c'=2,'yl'=2,'x'=4] {'yl','x'}, dimensions={0} | all-to-all | bytes 589824 | tf_op jit(solution)/shard_map/all_to_all | solution.py:210
  56.3 0.0 collective-permute-done.5.far
  56.3 8.9 %all_to_all.26.scores = f32[8,72,128]{2,1,0:T(8,128)S(1)} all-to-all(f32[8,72,128]{2,1,0:T(8,128)S(1)} %shard_map.80), channel_id=1, replica_groups=mesh['yh'=2,'zh'=8,'zp'=2,'c'=2,'yl'=2,'x'=4] {'yl','x'}, dimensions={0} | all-to-all | bytes 589824 | tf_op jit(solution)/shard_map/all_to_all | solution.py:210
  65.2 0.7 shard_map.81
  65.9 9.2 %all-to-all-start.3 = ((f32[16,8,128]{2,1,0:T(8,128)}), f32[16,8,128]{2,1,0:T(8,128)S(1)}, u32[]{:S(2)}, u32[]{:S(2)}) async-start(f32[16,8,128]{2,1,0:T(8,128)} %get-tuple-element.21), calls=%async_computation.3 | async-start | bytes 131072 | tf_op jit(solution)/shard_map/all_to_all | solution.py:210
  75.2 3.3 %collective-permute-start.6 = (f32[4,72,128]{2,1,0:T(8,128)S(1)}, f32[4,72,128]{2,1,0:T(8,128)S(1)}, u32[]{:S(2)}, u32[]{:S(2)}) collective-permute-start(f32[4,72,128]{2,1,0:T(8,128)S(1)} %get-tuple-element.26), channel_id=1, source_target_pairs={{0,16},{16,0},{1,17},{17,1},{2,18},{18,2},{3,19},{19,3},{4,20},{20... | collective-permute-start | bytes 442376 | tf_op jit(solution)/shard_map/ppermute | solution.py:206
  78.4 8.5 %all-to-all-done.3 = f32[16,8,128]{2,1,0:T(8,128)S(1)} async-done(((f32[16,8,128]{2,1,0:T(8,128)}), f32[16,8,128]{2,1,0:T(8,128)S(1)}, u32[]{:S(2)}, u32[]{:S(2)}) %all-to-all-start.3) | async-done | bytes 65568 | tf_op jit(solution)/shard_map/all_to_all | solution.py:210
  86.9 1.5 %shard_map.82 = (bf16[8,32,512]{2,1,0:T(8,128)(2,1)}, f32[8,256]{1,0:T(8,128)S(1)}) custom-call(f32[8,2,8,128]{3,2,1,0:T(8,128)S(1)} %bitcast.3, f32[8,72,128]{2,1,0:T(8,128)S(1)} %all_to_all.26.scores, s32[8,256]{1,0:T(8,128)S(1)} %get-tuple-element.22.asked, bf16[512,512]{1,0:T(8,128)(2,1)S(1)} %shard_map.77.refs_0_, ...), custom_call_target="tpu_custom_call" | custom-call | tf_op jit(solution)/shard_map/pallas_call | solution.py:26
  88.5 3.4 %all-to-all-start.4 = ((bf16[8,32,512]{2,1,0:T(8,128)(2,1)}), bf16[8,32,512]{2,1,0:T(8,128)(2,1)S(1)}, u32[]{:S(2)}, u32[]{:S(2)}) async-start(bf16[8,32,512]{2,1,0:T(8,128)(2,1)} %get-tuple-element.23), calls=%async_computation.4 | async-start | bytes 524288 | tf_op jit(solution)/shard_map/all_to_all | solution.py:210
  91.9 0.8 shard_map.84
  92.7 6.8 %collective-permute-start.7 = (bf16[2,256,512]{2,1,0:T(8,128)(2,1)S(1)}, bf16[2,256,512]{2,1,0:T(8,128)(2,1)S(1)}, u32[]{:S(2)}, u32[]{:S(2)}) collective-permute-start(bf16[2,256,512]{2,1,0:T(8,128)(2,1)S(1)} %get-tuple-element.28), channel_id=1, source_target_pairs={{0,8},{8,0},{1,9},{9,1},{2,10},{10,2},{3,11},{11,3},{4,12},{12,4},... | collective-permute-start | bytes 1572872 | tf_op jit(solution)/shard_map/ppermute | solution.py:206
  99.5 1.5 %collective-permute-done.7.came = bf16[2,256,512]{2,1,0:T(8,128)(2,1)S(1)} collective-permute-done((bf16[2,256,512]{2,1,0:T(8,128)(2,1)S(1)}, bf16[2,256,512]{2,1,0:T(8,128)(2,1)S(1)}, u32[]{:S(2)}, u32[]{:S(2)}) %collective-permute-start.7) | collective-permute-done | bytes 524320 | tf_op jit(solution)/shard_map/ppermute | solution.py:206
  101.0 0.1 shard_map.85
  101.1 3.5 %collective-permute-start.8 = (bf16[256,512]{1,0:T(8,128)(2,1)S(1)}, bf16[256,512]{1,0:T(8,128)(2,1)S(1)}, u32[]{:S(2)}, u32[]{:S(2)}) collective-permute-start(bf16[256,512]{1,0:T(8,128)(2,1)S(1)} %get-tuple-element.30), channel_id=1, source_target_pairs={{0,256},{256,0},{1,257},{257,1},{2,258},{258,2},{3,259},{259,3},{4... | collective-permute-start | bytes 786440 | tf_op jit(solution)/shard_map/ppermute | solution.py:206
  104.6 7.4 %collective-permute-done.8.came = bf16[256,512]{1,0:T(8,128)(2,1)S(1)} collective-permute-done((bf16[256,512]{1,0:T(8,128)(2,1)S(1)}, bf16[256,512]{1,0:T(8,128)(2,1)S(1)}, u32[]{:S(2)}, u32[]{:S(2)}) %collective-permute-start.8) | collective-permute-done | bytes 262176 | tf_op jit(solution)/shard_map/ppermute | solution.py:206
  112.0 0.7 shard_map.86
  112.8 0.7 shard_map.83
  (7 shorter events, 0.1 us)
Async XLA Ops:
  2.5 23.3 %collective-permute-start = (bf16[256,512]{1,0:T(8,128)(2,1)}, bf16[256,512]{1,0:T(8,128)(2,1)S(1)}, u32[]{:S(2)}, u32[]{:S(2)}) collective-permute-start(bf16[256,512]{1,0:T(8,128)(2,1)} %get-tuple-element.19.first), channel_id=1, source_target_pairs={{0,16},{16,0},{1,17},{17,1},{2,18},{18,2},{3,19},{19,3},{4,20},{20... | collective-permute-start | bytes 786440 | tf_op jit(solution)/shard_map/ppermute | solution.py:206
  6.9 24.6 %collective-permute-start.2 = (bf16[256,512]{1,0:T(8,128)(2,1)}, bf16[256,512]{1,0:T(8,128)(2,1)S(1)}, u32[]{:S(2)}, u32[]{:S(2)}) collective-permute-start(bf16[256,512]{1,0:T(8,128)(2,1)} %get-tuple-element.19.first), channel_id=1, source_target_pairs={{0,256},{256,0},{1,257},{257,1},{2,258},{258,2},{3,259},{259,3},{4... | collective-permute-start | bytes 786440 | tf_op jit(solution)/shard_map/ppermute | solution.py:206
  11.7 16.0 %copy-start = (bf16[256,512]{1,0:T(8,128)(2,1)S(1)}, bf16[256,512]{1,0:T(8,128)(2,1)}, u32[]{:S(2)}) copy-start(bf16[256,512]{1,0:T(8,128)(2,1)} %get-tuple-element.19.first) | copy-start | bytes 786436
  11.7 30.6 %all-to-all-start = ((bf16[8,144,128]{2,1,0:T(8,128)(2,1)}), bf16[8,144,128]{2,1,0:T(8,128)(2,1)S(1)}, u32[]{:S(2)}, u32[]{:S(2)}) async-start(bf16[8,144,128]{2,1,0:T(8,128)(2,1)} %get-tuple-element.18), calls=%async_computation | async-start | bytes 589824 | tf_op jit(solution)/shard_map/all_to_all | solution.py:210
  25.8 9.7 %collective-permute-start.3 = (bf16[256,512]{1,0:T(8,128)(2,1)S(1)}, bf16[256,512]{1,0:T(8,128)(2,1)S(1)}, u32[]{:S(2)}, u32[]{:S(2)}) collective-permute-start(bf16[256,512]{1,0:T(8,128)(2,1)S(1)} %collective-permute-done.second), channel_id=1, source_target_pairs={{0,256},{256,0},{1,257},{257,1},{2,258},{258,2},{3,259},{259,3},{4... | collective-permute-start | bytes 786440 | tf_op jit(solution)/shard_map/ppermute | solution.py:206
  27.8 17.2 %collective-permute-start.1 = (bf16[512,512]{1,0:T(8,128)(2,1)S(1)}, bf16[512,512]{1,0:T(8,128)(2,1)S(1)}, u32[]{:S(2)}, u32[]{:S(2)}) collective-permute-start(bf16[512,512]{1,0:T(8,128)(2,1)S(1)} %shard_map.77.refs_0_), channel_id=1, source_target_pairs={{0,8},{8,0},{1,9},{9,1},{2,10},{10,2},{3,11},{11,3},{4,12},{12,4},... | collective-permute-start | bytes 1572872 | tf_op jit(solution)/shard_map/ppermute | solution.py:206
  35.5 9.5 %collective-permute-start.4 = (bf16[512,512]{1,0:T(8,128)(2,1)S(1)}, bf16[512,512]{1,0:T(8,128)(2,1)S(1)}, u32[]{:S(2)}, u32[]{:S(2)}) collective-permute-start(bf16[512,512]{1,0:T(8,128)(2,1)S(1)} %shard_map.78.refs_2_), channel_id=1, source_target_pairs={{0,8},{8,0},{1,9},{9,1},{2,10},{10,2},{3,11},{11,3},{4,12},{12,4},... | collective-permute-start | bytes 1572872 | tf_op jit(solution)/shard_map/ppermute | solution.py:206
  42.4 13.9 %collective-permute-start.5 = (bf16[8,144,128]{2,1,0:T(8,128)(2,1)S(1)}, bf16[8,144,128]{2,1,0:T(8,128)(2,1)S(1)}, u32[]{:S(2)}, u32[]{:S(2)}) collective-permute-start(bf16[8,144,128]{2,1,0:T(8,128)(2,1)S(1)} %all-to-all-done.near), channel_id=1, source_target_pairs={{0,16},{16,0},{1,17},{17,1},{2,18},{18,2},{3,19},{19,3},{4,20},{20... | collective-permute-start | bytes 884744 | tf_op jit(solution)/shard_map/ppermute | solution.py:206
  65.9 21.0 %all-to-all-start.3 = ((f32[16,8,128]{2,1,0:T(8,128)}), f32[16,8,128]{2,1,0:T(8,128)S(1)}, u32[]{:S(2)}, u32[]{:S(2)}) async-start(f32[16,8,128]{2,1,0:T(8,128)} %get-tuple-element.21), calls=%async_computation.3 | async-start | bytes 131072 | tf_op jit(solution)/shard_map/all_to_all | solution.py:210
  75.2 16.7 %collective-permute-start.6 = (f32[4,72,128]{2,1,0:T(8,128)S(1)}, f32[4,72,128]{2,1,0:T(8,128)S(1)}, u32[]{:S(2)}, u32[]{:S(2)}) collective-permute-start(f32[4,72,128]{2,1,0:T(8,128)S(1)} %get-tuple-element.26), channel_id=1, source_target_pairs={{0,16},{16,0},{1,17},{17,1},{2,18},{18,2},{3,19},{19,3},{4,20},{20... | collective-permute-start | bytes 442376 | tf_op jit(solution)/shard_map/ppermute | solution.py:206
  88.5 24.3 %all-to-all-start.4 = ((bf16[8,32,512]{2,1,0:T(8,128)(2,1)}), bf16[8,32,512]{2,1,0:T(8,128)(2,1)S(1)}, u32[]{:S(2)}, u32[]{:S(2)}) async-start(bf16[8,32,512]{2,1,0:T(8,128)(2,1)} %get-tuple-element.23), calls=%async_computation.4 | async-start | bytes 524288 | tf_op jit(solution)/shard_map/all_to_all | solution.py:210
  92.7 8.3 %collective-permute-start.7 = (bf16[2,256,512]{2,1,0:T(8,128)(2,1)S(1)}, bf16[2,256,512]{2,1,0:T(8,128)(2,1)S(1)}, u32[]{:S(2)}, u32[]{:S(2)}) collective-permute-start(bf16[2,256,512]{2,1,0:T(8,128)(2,1)S(1)} %get-tuple-element.28), channel_id=1, source_target_pairs={{0,8},{8,0},{1,9},{9,1},{2,10},{10,2},{3,11},{11,3},{4,12},{12,4},... | collective-permute-start | bytes 1572872 | tf_op jit(solution)/shard_map/ppermute | solution.py:206
  101.1 10.9 %collective-permute-start.8 = (bf16[256,512]{1,0:T(8,128)(2,1)S(1)}, bf16[256,512]{1,0:T(8,128)(2,1)S(1)}, u32[]{:S(2)}, u32[]{:S(2)}) collective-permute-start(bf16[256,512]{1,0:T(8,128)(2,1)S(1)} %get-tuple-element.30), channel_id=1, source_target_pairs={{0,256},{256,0},{1,257},{257,1},{2,258},{258,2},{3,259},{259,3},{4... | collective-permute-start | bytes 786440 | tf_op jit(solution)/shard_map/ppermute | solution.py:206

commit v12 on v11

--- a/solution.py
+++ b/solution.py
@@ -190,15 +190,12 @@
     sent[...] = (keep[1].astype(F32) + came[1].astype(F32)).astype(BF16)
 
 
-def column_kernel(own, came, passage_out, negative_out):
+def last_kernel(own, came, q_came, query_out, passage_out, negative_out):
     passage_out[...] = (own[0:32, :] + came[0:32, :].astype(F32)).astype(BF16)
     negative_out[...] = (own[32:256, :] + came[32:256, :].astype(F32)).astype(BF16)
-
-
-def query_kernel(came, query_out):
-    total = came[0].astype(F32)
+    total = q_came[0].astype(F32)
     for z in range(1, NH):
-        total = total + came[z].astype(F32)
+        total = total + q_came[z].astype(F32)
     query_out[...] = total.astype(BF16)
 
 
@@ -245,9 +242,7 @@
     )
     own, cross = call(pair_kernel, [((256, 512), F32), ((256, 512), BF16)], keep, swap(give, "c"))
     cross = swap(cross, "yh")
-    passage_out, negative_out = call(column_kernel, [((32, 512), BF16), ((224, 512), BF16)], own, cross)
-    (query_out,) = call(query_kernel, [((32, 512), BF16)], q_came)
-    return (query_out, passage_out, negative_out)
+    return tuple(call(last_kernel, [((32, 512), BF16), ((32, 512), BF16), ((224, 512), BF16)], own, cross, q_came))
 
 
 def solution(mesh):

time: 114 us -> 114 us (level)
    pallas_call x11 -> x10, Pallas kernels: 7.25 us -> 6.58 us  [call(): pl.pallas_call(kernel, out_shape=[jax.ShapeDtypeStruct(shape, dtype) for...]
  transfers between devices with their start and end apart: 12 -> 12, of which waited for: 5 -> 5; matrix products, arithmetic and copies ran while one was open for 0% -> 0% of each run, Pallas kernels for 4% -> 3%
where the time goes in v12:
time: 114 us; the launch traced here: 113 us
  starting transfers between devices  62.1 us (54%)
  waiting for transfers between devices  23.9 us (21%)
  blocking collectives  19.3 us (17%)
  Pallas kernels  6.58 us (6%)
    ppermute x9, starting transfers between devices, swap(): return lax.ppermute(x, axis, [(0, 1), (1, 0)])  35.4 us
    all_to_all x3, starting transfers between devices, exchange(): return lax.all_to_all(x, axes, split_axis=0, concat_axis=0, tiled=True)  26.7 us
    all_to_all x2, blocking collectives, exchange(): return lax.all_to_all(x, axes, split_axis=0, concat_axis=0, tiled=True)  19.3 us
    ppermute x9, waiting for transfers between devices, swap(): return lax.ppermute(x, axis, [(0, 1), (1, 0)])  12.9 us
    all_to_all x3, waiting for transfers between devices, exchange(): return lax.all_to_all(x, axes, split_axis=0, concat_axis=0, tiled=True)  11 us
    pallas_call x10, Pallas kernels, call(): pl.pallas_call(kernel, out_shape=[jax.ShapeDtypeStruct(shape, dtype) for...  6.58 us
  transfers between devices with their start and end apart: 12, of which 5 were waited for; matrix products, arithmetic and copies ran while one was open for 0% of the time, Pallas kernels for 3%

profile of v12, /device:TPU:1, one launch (start us, length us, event | category | flops | bytes accessed | tf_op | source)
XLA Modules:
  0.0 112.8 jit_solution(18048247790214223009)
XLA Ops:
  0.6 1.8 %shard_map.76 = (bf16[8,144,128]{2,1,0:T(8,128)(2,1)}, bf16[256,512]{1,0:T(8,128)(2,1)}) custom-call(bf16[32,512]{1,0:T(8,128)(2,1)} %queries.1, s32[7,32]{1,0:T(8,128)} %bitcast.4, s32[7,32]{1,0:T(8,128)} %bitcast.5, bf16[224,512]{1,0:T(8,128)(2,1)} %negatives.1, bf16[32,512]{1,0:T(8,128)(2,1)} %passages.1), custom_call_target="tpu_custom_call" | custom-call | tf_op jit(solution)/shard_map/pallas_call | solution.py:26
  2.5 4.4 %collective-permute-start = (bf16[256,512]{1,0:T(8,128)(2,1)}, bf16[256,512]{1,0:T(8,128)(2,1)S(1)}, u32[]{:S(2)}, u32[]{:S(2)}) collective-permute-start(bf16[256,512]{1,0:T(8,128)(2,1)} %get-tuple-element.17.first), channel_id=1, source_target_pairs={{0,16},{16,0},{1,17},{17,1},{2,18},{18,2},{3,19},{19,3},{4,20},{20... | collective-permute-start | bytes 786440 | tf_op jit(solution)/shard_map/ppermute | solution.py:203
  6.9 4.8 %collective-permute-start.2 = (bf16[256,512]{1,0:T(8,128)(2,1)}, bf16[256,512]{1,0:T(8,128)(2,1)S(1)}, u32[]{:S(2)}, u32[]{:S(2)}) collective-permute-start(bf16[256,512]{1,0:T(8,128)(2,1)} %get-tuple-element.17.first), channel_id=1, source_target_pairs={{0,256},{256,0},{1,257},{257,1},{2,258},{258,2},{3,259},{259,3},{4... | collective-permute-start | bytes 786440 | tf_op jit(solution)/shard_map/ppermute | solution.py:203
  11.7 14.1 %all-to-all-start = ((bf16[8,144,128]{2,1,0:T(8,128)(2,1)}), bf16[8,144,128]{2,1,0:T(8,128)(2,1)S(1)}, u32[]{:S(2)}, u32[]{:S(2)}) async-start(bf16[8,144,128]{2,1,0:T(8,128)(2,1)} %get-tuple-element.16), calls=%async_computation | async-start | bytes 589824 | tf_op jit(solution)/shard_map/all_to_all | solution.py:207
  25.8 0.0 collective-permute-done.second
  25.8 2.0 %collective-permute-start.3 = (bf16[256,512]{1,0:T(8,128)(2,1)S(1)}, bf16[256,512]{1,0:T(8,128)(2,1)S(1)}, u32[]{:S(2)}, u32[]{:S(2)}) collective-permute-start(bf16[256,512]{1,0:T(8,128)(2,1)S(1)} %collective-permute-done.second), channel_id=1, source_target_pairs={{0,256},{256,0},{1,257},{257,1},{2,258},{258,2},{3,259},{259,3},{4... | collective-permute-start | bytes 786440 | tf_op jit(solution)/shard_map/ppermute | solution.py:203
  27.8 3.7 %collective-permute-start.1 = (bf16[512,512]{1,0:T(8,128)(2,1)S(1)}, bf16[512,512]{1,0:T(8,128)(2,1)S(1)}, u32[]{:S(2)}, u32[]{:S(2)}) collective-permute-start(bf16[512,512]{1,0:T(8,128)(2,1)S(1)} %shard_map.77.refs_0_), channel_id=1, source_target_pairs={{0,8},{8,0},{1,9},{9,1},{2,10},{10,2},{3,11},{11,3},{4,12},{12,4},... | collective-permute-start | bytes 1572872 | tf_op jit(solution)/shard_map/ppermute | solution.py:203
  31.5 0.0 collective-permute-done.2.first
  31.5 3.9 %collective-permute-done.3.second = bf16[256,512]{1,0:T(8,128)(2,1)S(1)} collective-permute-done((bf16[256,512]{1,0:T(8,128)(2,1)S(1)}, bf16[256,512]{1,0:T(8,128)(2,1)S(1)}, u32[]{:S(2)}, u32[]{:S(2)}) %collective-permute-start.3) | collective-permute-done | bytes 262176 | tf_op jit(solution)/shard_map/ppermute | solution.py:203
  35.5 4.3 %collective-permute-start.4 = (bf16[512,512]{1,0:T(8,128)(2,1)S(1)}, bf16[512,512]{1,0:T(8,128)(2,1)S(1)}, u32[]{:S(2)}, u32[]{:S(2)}) collective-permute-start(bf16[512,512]{1,0:T(8,128)(2,1)S(1)} %shard_map.78.refs_2_), channel_id=1, source_target_pairs={{0,8},{8,0},{1,9},{9,1},{2,10},{10,2},{3,11},{11,3},{4,12},{12,4},... | collective-permute-start | bytes 1572872 | tf_op jit(solution)/shard_map/ppermute | solution.py:203
  39.8 2.5 %all-to-all-done.near = bf16[8,144,128]{2,1,0:T(8,128)(2,1)S(1)} async-done(((bf16[8,144,128]{2,1,0:T(8,128)(2,1)}), bf16[8,144,128]{2,1,0:T(8,128)(2,1)S(1)}, u32[]{:S(2)}, u32[]{:S(2)}) %all-to-all-start) | async-done | bytes 294944 | tf_op jit(solution)/shard_map/all_to_all | solution.py:207
  42.3 2.7 %collective-permute-start.5 = (bf16[8,144,128]{2,1,0:T(8,128)(2,1)S(1)}, bf16[8,144,128]{2,1,0:T(8,128)(2,1)S(1)}, u32[]{:S(2)}, u32[]{:S(2)}) collective-permute-start(bf16[8,144,128]{2,1,0:T(8,128)(2,1)S(1)} %all-to-all-done.near), channel_id=1, source_target_pairs={{0,16},{16,0},{1,17},{17,1},{2,18},{18,2},{3,19},{19,3},{4,20},{20... | collective-permute-start | bytes 884744 | tf_op jit(solution)/shard_map/ppermute | solution.py:203
  45.0 0.0 collective-permute-done.1.refs_1_
  45.0 0.0 collective-permute-done.4.refs_3_
  45.0 0.8 shard_map.79
  45.8 10.4 %all_to_all.25.came = f32[8,72,128]{2,1,0:T(8,128)S(1)} all-to-all(f32[8,72,128]{2,1,0:T(8,128)S(1)} %get-tuple-element.18), channel_id=1, replica_groups=mesh['yh'=2,'zh'=8,'zp'=2,'c'=2,'yl'=2,'x'=4] {'yl','x'}, dimensions={0} | all-to-all | bytes 589824 | tf_op jit(solution)/shard_map/all_to_all | solution.py:207
  56.3 0.0 collective-permute-done.5.far
  56.3 8.9 %all_to_all.26.scores = f32[8,72,128]{2,1,0:T(8,128)S(1)} all-to-all(f32[8,72,128]{2,1,0:T(8,128)S(1)} %shard_map.80), channel_id=1, replica_groups=mesh['yh'=2,'zh'=8,'zp'=2,'c'=2,'yl'=2,'x'=4] {'yl','x'}, dimensions={0} | all-to-all | bytes 589824 | tf_op jit(solution)/shard_map/all_to_all | solution.py:207
  65.2 0.7 shard_map.81
  65.9 9.2 %all-to-all-start.3 = ((f32[16,8,128]{2,1,0:T(8,128)}), f32[16,8,128]{2,1,0:T(8,128)S(1)}, u32[]{:S(2)}, u32[]{:S(2)}) async-start(f32[16,8,128]{2,1,0:T(8,128)} %get-tuple-element.19), calls=%async_computation.3 | async-start | bytes 131072 | tf_op jit(solution)/shard_map/all_to_all | solution.py:207
  75.1 3.3 %collective-permute-start.6 = (f32[4,72,128]{2,1,0:T(8,128)S(1)}, f32[4,72,128]{2,1,0:T(8,128)S(1)}, u32[]{:S(2)}, u32[]{:S(2)}) collective-permute-start(f32[4,72,128]{2,1,0:T(8,128)S(1)} %get-tuple-element.23), channel_id=1, source_target_pairs={{0,16},{16,0},{1,17},{17,1},{2,18},{18,2},{3,19},{19,3},{4,20},{20... | collective-permute-start | bytes 442376 | tf_op jit(solution)/shard_map/ppermute | solution.py:203
  78.4 8.5 %all-to-all-done.3 = f32[16,8,128]{2,1,0:T(8,128)S(1)} async-done(((f32[16,8,128]{2,1,0:T(8,128)}), f32[16,8,128]{2,1,0:T(8,128)S(1)}, u32[]{:S(2)}, u32[]{:S(2)}) %all-to-all-start.3) | async-done | bytes 65568 | tf_op jit(solution)/shard_map/all_to_all | solution.py:207
  86.9 1.5 %shard_map.82 = (bf16[8,32,512]{2,1,0:T(8,128)(2,1)}, f32[8,256]{1,0:T(8,128)S(1)}) custom-call(f32[8,2,8,128]{3,2,1,0:T(8,128)S(1)} %bitcast.3, f32[8,72,128]{2,1,0:T(8,128)S(1)} %all_to_all.26.scores, s32[8,256]{1,0:T(8,128)S(1)} %get-tuple-element.20.asked, bf16[512,512]{1,0:T(8,128)(2,1)S(1)} %shard_map.77.refs_0_, ...), custom_call_target="tpu_custom_call" | custom-call | tf_op jit(solution)/shard_map/pallas_call | solution.py:26
  88.4 3.4 %all-to-all-start.4 = ((bf16[8,32,512]{2,1,0:T(8,128)(2,1)}), bf16[8,32,512]{2,1,0:T(8,128)(2,1)S(1)}, u32[]{:S(2)}, u32[]{:S(2)}) async-start(bf16[8,32,512]{2,1,0:T(8,128)(2,1)} %get-tuple-element.28), calls=%async_computation.4 | async-start | bytes 524288 | tf_op jit(solution)/shard_map/all_to_all | solution.py:207
  91.9 0.8 shard_map.83
  92.6 6.8 %collective-permute-start.7 = (bf16[2,256,512]{2,1,0:T(8,128)(2,1)S(1)}, bf16[2,256,512]{2,1,0:T(8,128)(2,1)S(1)}, u32[]{:S(2)}, u32[]{:S(2)}) collective-permute-start(bf16[2,256,512]{2,1,0:T(8,128)(2,1)S(1)} %get-tuple-element.25), channel_id=1, source_target_pairs={{0,8},{8,0},{1,9},{9,1},{2,10},{10,2},{3,11},{11,3},{4,12},{12,4},... | collective-permute-start | bytes 1572872 | tf_op jit(solution)/shard_map/ppermute | solution.py:203
  99.5 1.5 %collective-permute-done.7.came = bf16[2,256,512]{2,1,0:T(8,128)(2,1)S(1)} collective-permute-done((bf16[2,256,512]{2,1,0:T(8,128)(2,1)S(1)}, bf16[2,256,512]{2,1,0:T(8,128)(2,1)S(1)}, u32[]{:S(2)}, u32[]{:S(2)}) %collective-permute-start.7) | collective-permute-done | bytes 524320 | tf_op jit(solution)/shard_map/ppermute | solution.py:203
  101.0 0.1 shard_map.84
  101.1 3.5 %collective-permute-start.8 = (bf16[256,512]{1,0:T(8,128)(2,1)S(1)}, bf16[256,512]{1,0:T(8,128)(2,1)S(1)}, u32[]{:S(2)}, u32[]{:S(2)}) collective-permute-start(bf16[256,512]{1,0:T(8,128)(2,1)S(1)} %get-tuple-element.27), channel_id=1, source_target_pairs={{0,256},{256,0},{1,257},{257,1},{2,258},{258,2},{3,259},{259,3},{4... | collective-permute-start | bytes 786440 | tf_op jit(solution)/shard_map/ppermute | solution.py:203
  104.6 7.4 %collective-permute-done.8.came = bf16[256,512]{1,0:T(8,128)(2,1)S(1)} collective-permute-done((bf16[256,512]{1,0:T(8,128)(2,1)S(1)}, bf16[256,512]{1,0:T(8,128)(2,1)S(1)}, u32[]{:S(2)}, u32[]{:S(2)}) %collective-permute-start.8) | collective-permute-done | bytes 262176 | tf_op jit(solution)/shard_map/ppermute | solution.py:203
  112.0 0.0 all-to-all-done.4.q_came
  112.0 0.7 shard_map.85
  (6 shorter events, 0.1 us)
Async XLA Ops:
  2.5 23.3 %collective-permute-start = (bf16[256,512]{1,0:T(8,128)(2,1)}, bf16[256,512]{1,0:T(8,128)(2,1)S(1)}, u32[]{:S(2)}, u32[]{:S(2)}) collective-permute-start(bf16[256,512]{1,0:T(8,128)(2,1)} %get-tuple-element.17.first), channel_id=1, source_target_pairs={{0,16},{16,0},{1,17},{17,1},{2,18},{18,2},{3,19},{19,3},{4,20},{20... | collective-permute-start | bytes 786440 | tf_op jit(solution)/shard_map/ppermute | solution.py:203
  6.9 24.6 %collective-permute-start.2 = (bf16[256,512]{1,0:T(8,128)(2,1)}, bf16[256,512]{1,0:T(8,128)(2,1)S(1)}, u32[]{:S(2)}, u32[]{:S(2)}) collective-permute-start(bf16[256,512]{1,0:T(8,128)(2,1)} %get-tuple-element.17.first), channel_id=1, source_target_pairs={{0,256},{256,0},{1,257},{257,1},{2,258},{258,2},{3,259},{259,3},{4... | collective-permute-start | bytes 786440 | tf_op jit(solution)/shard_map/ppermute | solution.py:203
  11.7 16.0 %copy-start = (bf16[256,512]{1,0:T(8,128)(2,1)S(1)}, bf16[256,512]{1,0:T(8,128)(2,1)}, u32[]{:S(2)}) copy-start(bf16[256,512]{1,0:T(8,128)(2,1)} %get-tuple-element.17.first) | copy-start | bytes 786436
  11.7 30.6 %all-to-all-start = ((bf16[8,144,128]{2,1,0:T(8,128)(2,1)}), bf16[8,144,128]{2,1,0:T(8,128)(2,1)S(1)}, u32[]{:S(2)}, u32[]{:S(2)}) async-start(bf16[8,144,128]{2,1,0:T(8,128)(2,1)} %get-tuple-element.16), calls=%async_computation | async-start | bytes 589824 | tf_op jit(solution)/shard_map/all_to_all | solution.py:207
  25.8 9.7 %collective-permute-start.3 = (bf16[256,512]{1,0:T(8,128)(2,1)S(1)}, bf16[256,512]{1,0:T(8,128)(2,1)S(1)}, u32[]{:S(2)}, u32[]{:S(2)}) collective-permute-start(bf16[256,512]{1,0:T(8,128)(2,1)S(1)} %collective-permute-done.second), channel_id=1, source_target_pairs={{0,256},{256,0},{1,257},{257,1},{2,258},{258,2},{3,259},{259,3},{4... | collective-permute-start | bytes 786440 | tf_op jit(solution)/shard_map/ppermute | solution.py:203
  27.8 17.2 %collective-permute-start.1 = (bf16[512,512]{1,0:T(8,128)(2,1)S(1)}, bf16[512,512]{1,0:T(8,128)(2,1)S(1)}, u32[]{:S(2)}, u32[]{:S(2)}) collective-permute-start(bf16[512,512]{1,0:T(8,128)(2,1)S(1)} %shard_map.77.refs_0_), channel_id=1, source_target_pairs={{0,8},{8,0},{1,9},{9,1},{2,10},{10,2},{3,11},{11,3},{4,12},{12,4},... | collective-permute-start | bytes 1572872 | tf_op jit(solution)/shard_map/ppermute | solution.py:203
  35.5 9.5 %collective-permute-start.4 = (bf16[512,512]{1,0:T(8,128)(2,1)S(1)}, bf16[512,512]{1,0:T(8,128)(2,1)S(1)}, u32[]{:S(2)}, u32[]{:S(2)}) collective-permute-start(bf16[512,512]{1,0:T(8,128)(2,1)S(1)} %shard_map.78.refs_2_), channel_id=1, source_target_pairs={{0,8},{8,0},{1,9},{9,1},{2,10},{10,2},{3,11},{11,3},{4,12},{12,4},... | collective-permute-start | bytes 1572872 | tf_op jit(solution)/shard_map/ppermute | solution.py:203
  42.3 13.9 %collective-permute-start.5 = (bf16[8,144,128]{2,1,0:T(8,128)(2,1)S(1)}, bf16[8,144,128]{2,1,0:T(8,128)(2,1)S(1)}, u32[]{:S(2)}, u32[]{:S(2)}) collective-permute-start(bf16[8,144,128]{2,1,0:T(8,128)(2,1)S(1)} %all-to-all-done.near), channel_id=1, source_target_pairs={{0,16},{16,0},{1,17},{17,1},{2,18},{18,2},{3,19},{19,3},{4,20},{20... | collective-permute-start | bytes 884744 | tf_op jit(solution)/shard_map/ppermute | solution.py:203
  65.9 21.0 %all-to-all-start.3 = ((f32[16,8,128]{2,1,0:T(8,128)}), f32[16,8,128]{2,1,0:T(8,128)S(1)}, u32[]{:S(2)}, u32[]{:S(2)}) async-start(f32[16,8,128]{2,1,0:T(8,128)} %get-tuple-element.19), calls=%async_computation.3 | async-start | bytes 131072 | tf_op jit(solution)/shard_map/all_to_all | solution.py:207
  75.1 16.7 %collective-permute-start.6 = (f32[4,72,128]{2,1,0:T(8,128)S(1)}, f32[4,72,128]{2,1,0:T(8,128)S(1)}, u32[]{:S(2)}, u32[]{:S(2)}) collective-permute-start(f32[4,72,128]{2,1,0:T(8,128)S(1)} %get-tuple-element.23), channel_id=1, source_target_pairs={{0,16},{16,0},{1,17},{17,1},{2,18},{18,2},{3,19},{19,3},{4,20},{20... | collective-permute-start | bytes 442376 | tf_op jit(solution)/shard_map/ppermute | solution.py:203
  88.4 23.6 %all-to-all-start.4 = ((bf16[8,32,512]{2,1,0:T(8,128)(2,1)}), bf16[8,32,512]{2,1,0:T(8,128)(2,1)S(1)}, u32[]{:S(2)}, u32[]{:S(2)}) async-start(bf16[8,32,512]{2,1,0:T(8,128)(2,1)} %get-tuple-element.28), calls=%async_computation.4 | async-start | bytes 524288 | tf_op jit(solution)/shard_map/all_to_all | solution.py:207
  92.6 8.3 %collective-permute-start.7 = (bf16[2,256,512]{2,1,0:T(8,128)(2,1)S(1)}, bf16[2,256,512]{2,1,0:T(8,128)(2,1)S(1)}, u32[]{:S(2)}, u32[]{:S(2)}) collective-permute-start(bf16[2,256,512]{2,1,0:T(8,128)(2,1)S(1)} %get-tuple-element.25), channel_id=1, source_target_pairs={{0,8},{8,0},{1,9},{9,1},{2,10},{10,2},{3,11},{11,3},{4,12},{12,4},... | collective-permute-start | bytes 1572872 | tf_op jit(solution)/shard_map/ppermute | solution.py:203
  101.1 10.9 %collective-permute-start.8 = (bf16[256,512]{1,0:T(8,128)(2,1)S(1)}, bf16[256,512]{1,0:T(8,128)(2,1)S(1)}, u32[]{:S(2)}, u32[]{:S(2)}) collective-permute-start(bf16[256,512]{1,0:T(8,128)(2,1)S(1)} %get-tuple-element.27), channel_id=1, source_target_pairs={{0,256},{256,0},{1,257},{257,1},{2,258},{258,2},{3,259},{259,3},{4... | collective-permute-start | bytes 786440 | tf_op jit(solution)/shard_map/ppermute | solution.py:203

commit v13 on v12

--- a/solution.py
+++ b/solution.py
@@ -114,7 +114,7 @@
         sent[i] = total
 
 
-def stat_kernel(scores, sent, cross):
+def stat_kernel(scores, sent, cross, tops):
     cross[...] = scores[4:8]
     for l in range(2):
         batch = [scores[h * 2 + l, 0:64, :] for h in range(4)]
@@ -125,6 +125,7 @@
         )
         total = jnp.sum(sum(jnp.exp(b - top) for b in batch), axis=0, keepdims=True)
         total = total + jnp.sum(sum(jnp.exp(h - top) for h in hard), axis=0, keepdims=True)
+        tops[:, l * 128 : (l + 1) * 128] = top
         for to in range(NZ):
             sent[to, l : l + 1, :] = top
             sent[to, 2 + l : 3 + l, :] = total
@@ -142,45 +143,71 @@
     return jnp.concatenate(logs, axis=1)
 
 
-def block_weights(scores, o, logs, want, targets):
+def is_target():
+    row = lax.broadcasted_iota(jnp.int32, (32, ROWS), 0)
+    lane = lax.broadcasted_iota(jnp.int32, (32, ROWS), 1)
+    return lane == lax.axis_index("zh") * 32 + row
+
+
+def batch_scores(scores, o):
     h, a = o // 2, o % 2
-    batch = jnp.concatenate([scores[h * 2 + l, a * 32 : (a + 1) * 32, :] for l in range(2)], axis=1)
+    return jnp.concatenate([scores[h * 2 + l, a * 32 : (a + 1) * 32, :] for l in range(2)], axis=1)
+
+
+def block_weights(scores, o, logs, want, target):
+    h, a = o // 2, o % 2
     hard = jnp.concatenate([scores[h * 2 + l, 64 + a : 65 + a, :] for l in range(2)], axis=1)
-    weights = jnp.exp(batch - logs)
-    if targets and o == 0:
-        row = lax.broadcasted_iota(jnp.int32, (32, ROWS), 0)
-        lane = lax.broadcasted_iota(jnp.int32, (32, ROWS), 1)
-        weights = weights - (lane == lax.axis_index("zh") * 32 + row).astype(F32)
+    weights = jnp.exp(batch_scores(scores, o) - logs)
+    if target is not None and o == 0:
+        weights = jnp.where(is_target(), target(weights), weights)
     line = lax.broadcasted_iota(jnp.int32, (224, ROWS), 0)
     hard = jnp.where(line == want, jnp.exp(hard - logs), 0.0)
     return jnp.concatenate([weights.astype(BF16), hard.astype(BF16)], axis=0)
 
 
-def share_kernel(stats, scores, asked, *refs):
-    columns, (sent, logs, total) = refs[:4], refs[4:]
-    zp = lax.axis_index("zp")
-    near = row_logs(stats, zp)
-    logs[0:1, :] = near
-    logs[1:2, :] = row_logs(stats, 1 - zp)
+def share_kernel(tops, scores, asked, *refs):
+    columns, (total,) = refs[:4], refs[4:]
     for o in range(NB):
-        weights = block_weights(scores, o, near, asked[o : o + 1, :], True)
+        weights = block_weights(scores, o, tops[...], asked[o : o + 1, :], jnp.zeros_like)
         cols = columns[o % 4][o // 4 * 256 : (o // 4 + 1) * 256, :]
         term = lax.dot_general(weights, cols, (((0,), (0,)), ((), ())), preferred_element_type=F32)
         if o == 0:
             total[...] = term
-        elif o < NB - 1:
+        else:
             total[...] += term
-        else:
-            sent[...] = (total[...] + term).astype(BF16).reshape(NH, 32, 512)
-
-
-def column_grad_kernel(logs, scores, asked, queries, far_scores, far, keep, give, far_queries, far_asked):
+
+
+def scale_kernel(stats, tops, scores, total, own, sent, logs, turned):
+    zh, zp = lax.axis_index("zh"), lax.axis_index("zp")
+    near = row_logs(stats, zp)
+    logs[0:1, :] = near
+    logs[1:2, :] = row_logs(stats, 1 - zp)
+    factors = jnp.exp(tops[...] - near)
+    at_target = jnp.exp(batch_scores(scores, 0) - near) - 1.0
+    at_target = jnp.sum(jnp.where(is_target(), at_target, 0.0), axis=0, keepdims=True)
+    at_target = at_target.astype(BF16).astype(F32)
+    for l in range(2):
+        lanes = slice(l * 128, (l + 1) * 128)
+        both = jnp.concatenate([factors[:, lanes], at_target[:, lanes], jnp.zeros((126, 128), F32)], axis=0)
+        turned[lanes, :] = both.T
+        part = total[lanes, :] * turned[lanes, 0:1]
+        sent[l * 4 : (l + 1) * 4] = part.astype(BF16).reshape(4, 32, 512)
+    mine = pl.ds(pl.multiple_of(zh * 32, 32), 32)
+    part = total[mine, :] * turned[mine, 0:1] + own[0:32, :].astype(F32) * turned[mine, 1:2]
+    sent[zh] = part.astype(BF16)
+
+
+def column_grad_kernel(came, logs, scores, asked, queries, far, keep, give, far_queries, far_asked, far_scores, sem):
+    copy = pltpu.make_async_copy(came, far_scores, sem)
+    copy.start()
     unpack(far, slice(4, 8), far_queries, far_asked)
     near_queries, other_queries = queries[...], far_queries[...]
     for o in range(4):
-        weights = block_weights(scores, o, logs[0:1, :], asked[o : o + 1, :], True)
+        weights = block_weights(scores, o, logs[0:1, :], asked[o : o + 1, :], lambda w: w - 1.0)
         grad = jnp.dot(weights, near_queries, preferred_element_type=F32)
-        weights = block_weights(far_scores, o, logs[1:2, :], far_asked[o : o + 1, :], False)
+        if o == 0:
+            copy.wait()
+        weights = block_weights(far_scores, o, logs[1:2, :], far_asked[o : o + 1, :], None)
         grad = grad + jnp.dot(weights, other_queries, preferred_element_type=F32)
         (give if o % 2 else keep)[o // 2] = grad.astype(BF16)
 
@@ -227,18 +254,24 @@
     far = swap(near, "zp")
     (summed,) = call(add_kernel, [((8, 72, 128), F32)], exchange(parts, ("yl", "x")), far)
     scores = exchange(summed, ("yl", "x"))
-    stats, cross = call(stat_kernel, [((NZ, 8, 128), F32), ((4, 72, 128), F32)], scores)
+    stats, cross, tops = call(
+        stat_kernel, [((NZ, 8, 128), F32), ((4, 72, 128), F32), ((1, ROWS), F32)], scores
+    )
     stats = exchange(stats, ("zh", "zp")).reshape(NH, 2, 8, 128)
     far_scores = swap(cross, "zp")
+    (total,) = call(share_kernel, [((ROWS, 512), F32)], tops, scores, asked, *columns)
     q_part, logs = call(
-        share_kernel, [((NH, 32, 512), BF16), ((8, ROWS), F32)], stats, scores, asked, *columns,
-        scratch=[pltpu.VMEM((ROWS, 512), F32)],
+        scale_kernel, [((NH, 32, 512), BF16), ((8, ROWS), F32)], stats, tops, scores, total, pair,
+        scratch=[pltpu.VMEM((ROWS, 128), F32)],
     )
     q_came = exchange(q_part, "zh")
     keep, give = call(
         column_grad_kernel, [((2, 256, 512), BF16), ((2, 256, 512), BF16)],
-        logs, scores, asked, queries, far_scores, far,
-        scratch=[pltpu.VMEM((ROWS, 512), BF16), pltpu.VMEM((4, ROWS), jnp.int32)],
+        far_scores, logs, scores, asked, queries, far, hbm=1,
+        scratch=[
+            pltpu.VMEM((ROWS, 512), BF16), pltpu.VMEM((4, ROWS), jnp.int32), pltpu.VMEM((4, 72, 128), F32),
+            pltpu.SemaphoreType.DMA,
+        ],
     )
     own, cross = call(pair_kernel, [((256, 512), F32), ((256, 512), BF16)], keep, swap(give, "c"))
     cross = swap(cross, "yh")

time: 114 us -> 114 us (level)
    pallas_call x10 -> x11, Pallas kernels: 6.58 us -> 7.64 us  [call(): pl.pallas_call(kernel, out_shape=[jax.ShapeDtypeStruct(shape, dtype) for...]
  transfers between devices with their start and end apart: 12 -> 12, of which waited for: 5 -> 5; matrix products, arithmetic and copies ran while one was open for 0% -> 0% of each run, Pallas kernels for 3% -> 4%
where the time goes in v13:
time: 114 us; the launch traced here: 113 us
  starting transfers between devices  62.2 us (55%)
  waiting for transfers between devices  23 us (20%)
  blocking collectives  19.3 us (17%)
  Pallas kernels  7.64 us (7%)
    ppermute x9, starting transfers between devices, swap(): return lax.ppermute(x, axis, [(0, 1), (1, 0)])  35.5 us
    all_to_all x3, starting transfers between devices, exchange(): return lax.all_to_all(x, axes, split_axis=0, concat_axis=0, tiled=True)  26.7 us
    all_to_all x2, blocking collectives, exchange(): return lax.all_to_all(x, axes, split_axis=0, concat_axis=0, tiled=True)  19.3 us
    ppermute x9, waiting for transfers between devices, swap(): return lax.ppermute(x, axis, [(0, 1), (1, 0)])  12.9 us
    all_to_all x3, waiting for transfers between devices, exchange(): return lax.all_to_all(x, axes, split_axis=0, concat_axis=0, tiled=True)  10.1 us
    pallas_call x11, Pallas kernels, call(): pl.pallas_call(kernel, out_shape=[jax.ShapeDtypeStruct(shape, dtype) for...  7.64 us
  transfers between devices with their start and end apart: 12, of which 5 were waited for; matrix products, arithmetic and copies ran while one was open for 0% of the time, Pallas kernels for 4%

profile of v13, /device:TPU:1, one launch (start us, length us, event | category | flops | bytes accessed | tf_op | source)
XLA Modules:
  0.0 113.0 jit_solution(16993995259330572742)
XLA Ops:
  0.6 1.8 %shard_map.76 = (bf16[8,144,128]{2,1,0:T(8,128)(2,1)}, bf16[256,512]{1,0:T(8,128)(2,1)}) custom-call(bf16[32,512]{1,0:T(8,128)(2,1)} %queries.1, s32[7,32]{1,0:T(8,128)} %bitcast.4, s32[7,32]{1,0:T(8,128)} %bitcast.5, bf16[224,512]{1,0:T(8,128)(2,1)} %negatives.1, bf16[32,512]{1,0:T(8,128)(2,1)} %passages.1), custom_call_target="tpu_custom_call" | custom-call | tf_op jit(solution)/shard_map/pallas_call | solution.py:26
  2.5 4.4 %collective-permute-start = (bf16[256,512]{1,0:T(8,128)(2,1)}, bf16[256,512]{1,0:T(8,128)(2,1)S(1)}, u32[]{:S(2)}, u32[]{:S(2)}) collective-permute-start(bf16[256,512]{1,0:T(8,128)(2,1)} %get-tuple-element.18.first), channel_id=1, source_target_pairs={{0,16},{16,0},{1,17},{17,1},{2,18},{18,2},{3,19},{19,3},{4,20},{20... | collective-permute-start | bytes 786440 | tf_op jit(solution)/shard_map/ppermute | solution.py:230
  6.9 4.8 %collective-permute-start.2 = (bf16[256,512]{1,0:T(8,128)(2,1)}, bf16[256,512]{1,0:T(8,128)(2,1)S(1)}, u32[]{:S(2)}, u32[]{:S(2)}) collective-permute-start(bf16[256,512]{1,0:T(8,128)(2,1)} %get-tuple-element.18.first), channel_id=1, source_target_pairs={{0,256},{256,0},{1,257},{257,1},{2,258},{258,2},{3,259},{259,3},{4... | collective-permute-start | bytes 786440 | tf_op jit(solution)/shard_map/ppermute | solution.py:230
  11.7 14.1 %all-to-all-start = ((bf16[8,144,128]{2,1,0:T(8,128)(2,1)}), bf16[8,144,128]{2,1,0:T(8,128)(2,1)S(1)}, u32[]{:S(2)}, u32[]{:S(2)}) async-start(bf16[8,144,128]{2,1,0:T(8,128)(2,1)} %get-tuple-element.17), calls=%async_computation | async-start | bytes 589824 | tf_op jit(solution)/shard_map/all_to_all | solution.py:234
  25.8 0.0 collective-permute-done.second
  25.8 2.0 %collective-permute-start.3 = (bf16[256,512]{1,0:T(8,128)(2,1)S(1)}, bf16[256,512]{1,0:T(8,128)(2,1)S(1)}, u32[]{:S(2)}, u32[]{:S(2)}) collective-permute-start(bf16[256,512]{1,0:T(8,128)(2,1)S(1)} %collective-permute-done.second), channel_id=1, source_target_pairs={{0,256},{256,0},{1,257},{257,1},{2,258},{258,2},{3,259},{259,3},{4... | collective-permute-start | bytes 786440 | tf_op jit(solution)/shard_map/ppermute | solution.py:230
  27.8 3.7 %collective-permute-start.1 = (bf16[512,512]{1,0:T(8,128)(2,1)S(1)}, bf16[512,512]{1,0:T(8,128)(2,1)S(1)}, u32[]{:S(2)}, u32[]{:S(2)}) collective-permute-start(bf16[512,512]{1,0:T(8,128)(2,1)S(1)} %shard_map.77.refs_0_.own), channel_id=1, source_target_pairs={{0,8},{8,0},{1,9},{9,1},{2,10},{10,2},{3,11},{11,3},{4,12},{12,4},... | collective-permute-start | bytes 1572872 | tf_op jit(solution)/shard_map/ppermute | solution.py:230
  31.5 0.0 collective-permute-done.2.first
  31.5 3.9 %collective-permute-done.3.second = bf16[256,512]{1,0:T(8,128)(2,1)S(1)} collective-permute-done((bf16[256,512]{1,0:T(8,128)(2,1)S(1)}, bf16[256,512]{1,0:T(8,128)(2,1)S(1)}, u32[]{:S(2)}, u32[]{:S(2)}) %collective-permute-start.3) | collective-permute-done | bytes 262176 | tf_op jit(solution)/shard_map/ppermute | solution.py:230
  35.5 4.3 %collective-permute-start.4 = (bf16[512,512]{1,0:T(8,128)(2,1)S(1)}, bf16[512,512]{1,0:T(8,128)(2,1)S(1)}, u32[]{:S(2)}, u32[]{:S(2)}) collective-permute-start(bf16[512,512]{1,0:T(8,128)(2,1)S(1)} %shard_map.78.refs_2_), channel_id=1, source_target_pairs={{0,8},{8,0},{1,9},{9,1},{2,10},{10,2},{3,11},{11,3},{4,12},{12,4},... | collective-permute-start | bytes 1572872 | tf_op jit(solution)/shard_map/ppermute | solution.py:230
  39.8 2.5 %all-to-all-done.near = bf16[8,144,128]{2,1,0:T(8,128)(2,1)S(1)} async-done(((bf16[8,144,128]{2,1,0:T(8,128)(2,1)}), bf16[8,144,128]{2,1,0:T(8,128)(2,1)S(1)}, u32[]{:S(2)}, u32[]{:S(2)}) %all-to-all-start) | async-done | bytes 294944 | tf_op jit(solution)/shard_map/all_to_all | solution.py:234
  42.3 2.7 %collective-permute-start.5 = (bf16[8,144,128]{2,1,0:T(8,128)(2,1)S(1)}, bf16[8,144,128]{2,1,0:T(8,128)(2,1)S(1)}, u32[]{:S(2)}, u32[]{:S(2)}) collective-permute-start(bf16[8,144,128]{2,1,0:T(8,128)(2,1)S(1)} %all-to-all-done.near), channel_id=1, source_target_pairs={{0,16},{16,0},{1,17},{17,1},{2,18},{18,2},{3,19},{19,3},{4,20},{20... | collective-permute-start | bytes 884744 | tf_op jit(solution)/shard_map/ppermute | solution.py:230
  45.0 0.0 collective-permute-done.1.refs_1_
  45.0 0.0 collective-permute-done.4.refs_3_
  45.0 0.8 shard_map.79
  45.8 10.4 %all_to_all.25.came = f32[8,72,128]{2,1,0:T(8,128)S(1)} all-to-all(f32[8,72,128]{2,1,0:T(8,128)S(1)} %get-tuple-element.19), channel_id=1, replica_groups=mesh['yh'=2,'zh'=8,'zp'=2,'c'=2,'yl'=2,'x'=4] {'yl','x'}, dimensions={0} | all-to-all | bytes 589824 | tf_op jit(solution)/shard_map/all_to_all | solution.py:234
  56.3 0.0 collective-permute-done.5.far
  56.3 8.9 %all_to_all.26.scores = f32[8,72,128]{2,1,0:T(8,128)S(1)} all-to-all(f32[8,72,128]{2,1,0:T(8,128)S(1)} %shard_map.80), channel_id=1, replica_groups=mesh['yh'=2,'zh'=8,'zp'=2,'c'=2,'yl'=2,'x'=4] {'yl','x'}, dimensions={0} | all-to-all | bytes 589824 | tf_op jit(solution)/shard_map/all_to_all | solution.py:234
  65.2 0.7 shard_map.81
  65.9 9.2 %all-to-all-start.3 = ((f32[16,8,128]{2,1,0:T(8,128)}), f32[16,8,128]{2,1,0:T(8,128)S(1)}, u32[]{:S(2)}, u32[]{:S(2)}) async-start(f32[16,8,128]{2,1,0:T(8,128)} %get-tuple-element.21), calls=%async_computation.3 | async-start | bytes 131072 | tf_op jit(solution)/shard_map/all_to_all | solution.py:234
  75.1 3.3 %collective-permute-start.6 = (f32[4,72,128]{2,1,0:T(8,128)}, f32[4,72,128]{2,1,0:T(8,128)}, u32[]{:S(2)}, u32[]{:S(2)}) collective-permute-start(f32[4,72,128]{2,1,0:T(8,128)} %get-tuple-element.20), channel_id=1, source_target_pairs={{0,16},{16,0},{1,17},{17,1},{2,18},{18,2},{3,19},{19,3},{4,20},{20... | collective-permute-start | bytes 442376 | tf_op jit(solution)/shard_map/ppermute | solution.py:230
  78.4 0.7 shard_map.82.total
  79.2 7.6 %all-to-all-done.3 = f32[16,8,128]{2,1,0:T(8,128)S(1)} async-done(((f32[16,8,128]{2,1,0:T(8,128)}), f32[16,8,128]{2,1,0:T(8,128)S(1)}, u32[]{:S(2)}, u32[]{:S(2)}) %all-to-all-start.3) | async-done | bytes 65568 | tf_op jit(solution)/shard_map/all_to_all | solution.py:234
  86.8 1.0 shard_map.83
  87.8 3.4 %all-to-all-start.4 = ((bf16[8,32,512]{2,1,0:T(8,128)(2,1)}), bf16[8,32,512]{2,1,0:T(8,128)(2,1)S(1)}, u32[]{:S(2)}, u32[]{:S(2)}) async-start(bf16[8,32,512]{2,1,0:T(8,128)(2,1)} %get-tuple-element.30), calls=%async_computation.4 | async-start | bytes 524288 | tf_op jit(solution)/shard_map/all_to_all | solution.py:234
  91.2 1.6 %shard_map.84 = (bf16[2,256,512]{2,1,0:T(8,128)(2,1)S(1)}, bf16[2,256,512]{2,1,0:T(8,128)(2,1)S(1)}) custom-call(f32[4,72,128]{2,1,0:T(8,128)} %collective-permute-done.6.came, f32[8,256]{1,0:T(8,128)S(1)} %get-tuple-element.24.logs, f32[8,72,128]{2,1,0:T(8,128)S(1)} %all_to_all.26.scores, s32[8,256]{1,0:T(8,128)S(1)} %get-tuple-element.23.asked, ...), custom_call_target="tpu_custom_call" | custom-call | tf_op jit(solution)/shard_map/pallas_call | solution.py:26
  92.8 6.8 %collective-permute-start.7 = (bf16[2,256,512]{2,1,0:T(8,128)(2,1)S(1)}, bf16[2,256,512]{2,1,0:T(8,128)(2,1)S(1)}, u32[]{:S(2)}, u32[]{:S(2)}) collective-permute-start(bf16[2,256,512]{2,1,0:T(8,128)(2,1)S(1)} %get-tuple-element.27), channel_id=1, source_target_pairs={{0,8},{8,0},{1,9},{9,1},{2,10},{10,2},{3,11},{11,3},{4,12},{12,4},... | collective-permute-start | bytes 1572872 | tf_op jit(solution)/shard_map/ppermute | solution.py:230
  99.7 1.5 %collective-permute-done.7.came = bf16[2,256,512]{2,1,0:T(8,128)(2,1)S(1)} collective-permute-done((bf16[2,256,512]{2,1,0:T(8,128)(2,1)S(1)}, bf16[2,256,512]{2,1,0:T(8,128)(2,1)S(1)}, u32[]{:S(2)}, u32[]{:S(2)}) %collective-permute-start.7) | collective-permute-done | bytes 524320 | tf_op jit(solution)/shard_map/ppermute | solution.py:230
  101.2 0.1 shard_map.85
  101.3 3.5 %collective-permute-start.8 = (bf16[256,512]{1,0:T(8,128)(2,1)S(1)}, bf16[256,512]{1,0:T(8,128)(2,1)S(1)}, u32[]{:S(2)}, u32[]{:S(2)}) collective-permute-start(bf16[256,512]{1,0:T(8,128)(2,1)S(1)} %get-tuple-element.29), channel_id=1, source_target_pairs={{0,256},{256,0},{1,257},{257,1},{2,258},{258,2},{3,259},{259,3},{4... | collective-permute-start | bytes 786440 | tf_op jit(solution)/shard_map/ppermute | solution.py:230
  104.8 7.4 %collective-permute-done.8.came = bf16[256,512]{1,0:T(8,128)(2,1)S(1)} collective-permute-done((bf16[256,512]{1,0:T(8,128)(2,1)S(1)}, bf16[256,512]{1,0:T(8,128)(2,1)S(1)}, u32[]{:S(2)}, u32[]{:S(2)}) %collective-permute-start.8) | collective-permute-done | bytes 262176 | tf_op jit(solution)/shard_map/ppermute | solution.py:230
  112.2 0.7 shard_map.86
  (7 shorter events, 0.1 us)
Async XLA Ops:
  2.5 23.3 %collective-permute-start = (bf16[256,512]{1,0:T(8,128)(2,1)}, bf16[256,512]{1,0:T(8,128)(2,1)S(1)}, u32[]{:S(2)}, u32[]{:S(2)}) collective-permute-start(bf16[256,512]{1,0:T(8,128)(2,1)} %get-tuple-element.18.first), channel_id=1, source_target_pairs={{0,16},{16,0},{1,17},{17,1},{2,18},{18,2},{3,19},{19,3},{4,20},{20... | collective-permute-start | bytes 786440 | tf_op jit(solution)/shard_map/ppermute | solution.py:230
  6.9 24.6 %collective-permute-start.2 = (bf16[256,512]{1,0:T(8,128)(2,1)}, bf16[256,512]{1,0:T(8,128)(2,1)S(1)}, u32[]{:S(2)}, u32[]{:S(2)}) collective-permute-start(bf16[256,512]{1,0:T(8,128)(2,1)} %get-tuple-element.18.first), channel_id=1, source_target_pairs={{0,256},{256,0},{1,257},{257,1},{2,258},{258,2},{3,259},{259,3},{4... | collective-permute-start | bytes 786440 | tf_op jit(solution)/shard_map/ppermute | solution.py:230
  11.7 16.0 %copy-start = (bf16[256,512]{1,0:T(8,128)(2,1)S(1)}, bf16[256,512]{1,0:T(8,128)(2,1)}, u32[]{:S(2)}) copy-start(bf16[256,512]{1,0:T(8,128)(2,1)} %get-tuple-element.18.first) | copy-start | bytes 786436
  11.7 30.6 %all-to-all-start = ((bf16[8,144,128]{2,1,0:T(8,128)(2,1)}), bf16[8,144,128]{2,1,0:T(8,128)(2,1)S(1)}, u32[]{:S(2)}, u32[]{:S(2)}) async-start(bf16[8,144,128]{2,1,0:T(8,128)(2,1)} %get-tuple-element.17), calls=%async_computation | async-start | bytes 589824 | tf_op jit(solution)/shard_map/all_to_all | solution.py:234
  25.8 9.7 %collective-permute-start.3 = (bf16[256,512]{1,0:T(8,128)(2,1)S(1)}, bf16[256,512]{1,0:T(8,128)(2,1)S(1)}, u32[]{:S(2)}, u32[]{:S(2)}) collective-permute-start(bf16[256,512]{1,0:T(8,128)(2,1)S(1)} %collective-permute-done.second), channel_id=1, source_target_pairs={{0,256},{256,0},{1,257},{257,1},{2,258},{258,2},{3,259},{259,3},{4... | collective-permute-start | bytes 786440 | tf_op jit(solution)/shard_map/ppermute | solution.py:230
  27.8 17.2 %collective-permute-start.1 = (bf16[512,512]{1,0:T(8,128)(2,1)S(1)}, bf16[512,512]{1,0:T(8,128)(2,1)S(1)}, u32[]{:S(2)}, u32[]{:S(2)}) collective-permute-start(bf16[512,512]{1,0:T(8,128)(2,1)S(1)} %shard_map.77.refs_0_.own), channel_id=1, source_target_pairs={{0,8},{8,0},{1,9},{9,1},{2,10},{10,2},{3,11},{11,3},{4,12},{12,4},... | collective-permute-start | bytes 1572872 | tf_op jit(solution)/shard_map/ppermute | solution.py:230
  35.5 9.5 %collective-permute-start.4 = (bf16[512,512]{1,0:T(8,128)(2,1)S(1)}, bf16[512,512]{1,0:T(8,128)(2,1)S(1)}, u32[]{:S(2)}, u32[]{:S(2)}) collective-permute-start(bf16[512,512]{1,0:T(8,128)(2,1)S(1)} %shard_map.78.refs_2_), channel_id=1, source_target_pairs={{0,8},{8,0},{1,9},{9,1},{2,10},{10,2},{3,11},{11,3},{4,12},{12,4},... | collective-permute-start | bytes 1572872 | tf_op jit(solution)/shard_map/ppermute | solution.py:230
  42.3 13.9 %collective-permute-start.5 = (bf16[8,144,128]{2,1,0:T(8,128)(2,1)S(1)}, bf16[8,144,128]{2,1,0:T(8,128)(2,1)S(1)}, u32[]{:S(2)}, u32[]{:S(2)}) collective-permute-start(bf16[8,144,128]{2,1,0:T(8,128)(2,1)S(1)} %all-to-all-done.near), channel_id=1, source_target_pairs={{0,16},{16,0},{1,17},{17,1},{2,18},{18,2},{3,19},{19,3},{4,20},{20... | collective-permute-start | bytes 884744 | tf_op jit(solution)/shard_map/ppermute | solution.py:230
  65.9 20.9 %all-to-all-start.3 = ((f32[16,8,128]{2,1,0:T(8,128)}), f32[16,8,128]{2,1,0:T(8,128)S(1)}, u32[]{:S(2)}, u32[]{:S(2)}) async-start(f32[16,8,128]{2,1,0:T(8,128)} %get-tuple-element.21), calls=%async_computation.3 | async-start | bytes 131072 | tf_op jit(solution)/shard_map/all_to_all | solution.py:234
  75.1 16.0 %collective-permute-start.6 = (f32[4,72,128]{2,1,0:T(8,128)}, f32[4,72,128]{2,1,0:T(8,128)}, u32[]{:S(2)}, u32[]{:S(2)}) collective-permute-start(f32[4,72,128]{2,1,0:T(8,128)} %get-tuple-element.20), channel_id=1, source_target_pairs={{0,16},{16,0},{1,17},{17,1},{2,18},{18,2},{3,19},{19,3},{4,20},{20... | collective-permute-start | bytes 442376 | tf_op jit(solution)/shard_map/ppermute | solution.py:230
  87.8 24.5 %all-to-all-start.4 = ((bf16[8,32,512]{2,1,0:T(8,128)(2,1)}), bf16[8,32,512]{2,1,0:T(8,128)(2,1)S(1)}, u32[]{:S(2)}, u32[]{:S(2)}) async-start(bf16[8,32,512]{2,1,0:T(8,128)(2,1)} %get-tuple-element.30), calls=%async_computation.4 | async-start | bytes 524288 | tf_op jit(solution)/shard_map/all_to_all | solution.py:234
  92.8 8.4 %collective-permute-start.7 = (bf16[2,256,512]{2,1,0:T(8,128)(2,1)S(1)}, bf16[2,256,512]{2,1,0:T(8,128)(2,1)S(1)}, u32[]{:S(2)}, u32[]{:S(2)}) collective-permute-start(bf16[2,256,512]{2,1,0:T(8,128)(2,1)S(1)} %get-tuple-element.27), channel_id=1, source_target_pairs={{0,8},{8,0},{1,9},{9,1},{2,10},{10,2},{3,11},{11,3},{4,12},{12,4},... | collective-permute-start | bytes 1572872 | tf_op jit(solution)/shard_map/ppermute | solution.py:230
  101.3 10.9 %collective-permute-start.8 = (bf16[256,512]{1,0:T(8,128)(2,1)S(1)}, bf16[256,512]{1,0:T(8,128)(2,1)S(1)}, u32[]{:S(2)}, u32[]{:S(2)}) collective-permute-start(bf16[256,512]{1,0:T(8,128)(2,1)S(1)} %get-tuple-element.29), channel_id=1, source_target_pairs={{0,256},{256,0},{1,257},{257,1},{2,258},{258,2},{3,259},{259,3},{4... | collective-permute-start | bytes 786440 | tf_op jit(solution)/shard_map/ppermute | solution.py:230

commit v14 on v13

--- a/solution.py
+++ b/solution.py
@@ -116,6 +116,7 @@
 
 def stat_kernel(scores, sent, cross, tops):
     cross[...] = scores[4:8]
+    lines = {}
     for l in range(2):
         batch = [scores[h * 2 + l, 0:64, :] for h in range(4)]
         hard = [scores[h * 2 + l, 64:66, :] for h in range(4)]
@@ -126,11 +127,10 @@
         total = jnp.sum(sum(jnp.exp(b - top) for b in batch), axis=0, keepdims=True)
         total = total + jnp.sum(sum(jnp.exp(h - top) for h in hard), axis=0, keepdims=True)
         tops[:, l * 128 : (l + 1) * 128] = top
-        for to in range(NZ):
-            sent[to, l : l + 1, :] = top
-            sent[to, 2 + l : 3 + l, :] = total
+        lines[l], lines[2 + l] = top, total
+    tile = jnp.concatenate([lines[i] for i in range(4)] + [jnp.zeros((4, 128), F32)], axis=0)
     for to in range(NZ):
-        sent[to, 4:8, :] = jnp.zeros((4, 128), F32)
+        sent[to] = tile
 
 
 def row_logs(stats, zp):

time: 114 us -> 114 us (level)
  no operation moved by 1% of the time
where the time goes in v14:
time: 114 us; the launch traced here: 113 us
  starting transfers between devices  62.2 us (55%)
  waiting for transfers between devices  23 us (20%)
  blocking collectives  19.3 us (17%)
  Pallas kernels  7.64 us (7%)
    ppermute x9, starting transfers between devices, swap(): return lax.ppermute(x, axis, [(0, 1), (1, 0)])  35.5 us
    all_to_all x3, starting transfers between devices, exchange(): return lax.all_to_all(x, axes, split_axis=0, concat_axis=0, tiled=True)  26.7 us
    all_to_all x2, blocking collectives, exchange(): return lax.all_to_all(x, axes, split_axis=0, concat_axis=0, tiled=True)  19.3 us
    ppermute x9, waiting for transfers between devices, swap(): return lax.ppermute(x, axis, [(0, 1), (1, 0)])  12.9 us
    all_to_all x3, waiting for transfers between devices, exchange(): return lax.all_to_all(x, axes, split_axis=0, concat_axis=0, tiled=True)  10.1 us
    pallas_call x11, Pallas kernels, call(): pl.pallas_call(kernel, out_shape=[jax.ShapeDtypeStruct(shape, dtype) for...  7.64 us
  transfers between devices with their start and end apart: 12, of which 5 were waited for; matrix products, arithmetic and copies ran while one was open for 0% of the time, Pallas kernels for 4%

profile of v14, /device:TPU:1, one launch (start us, length us, event | category | flops | bytes accessed | tf_op | source)
XLA Modules:
  0.0 113.0 jit_solution(17498948403936328673)
XLA Ops:
  0.6 1.8 %shard_map.76 = (bf16[8,144,128]{2,1,0:T(8,128)(2,1)}, bf16[256,512]{1,0:T(8,128)(2,1)}) custom-call(bf16[32,512]{1,0:T(8,128)(2,1)} %queries.1, s32[7,32]{1,0:T(8,128)} %bitcast.4, s32[7,32]{1,0:T(8,128)} %bitcast.5, bf16[224,512]{1,0:T(8,128)(2,1)} %negatives.1, bf16[32,512]{1,0:T(8,128)(2,1)} %passages.1), custom_call_target="tpu_custom_call" | custom-call | tf_op jit(solution)/shard_map/pallas_call | solution.py:26
  2.5 4.4 %collective-permute-start = (bf16[256,512]{1,0:T(8,128)(2,1)}, bf16[256,512]{1,0:T(8,128)(2,1)S(1)}, u32[]{:S(2)}, u32[]{:S(2)}) collective-permute-start(bf16[256,512]{1,0:T(8,128)(2,1)} %get-tuple-element.18.first), channel_id=1, source_target_pairs={{0,16},{16,0},{1,17},{17,1},{2,18},{18,2},{3,19},{19,3},{4,20},{20... | collective-permute-start | bytes 786440 | tf_op jit(solution)/shard_map/ppermute | solution.py:230
  6.9 4.8 %collective-permute-start.2 = (bf16[256,512]{1,0:T(8,128)(2,1)}, bf16[256,512]{1,0:T(8,128)(2,1)S(1)}, u32[]{:S(2)}, u32[]{:S(2)}) collective-permute-start(bf16[256,512]{1,0:T(8,128)(2,1)} %get-tuple-element.18.first), channel_id=1, source_target_pairs={{0,256},{256,0},{1,257},{257,1},{2,258},{258,2},{3,259},{259,3},{4... | collective-permute-start | bytes 786440 | tf_op jit(solution)/shard_map/ppermute | solution.py:230
  11.7 14.1 %all-to-all-start = ((bf16[8,144,128]{2,1,0:T(8,128)(2,1)}), bf16[8,144,128]{2,1,0:T(8,128)(2,1)S(1)}, u32[]{:S(2)}, u32[]{:S(2)}) async-start(bf16[8,144,128]{2,1,0:T(8,128)(2,1)} %get-tuple-element.17), calls=%async_computation | async-start | bytes 589824 | tf_op jit(solution)/shard_map/all_to_all | solution.py:234
  25.8 0.0 collective-permute-done.second
  25.8 2.0 %collective-permute-start.3 = (bf16[256,512]{1,0:T(8,128)(2,1)S(1)}, bf16[256,512]{1,0:T(8,128)(2,1)S(1)}, u32[]{:S(2)}, u32[]{:S(2)}) collective-permute-start(bf16[256,512]{1,0:T(8,128)(2,1)S(1)} %collective-permute-done.second), channel_id=1, source_target_pairs={{0,256},{256,0},{1,257},{257,1},{2,258},{258,2},{3,259},{259,3},{4... | collective-permute-start | bytes 786440 | tf_op jit(solution)/shard_map/ppermute | solution.py:230
  27.8 3.7 %collective-permute-start.1 = (bf16[512,512]{1,0:T(8,128)(2,1)S(1)}, bf16[512,512]{1,0:T(8,128)(2,1)S(1)}, u32[]{:S(2)}, u32[]{:S(2)}) collective-permute-start(bf16[512,512]{1,0:T(8,128)(2,1)S(1)} %shard_map.77.refs_0_.own), channel_id=1, source_target_pairs={{0,8},{8,0},{1,9},{9,1},{2,10},{10,2},{3,11},{11,3},{4,12},{12,4},... | collective-permute-start | bytes 1572872 | tf_op jit(solution)/shard_map/ppermute | solution.py:230
  31.5 0.0 collective-permute-done.2.first
  31.5 3.9 %collective-permute-done.3.second = bf16[256,512]{1,0:T(8,128)(2,1)S(1)} collective-permute-done((bf16[256,512]{1,0:T(8,128)(2,1)S(1)}, bf16[256,512]{1,0:T(8,128)(2,1)S(1)}, u32[]{:S(2)}, u32[]{:S(2)}) %collective-permute-start.3) | collective-permute-done | bytes 262176 | tf_op jit(solution)/shard_map/ppermute | solution.py:230
  35.5 4.3 %collective-permute-start.4 = (bf16[512,512]{1,0:T(8,128)(2,1)S(1)}, bf16[512,512]{1,0:T(8,128)(2,1)S(1)}, u32[]{:S(2)}, u32[]{:S(2)}) collective-permute-start(bf16[512,512]{1,0:T(8,128)(2,1)S(1)} %shard_map.78.refs_2_), channel_id=1, source_target_pairs={{0,8},{8,0},{1,9},{9,1},{2,10},{10,2},{3,11},{11,3},{4,12},{12,4},... | collective-permute-start | bytes 1572872 | tf_op jit(solution)/shard_map/ppermute | solution.py:230
  39.8 2.5 %all-to-all-done.near = bf16[8,144,128]{2,1,0:T(8,128)(2,1)S(1)} async-done(((bf16[8,144,128]{2,1,0:T(8,128)(2,1)}), bf16[8,144,128]{2,1,0:T(8,128)(2,1)S(1)}, u32[]{:S(2)}, u32[]{:S(2)}) %all-to-all-start) | async-done | bytes 294944 | tf_op jit(solution)/shard_map/all_to_all | solution.py:234
  42.3 2.7 %collective-permute-start.5 = (bf16[8,144,128]{2,1,0:T(8,128)(2,1)S(1)}, bf16[8,144,128]{2,1,0:T(8,128)(2,1)S(1)}, u32[]{:S(2)}, u32[]{:S(2)}) collective-permute-start(bf16[8,144,128]{2,1,0:T(8,128)(2,1)S(1)} %all-to-all-done.near), channel_id=1, source_target_pairs={{0,16},{16,0},{1,17},{17,1},{2,18},{18,2},{3,19},{19,3},{4,20},{20... | collective-permute-start | bytes 884744 | tf_op jit(solution)/shard_map/ppermute | solution.py:230
  45.0 0.0 collective-permute-done.1.refs_1_
  45.0 0.0 collective-permute-done.4.refs_3_
  45.0 0.8 shard_map.79
  45.8 10.4 %all_to_all.25.came = f32[8,72,128]{2,1,0:T(8,128)S(1)} all-to-all(f32[8,72,128]{2,1,0:T(8,128)S(1)} %get-tuple-element.19), channel_id=1, replica_groups=mesh['yh'=2,'zh'=8,'zp'=2,'c'=2,'yl'=2,'x'=4] {'yl','x'}, dimensions={0} | all-to-all | bytes 589824 | tf_op jit(solution)/shard_map/all_to_all | solution.py:234
  56.3 0.0 collective-permute-done.5.far
  56.3 8.9 %all_to_all.26.scores = f32[8,72,128]{2,1,0:T(8,128)S(1)} all-to-all(f32[8,72,128]{2,1,0:T(8,128)S(1)} %shard_map.80), channel_id=1, replica_groups=mesh['yh'=2,'zh'=8,'zp'=2,'c'=2,'yl'=2,'x'=4] {'yl','x'}, dimensions={0} | all-to-all | bytes 589824 | tf_op jit(solution)/shard_map/all_to_all | solution.py:234
  65.2 0.7 shard_map.81
  65.9 9.2 %all-to-all-start.3 = ((f32[16,8,128]{2,1,0:T(8,128)}), f32[16,8,128]{2,1,0:T(8,128)S(1)}, u32[]{:S(2)}, u32[]{:S(2)}) async-start(f32[16,8,128]{2,1,0:T(8,128)} %get-tuple-element.21), calls=%async_computation.3 | async-start | bytes 131072 | tf_op jit(solution)/shard_map/all_to_all | solution.py:234
  75.1 3.3 %collective-permute-start.6 = (f32[4,72,128]{2,1,0:T(8,128)}, f32[4,72,128]{2,1,0:T(8,128)}, u32[]{:S(2)}, u32[]{:S(2)}) collective-permute-start(f32[4,72,128]{2,1,0:T(8,128)} %get-tuple-element.20), channel_id=1, source_target_pairs={{0,16},{16,0},{1,17},{17,1},{2,18},{18,2},{3,19},{19,3},{4,20},{20... | collective-permute-start | bytes 442376 | tf_op jit(solution)/shard_map/ppermute | solution.py:230
  78.4 0.7 shard_map.82.total
  79.2 7.6 %all-to-all-done.3 = f32[16,8,128]{2,1,0:T(8,128)S(1)} async-done(((f32[16,8,128]{2,1,0:T(8,128)}), f32[16,8,128]{2,1,0:T(8,128)S(1)}, u32[]{:S(2)}, u32[]{:S(2)}) %all-to-all-start.3) | async-done | bytes 65568 | tf_op jit(solution)/shard_map/all_to_all | solution.py:234
  86.8 1.0 shard_map.83
  87.8 3.4 %all-to-all-start.4 = ((bf16[8,32,512]{2,1,0:T(8,128)(2,1)}), bf16[8,32,512]{2,1,0:T(8,128)(2,1)S(1)}, u32[]{:S(2)}, u32[]{:S(2)}) async-start(bf16[8,32,512]{2,1,0:T(8,128)(2,1)} %get-tuple-element.30), calls=%async_computation.4 | async-start | bytes 524288 | tf_op jit(solution)/shard_map/all_to_all | solution.py:234
  91.2 1.6 %shard_map.84 = (bf16[2,256,512]{2,1,0:T(8,128)(2,1)S(1)}, bf16[2,256,512]{2,1,0:T(8,128)(2,1)S(1)}) custom-call(f32[4,72,128]{2,1,0:T(8,128)} %collective-permute-done.6.came, f32[8,256]{1,0:T(8,128)S(1)} %get-tuple-element.24.logs, f32[8,72,128]{2,1,0:T(8,128)S(1)} %all_to_all.26.scores, s32[8,256]{1,0:T(8,128)S(1)} %get-tuple-element.23.asked, ...), custom_call_target="tpu_custom_call" | custom-call | tf_op jit(solution)/shard_map/pallas_call | solution.py:26
  92.8 6.8 %collective-permute-start.7 = (bf16[2,256,512]{2,1,0:T(8,128)(2,1)S(1)}, bf16[2,256,512]{2,1,0:T(8,128)(2,1)S(1)}, u32[]{:S(2)}, u32[]{:S(2)}) collective-permute-start(bf16[2,256,512]{2,1,0:T(8,128)(2,1)S(1)} %get-tuple-element.27), channel_id=1, source_target_pairs={{0,8},{8,0},{1,9},{9,1},{2,10},{10,2},{3,11},{11,3},{4,12},{12,4},... | collective-permute-start | bytes 1572872 | tf_op jit(solution)/shard_map/ppermute | solution.py:230
  99.7 1.5 %collective-permute-done.7.came = bf16[2,256,512]{2,1,0:T(8,128)(2,1)S(1)} collective-permute-done((bf16[2,256,512]{2,1,0:T(8,128)(2,1)S(1)}, bf16[2,256,512]{2,1,0:T(8,128)(2,1)S(1)}, u32[]{:S(2)}, u32[]{:S(2)}) %collective-permute-start.7) | collective-permute-done | bytes 524320 | tf_op jit(solution)/shard_map/ppermute | solution.py:230
  101.2 0.1 shard_map.85
  101.3 3.5 %collective-permute-start.8 = (bf16[256,512]{1,0:T(8,128)(2,1)S(1)}, bf16[256,512]{1,0:T(8,128)(2,1)S(1)}, u32[]{:S(2)}, u32[]{:S(2)}) collective-permute-start(bf16[256,512]{1,0:T(8,128)(2,1)S(1)} %get-tuple-element.29), channel_id=1, source_target_pairs={{0,256},{256,0},{1,257},{257,1},{2,258},{258,2},{3,259},{259,3},{4... | collective-permute-start | bytes 786440 | tf_op jit(solution)/shard_map/ppermute | solution.py:230
  104.8 7.4 %collective-permute-done.8.came = bf16[256,512]{1,0:T(8,128)(2,1)S(1)} collective-permute-done((bf16[256,512]{1,0:T(8,128)(2,1)S(1)}, bf16[256,512]{1,0:T(8,128)(2,1)S(1)}, u32[]{:S(2)}, u32[]{:S(2)}) %collective-permute-start.8) | collective-permute-done | bytes 262176 | tf_op jit(solution)/shard_map/ppermute | solution.py:230
  112.2 0.7 shard_map.86
  (7 shorter events, 0.1 us)
Async XLA Ops:
  2.5 23.3 %collective-permute-start = (bf16[256,512]{1,0:T(8,128)(2,1)}, bf16[256,512]{1,0:T(8,128)(2,1)S(1)}, u32[]{:S(2)}, u32[]{:S(2)}) collective-permute-start(bf16[256,512]{1,0:T(8,128)(2,1)} %get-tuple-element.18.first), channel_id=1, source_target_pairs={{0,16},{16,0},{1,17},{17,1},{2,18},{18,2},{3,19},{19,3},{4,20},{20... | collective-permute-start | bytes 786440 | tf_op jit(solution)/shard_map/ppermute | solution.py:230
  6.9 24.6 %collective-permute-start.2 = (bf16[256,512]{1,0:T(8,128)(2,1)}, bf16[256,512]{1,0:T(8,128)(2,1)S(1)}, u32[]{:S(2)}, u32[]{:S(2)}) collective-permute-start(bf16[256,512]{1,0:T(8,128)(2,1)} %get-tuple-element.18.first), channel_id=1, source_target_pairs={{0,256},{256,0},{1,257},{257,1},{2,258},{258,2},{3,259},{259,3},{4... | collective-permute-start | bytes 786440 | tf_op jit(solution)/shard_map/ppermute | solution.py:230
  11.7 16.0 %copy-start = (bf16[256,512]{1,0:T(8,128)(2,1)S(1)}, bf16[256,512]{1,0:T(8,128)(2,1)}, u32[]{:S(2)}) copy-start(bf16[256,512]{1,0:T(8,128)(2,1)} %get-tuple-element.18.first) | copy-start | bytes 786436
  11.7 30.6 %all-to-all-start = ((bf16[8,144,128]{2,1,0:T(8,128)(2,1)}), bf16[8,144,128]{2,1,0:T(8,128)(2,1)S(1)}, u32[]{:S(2)}, u32[]{:S(2)}) async-start(bf16[8,144,128]{2,1,0:T(8,128)(2,1)} %get-tuple-element.17), calls=%async_computation | async-start | bytes 589824 | tf_op jit(solution)/shard_map/all_to_all | solution.py:234
  25.8 9.7 %collective-permute-start.3 = (bf16[256,512]{1,0:T(8,128)(2,1)S(1)}, bf16[256,512]{1,0:T(8,128)(2,1)S(1)}, u32[]{:S(2)}, u32[]{:S(2)}) collective-permute-start(bf16[256,512]{1,0:T(8,128)(2,1)S(1)} %collective-permute-done.second), channel_id=1, source_target_pairs={{0,256},{256,0},{1,257},{257,1},{2,258},{258,2},{3,259},{259,3},{4... | collective-permute-start | bytes 786440 | tf_op jit(solution)/shard_map/ppermute | solution.py:230
  27.8 17.2 %collective-permute-start.1 = (bf16[512,512]{1,0:T(8,128)(2,1)S(1)}, bf16[512,512]{1,0:T(8,128)(2,1)S(1)}, u32[]{:S(2)}, u32[]{:S(2)}) collective-permute-start(bf16[512,512]{1,0:T(8,128)(2,1)S(1)} %shard_map.77.refs_0_.own), channel_id=1, source_target_pairs={{0,8},{8,0},{1,9},{9,1},{2,10},{10,2},{3,11},{11,3},{4,12},{12,4},... | collective-permute-start | bytes 1572872 | tf_op jit(solution)/shard_map/ppermute | solution.py:230
  35.5 9.5 %collective-permute-start.4 = (bf16[512,512]{1,0:T(8,128)(2,1)S(1)}, bf16[512,512]{1,0:T(8,128)(2,1)S(1)}, u32[]{:S(2)}, u32[]{:S(2)}) collective-permute-start(bf16[512,512]{1,0:T(8,128)(2,1)S(1)} %shard_map.78.refs_2_), channel_id=1, source_target_pairs={{0,8},{8,0},{1,9},{9,1},{2,10},{10,2},{3,11},{11,3},{4,12},{12,4},... | collective-permute-start | bytes 1572872 | tf_op jit(solution)/shard_map/ppermute | solution.py:230
  42.3 13.9 %collective-permute-start.5 = (bf16[8,144,128]{2,1,0:T(8,128)(2,1)S(1)}, bf16[8,144,128]{2,1,0:T(8,128)(2,1)S(1)}, u32[]{:S(2)}, u32[]{:S(2)}) collective-permute-start(bf16[8,144,128]{2,1,0:T(8,128)(2,1)S(1)} %all-to-all-done.near), channel_id=1, source_target_pairs={{0,16},{16,0},{1,17},{17,1},{2,18},{18,2},{3,19},{19,3},{4,20},{20... | collective-permute-start | bytes 884744 | tf_op jit(solution)/shard_map/ppermute | solution.py:230
  65.9 20.9 %all-to-all-start.3 = ((f32[16,8,128]{2,1,0:T(8,128)}), f32[16,8,128]{2,1,0:T(8,128)S(1)}, u32[]{:S(2)}, u32[]{:S(2)}) async-start(f32[16,8,128]{2,1,0:T(8,128)} %get-tuple-element.21), calls=%async_computation.3 | async-start | bytes 131072 | tf_op jit(solution)/shard_map/all_to_all | solution.py:234
  75.1 16.0 %collective-permute-start.6 = (f32[4,72,128]{2,1,0:T(8,128)}, f32[4,72,128]{2,1,0:T(8,128)}, u32[]{:S(2)}, u32[]{:S(2)}) collective-permute-start(f32[4,72,128]{2,1,0:T(8,128)} %get-tuple-element.20), channel_id=1, source_target_pairs={{0,16},{16,0},{1,17},{17,1},{2,18},{18,2},{3,19},{19,3},{4,20},{20... | collective-permute-start | bytes 442376 | tf_op jit(solution)/shard_map/ppermute | solution.py:230
  87.8 24.5 %all-to-all-start.4 = ((bf16[8,32,512]{2,1,0:T(8,128)(2,1)}), bf16[8,32,512]{2,1,0:T(8,128)(2,1)S(1)}, u32[]{:S(2)}, u32[]{:S(2)}) async-start(bf16[8,32,512]{2,1,0:T(8,128)(2,1)} %get-tuple-element.30), calls=%async_computation.4 | async-start | bytes 524288 | tf_op jit(solution)/shard_map/all_to_all | solution.py:234
  92.8 8.4 %collective-permute-start.7 = (bf16[2,256,512]{2,1,0:T(8,128)(2,1)S(1)}, bf16[2,256,512]{2,1,0:T(8,128)(2,1)S(1)}, u32[]{:S(2)}, u32[]{:S(2)}) collective-permute-start(bf16[2,256,512]{2,1,0:T(8,128)(2,1)S(1)} %get-tuple-element.27), channel_id=1, source_target_pairs={{0,8},{8,0},{1,9},{9,1},{2,10},{10,2},{3,11},{11,3},{4,12},{12,4},... | collective-permute-start | bytes 1572872 | tf_op jit(solution)/shard_map/ppermute | solution.py:230
  101.3 10.9 %collective-permute-start.8 = (bf16[256,512]{1,0:T(8,128)(2,1)S(1)}, bf16[256,512]{1,0:T(8,128)(2,1)S(1)}, u32[]{:S(2)}, u32[]{:S(2)}) collective-permute-start(bf16[256,512]{1,0:T(8,128)(2,1)S(1)} %get-tuple-element.29), channel_id=1, source_target_pairs={{0,256},{256,0},{1,257},{257,1},{2,258},{258,2},{3,259},{259,3},{4... | collective-permute-start | bytes 786440 | tf_op jit(solution)/shard_map/ppermute | solution.py:230
